TPU v7x, 32 devices: a whole 2x2x4 slice. The times are simulated.
32 devices in a mesh: tm: 8 (over z, x), chan: 4 (over y, core).
Axes of the slice: x: 2, y: 2, z: 4, core: 2. Of those that a mesh axis runs over, the one named last changes fastest.
Arguments:
- data: bfloat16 [384, 16384], P('chan', 'tm'), may hold values from 0.049804688 to 2
- motifs: bfloat16 [384, 2048], P('chan', 'tm'), may hold values from 9.727478e-05 to 0.001953125
- loadings: float32 [64, 16384], P(None, 'tm'), as said below
Outputs:
- factors_now: float32 [64, 16384], P(None, 'tm')
Inputs may be any that keep to these rules, and one draw needn't show every extreme that they name: `loadings`: every entry is positive.
All inputs are finite; a program needn't handle non-finite values.
Results may differ from a plain program's by a relative error of at most 0.0003.
Values may be sent and summed in bfloat16 or wider, within the bound.
No kernel may reach another device: no remote copies, remote signals or barrier semaphores. Data moves between devices by JAX's collectives and lax.ppermute only.
A program may use at most 128 MiB of HBM per device.

v0:
```python
import functools

import jax
import jax.numpy as jnp
from jax import lax
from jax.experimental import pallas as pl
from jax.experimental.pallas import tpu as pltpu
from jax.sharding import PartitionSpec as P

LAGS = 32
ITERS = 3
PENALTY = 0.2

PHASES = 4
CHUNKS = 16
REACH = LAGS // PHASES
LANES = 128
GROUP = 8

NT = (((1,), (1,)), ((), ()))
NN = (((1,), (0,)), ((), ()))
TN = (((0,), (0,)), ((), ()))
F32 = jnp.float32
BF16 = jnp.bfloat16


def dot(a, b, dims=NN):
    return lax.dot_general(a, b, dims, preferred_element_type=F32)


def split(a):
    high = a.astype(BF16)
    return high, (a - high.astype(F32)).astype(BF16)


def vmem(n=1):
    return [pl.BlockSpec(memory_space=pltpu.VMEM)] * n


def smem(n=1):
    return [pl.BlockSpec(memory_space=pltpu.SMEM)] * n


def call(body, out_shape, in_specs, scratch=(), flops=0, moved=0, limit=16):
    return pl.pallas_call(
        body,
        out_shape=out_shape,
        in_specs=in_specs,
        out_specs=jax.tree.map(lambda _: pl.BlockSpec(memory_space=pltpu.VMEM), out_shape),
        scratch_shapes=list(scratch),
        compiler_params=pltpu.CompilerParams(vmem_limit_bytes=limit * 2**20),
        cost_estimate=pl.CostEstimate(flops=flops, bytes_accessed=moved, transcendentals=0),
    )


class Plan:
    def __init__(self, steps, factors):
        self.steps = steps
        self.factors = factors
        self.width = PHASES * factors
        self.edge = 2 * REACH
        self.rows = steps // PHASES + 2 * self.edge
        self.per = self.rows // CHUNKS
        self.ext = self.per + 2 * REACH
        self.stride = PHASES * self.per
        self.halo = PHASES * (self.edge + REACH)
        self.front = PHASES * self.edge
        self.back = PHASES * (self.edge + REACH)
        wide = steps + 2 * self.halo
        self.wide = -(-wide // LANES) * LANES
        self.tiles = LAGS + PHASES


def lane_tiles(count):
    return [slice(i * LANES, (i + 1) * LANES) for i in range(count)]


def row_tile(m):
    return slice(m * CHUNKS, (m + 1) * CHUNKS)


def turned(buf, left, middle, right, tiles):
    parts = [left] + [middle[:, at] for at in lane_tiles(tiles)] + [right]
    for i, part in enumerate(parts):
        part = part.astype(F32)
        spare = LANES - part.shape[0]
        low = part if spare == part.shape[0] else jnp.zeros((spare, LANES), F32)
        buf[i * LANES : (i + 1) * LANES, :] = jnp.concatenate([part, low], 0).T


def spread(plan, tile, m, bits_ref):
    j = lax.broadcasted_iota(jnp.int32, tile.shape, 0)
    bits_ref[row_tile(m + REACH), :] = tile.astype(BF16)
    if m >= plan.per - REACH:
        low = jnp.where(j == 0, 0.0, pltpu.roll(tile, 1, 0))
        bits_ref[row_tile(m - plan.per + REACH), :] = low.astype(BF16)
    if m < REACH:
        high = jnp.where(j == CHUNKS - 1, 0.0, pltpu.roll(tile, CHUNKS - 1, 0))
        bits_ref[row_tile(m + plan.per + REACH), :] = high.astype(BF16)


def lay_loadings(plan, load_ref, left_ref, right_ref, x_ref, bits_ref, low_ref, buf):
    factors = plan.factors
    turned(buf, left_ref[:factors, :], load_ref, right_ref[:factors, :], plan.steps // LANES)
    lane = lax.broadcasted_iota(jnp.int32, (CHUNKS, LANES), 1)
    skip = LANES - plan.halo
    for m in range(plan.ext):
        halves = []
        for h in range(PHASES // 2):
            at = skip + PHASES * m + 2 * h
            even = buf[pl.ds(at, CHUNKS, stride=plan.stride), :]
            odd = buf[pl.ds(at + 1, CHUNKS, stride=plan.stride), :]
            halves.append(jnp.where(lane < factors, even, odd))
        tile = jnp.concatenate(halves, 1)
        bits = tile.astype(BF16)
        bits_ref[row_tile(m), :] = bits
        if REACH <= m < REACH + plan.per:
            x_ref[row_tile(m - REACH), :] = tile
            low_ref[row_tile(m - REACH), :] = (tile - bits.astype(F32)).astype(BF16)


def lay_data(plan, data_ref, rims_ref, out_ref, buf):
    turned(buf, rims_ref[:, :LANES], data_ref, rims_ref[:, LANES:], plan.steps // LANES)
    skip = LANES - plan.front
    for m in range(plan.per + REACH):
        for p, at in enumerate(lane_tiles(PHASES)):
            rows = pl.ds(skip + PHASES * m + p, CHUNKS, stride=plan.stride)
            out_ref[row_tile(m), at] = buf[rows, :].astype(BF16)


def first_gram(load_ref, out_ref):
    high, low = split(load_ref[...])
    cross = dot(high, low, NT)
    out_ref[...] = dot(high, high, NT) + cross + cross.T


def rim_body(plan, load_ref, data_ref, even_ref, tail_ref, head_ref):
    factors = plan.factors
    ends = ((tail_ref, slice(plan.steps - LANES, plan.steps)), (head_ref, slice(0, LANES)))
    for rim_ref, at in ends:
        rim_ref[:factors, :] = load_ref[:, at]
        rim_ref[factors:, :] = data_ref[:, at].astype(F32)


def lay_motifs(plan, me_ref, even_ref, odd_ref, stk_ref, padded):
    factors = plan.factors
    channels = even_ref.shape[1]
    span = GROUP * LAGS
    me = me_ref[0]
    padded[channels:, :] = jnp.zeros((LANES - channels, 2 * span), BF16)
    row = lax.broadcasted_iota(jnp.int32, (span, span), 0)
    col = lax.broadcasted_iota(jnp.int32, (span, span), 1)
    pick = jnp.where(col == (row % GROUP) * LAGS + row // GROUP, 1.0, 0.0).astype(BF16)
    for q in range(PHASES):
        rows = slice(q * factors, (q + 1) * factors)
        if q:
            stk_ref[rows, : q * LANES] = jnp.zeros((factors, q * LANES), BF16)
        stk_ref[rows, (LAGS + q) * LANES :] = jnp.zeros((factors, (PHASES - q) * LANES), BF16)
    swapped = me % 2
    for pair in range(factors // (2 * GROUP)):
        at = (me // 2) ^ pair
        one, two = even_ref[at].astype(F32), odd_ref[at].astype(F32)
        padded[:channels, :span] = jnp.where(swapped == 1, two, one).astype(BF16)
        padded[:channels, span:] = jnp.where(swapped == 1, one, two).astype(BF16)
        halves = [dot(pick, padded[:, h * span : (h + 1) * span], NT) for h in range(2)]
        for lag in range(LAGS):
            cut = slice(lag * GROUP, (lag + 1) * GROUP)
            tile = jnp.concatenate([halves[0][cut], halves[1][cut]], 0).astype(BF16)
            for q in range(PHASES):
                first = q * factors + pair * 2 * GROUP
                stk_ref[first : first + 2 * GROUP, (lag + q) * LANES : (lag + q + 1) * LANES] = tile


def auto_body(plan, me_ref, even_ref, odd_ref, *refs):
    before, (stk_ref, auto_ref, padded) = refs[:-3], refs[-3:]
    factors = plan.factors
    lay_motifs(plan, me_ref, even_ref, odd_ref, stk_ref, padded)
    last = (PHASES - 1) * factors
    chunk = 2 * LANES
    shift = PHASES * LANES // chunk
    auto_ref[...] = before[0][...] if before else jnp.zeros_like(auto_ref)
    for u in range(plan.tiles * LANES // chunk):
        taps = min(u // shift + 1, REACH)
        cuts = [u - shift * a for a in range(taps)]
        left = [stk_ref[last : last + factors, c * chunk : (c + 1) * chunk] for c in cuts]
        auto_ref[: taps * factors, :] += dot(
            jnp.concatenate(left, 0), stk_ref[:, u * chunk : (u + 1) * chunk], NT
        )


def numer_body(plan, stk_ref, data_ref, *refs):
    before, numer_ref = refs[:-1], refs[-1]
    deep = PHASES * LANES
    for s in range(REACH + 1):
        rows = slice(s * CHUNKS, s * CHUNKS + plan.rows)
        part = dot(data_ref[rows, :], stk_ref[:, s * deep : (s + 1) * deep], NT)
        if s:
            numer_ref[...] += part
        else:
            numer_ref[...] = part + before[0][...] if before else part


def tail_part(plan, stk_ref, bits_ref):
    width = plan.width
    deep = PHASES * LANES
    start = (plan.steps // PHASES + plan.edge) - (CHUNKS - 1) * plan.per + REACH
    inside = [
        bits_ref[row_tile(start - REACH + i), :].astype(F32)[CHUNKS - 1 :] for i in range(REACH)
    ]
    known = jnp.concatenate(inside + [jnp.zeros((REACH, width), F32)], 0)
    ahead = jnp.zeros((REACH, deep), F32)
    for s in range(1, REACH + 1):
        rows = known[REACH - s : 2 * REACH - s].astype(BF16)
        ahead += dot(rows, stk_ref[:, s * deep : (s + 1) * deep])
    blank = jnp.zeros((REACH, deep), F32)
    high = ahead.astype(BF16).astype(F32)
    high, low = jnp.concatenate([blank, high], 0), jnp.concatenate([blank, ahead - high], 0)
    out = jnp.zeros((2 * REACH, width), F32)
    for s in range(1, REACH + 1):
        both = jnp.concatenate([high[s : s + REACH], low[s : s + REACH]], 0).astype(BF16)
        out += dot(both, stk_ref[:, s * deep : (s + 1) * deep], NT)
    return out[:REACH] + out[REACH:]


def tail_body(plan, shards, me_ref, bits_ref, *refs):
    stks, out_ref = refs[:-1], refs[-1]
    out_ref[...] = jnp.zeros_like(out_ref)

    @pl.when(me_ref[0] == shards - 1)
    def _():
        for stk_ref in stks:
            out_ref[...] += tail_part(plan, stk_ref, bits_ref)


def taps_body(plan, auto_a, auto_b, high_ref, low_ref, line):
    factors, width = plan.factors, plan.width
    line[:, :width] = jnp.zeros((factors, width), F32)
    for a in range(REACH):
        rows = slice(a * factors, (a + 1) * factors)
        line[:, (REACH - a) * width : (REACH - a + 1) * width] = auto_a[rows, :] + auto_b[rows, :]
    zero = (REACH * PHASES + PHASES - 1) * factors
    back = [
        line[:, zero - d * factors : zero - (d - 1) * factors].T for d in range(1, PHASES)
    ]
    back.append(jnp.zeros((factors, factors), F32))
    line[:, (REACH + 1) * width :] = jnp.concatenate(back, 1)
    for s in range(REACH + 1):
        for p in range(PHASES):
            first = zero - (PHASES * s + p) * factors
            high, low = split(line[:, first : first + width])
            rows = slice(s * width + p * factors, s * width + (p + 1) * factors)
            high_ref[rows, :] = high
            low_ref[rows, :] = low


def conv_body(plan, offsets, bits_ref, high_ref, low_ref, *refs):
    before, out_ref = refs[:-1], refs[-1]
    width, rows = plan.width, plan.rows
    for i, s in enumerate(offsets):
        at = (REACH + s) * CHUNKS
        mat = slice(abs(s) * width, (abs(s) + 1) * width)
        dims = NN if s >= 0 else NT
        part = dot(bits_ref[at : at + rows, :], high_ref[mat, :], dims)
        part += dot(bits_ref[at : at + rows, :], low_ref[mat, :], dims)
        if i:
            out_ref[...] += part
        else:
            out_ref[...] = part + before[0][...] if before else part


def first_conv_body(plan, offsets, auto_a, auto_b, bits_ref, high_ref, low_ref, out_ref, line):
    taps_body(plan, auto_a, auto_b, high_ref, low_ref, line)
    conv_body(plan, offsets, bits_ref, high_ref, low_ref, out_ref)


def penalties(plan, scale, me_ref, grams, bits_ref, low_ref):
    factors, rows = plan.factors, plan.rows
    total = grams[0][...]
    if len(grams) > 1:
        here, far, both = (g[...] for g in grams[1:])
        odd = me_ref[1] == 1
        near = jnp.where(odd, far, here)
        next_one = jnp.where(odd, here, far)
        total = (total + near) + (next_one + both)
    r = lax.broadcasted_iota(jnp.int32, (factors, factors), 0)
    c = lax.broadcasted_iota(jnp.int32, (factors, factors), 1)
    off = jnp.where(r == c, 0.0, total) * scale
    blank = jnp.zeros((factors, factors), F32)
    high, low = split(
        jnp.concatenate(
            [
                jnp.concatenate([off if p == q else blank for q in range(PHASES)], 1)
                for p in range(PHASES)
            ],
            0,
        )
    )
    bits = bits_ref[REACH * CHUNKS : REACH * CHUNKS + rows, :]
    return dot(bits, high) + dot(bits, low) + dot(low_ref[...], high)


def new_tile(plan, shards, me_ref, m, x_ref, den_ref, numer, pen, tails):
    at = row_tile(m)
    den = den_ref[at, :] + pen[at, :]
    j = lax.broadcasted_iota(jnp.int32, den.shape, 0)
    end = (plan.steps // PHASES + plan.edge) - (CHUNKS - 1) * plan.per
    if end - REACH <= m < end:
        i = m - end + REACH
        over = tails[0][i : i + 1, :] + tails[1][i : i + 1, :]
        den -= jnp.where((j == CHUNKS - 1) & (me_ref[0] == shards - 1), over, 0.0)
    new = x_ref[at, :] * numer / den
    if m < plan.edge:
        new = jnp.where((j == 0) & (me_ref[0] == 0), 0.0, new)
    if m >= end:
        new = jnp.where((j == CHUNKS - 1) & (me_ref[0] == shards - 1), 0.0, new)
    return new


def update_body(plan, scale, shards, counts, me_ref, x_ref, bits_ref, low_ref, den_ref, *refs):
    numers, tails, grams = refs[: counts[0]], refs[counts[0] :][:2], refs[counts[0] + 2 :][: counts[1]]
    refs = refs[counts[0] + 2 + counts[1] :]
    if counts[0] > 1:
        numer_ref, refs = refs[0], refs[1:]
    out_ref, out_bits, out_low, gram_ref, pen, both = refs
    factors, width = plan.factors, plan.width
    pen[...] = penalties(plan, scale, me_ref, grams, bits_ref, low_ref)
    end = (plan.steps // PHASES + plan.edge) - (CHUNKS - 1) * plan.per
    for m in range(plan.per):
        at = row_tile(m)
        numer = numers[0][at, :]
        if counts[0] > 1:
            numer = numer + numers[1][at, :]
            numer_ref[at, :] = numer
        new = new_tile(plan, shards, me_ref, m, x_ref, den_ref, numer, pen, tails)
        out_ref[at, :] = new
        spread(plan, new, m, out_bits)
        high, low = split(new)
        out_low[at, :] = low
        j = lax.broadcasted_iota(jnp.int32, new.shape, 0)
        kept = new
        if m < plan.edge:
            kept = jnp.where(j == 0, 0.0, kept)
        if m >= end:
            kept = jnp.where(j == CHUNKS - 1, 0.0, kept)
        high, low = split(kept)
        both[at, :width] = high
        both[at, width:] = low
    full = dot(both[:, :width], both[...], TN)
    cross = full[:, width:]
    full = full[:, :width] + cross + cross.T
    gram_ref[...] = sum(
        full[p * factors : (p + 1) * factors, p * factors : (p + 1) * factors] for p in range(PHASES)
    )


def last_body(plan, scale, shards, counts, me_ref, x_ref, bits_ref, low_ref, den_ref, *refs):
    numers, tails, grams = refs[: counts[0]], refs[counts[0] :][:2], refs[counts[0] + 2 :][: counts[1]]
    out_ref, pen, buf = refs[counts[0] + 2 + counts[1] :]
    pen[...] = penalties(plan, scale, me_ref, grams, bits_ref, low_ref)
    for m in range(plan.per):
        numer = sum(n[row_tile(m), :] for n in numers)
        new = new_tile(plan, shards, me_ref, m, x_ref, den_ref, numer, pen, tails)
        for h, lanes in enumerate(lane_tiles(PHASES // 2)):
            at = PHASES * m + 2 * h
            buf[pl.ds(at, CHUNKS, stride=plan.stride), :] = new[:, lanes]
            turn = pltpu.roll(new[:, lanes], LANES // 2, 1)
            buf[pl.ds(at + 1, CHUNKS, stride=plan.stride), :] = turn
    for i, lanes in enumerate(lane_tiles(plan.steps // LANES)):
        at = plan.front + i * LANES
        out_ref[:, lanes] = buf[at : at + LANES, :].T[: plan.factors, :]


def swap(x, axis, bit):
    count = lax.axis_size(axis)
    return lax.ppermute(x, axis, [(i, i ^ bit) for i in range(count)])


def mixed(x, bit_even, bit_odd):
    wide = lax.axis_size("chan")
    pairs = []
    for t in range(lax.axis_size("tm")):
        for c in range(wide):
            far = t ^ (bit_odd if c % 2 else bit_even)
            pairs.append((t * wide + c, far * wide + c))
    return lax.ppermute(x, ("tm", "chan"), pairs)


def shifted(x, axis, by):
    count = lax.axis_size(axis)
    return lax.ppermute(x, axis, [(i, i + by) for i in range(count) if 0 <= i + by < count])


def doubling(axis):
    count = lax.axis_size(axis)
    bits = [1 << b for b in range(count.bit_length() - 1)]
    return bits[1:] + bits[:1]


def after(x, *others):
    return lax.optimization_barrier((x, *others))[0]


def gram_rounds(x, odd, meanwhile):
    bits = doubling("tm")
    singles, pairs = bits[-1:], bits[:-1]
    if len(pairs) % 2:
        singles, pairs = singles + pairs[-1:], pairs[:-1]
    gaps = list(meanwhile)

    def gap(y):
        return after(y, *gaps.pop(0)()) if gaps else y

    for bit in singles:
        x = x + gap(swap(x, "tm", bit))
    terms = [x]
    while pairs:
        one, two, pairs = pairs[0], pairs[1], pairs[2:]
        here, both = mixed(x, one, two), swap(x, "tm", one ^ two)
        here = gap(here)
        far = swap(here, "chan", 1)
        terms = [x, here, far, both]
        if pairs:
            near, other = jnp.where(odd, far, here), jnp.where(odd, here, far)
            x = (x + near) + (other + both)
    return terms


def on_device(data, motifs, loadings):
    channels, steps = data.shape
    factors = loadings.shape[0]
    plan = Plan(steps, factors)
    shards = lax.axis_size("tm")
    width, rows = plan.width, plan.rows
    ext_rows = plan.ext * CHUNKS
    sds = jax.ShapeDtypeStruct
    place = jnp.stack([lax.axis_index("tm"), lax.axis_index("chan") % 2]).astype(jnp.int32)
    odd = place[1] == 1

    rim = sds((factors + channels, LANES), F32)
    gram = call(first_gram, sds((factors, factors), F32), vmem())(loadings)

    start = place
    bits = doubling("tm")
    even = motifs[None]
    for i, bit in enumerate(bits[:-1]):
        near, gram_near = swap(even, "tm", bit), swap(gram, "tm", bit)
        if i == 1:
            near, gram_near, right = lax.optimization_barrier((near, gram_near, right))
        else:
            near, gram_near = lax.optimization_barrier((near, gram_near))
        even, gram = jnp.concatenate([even, near], 0), gram + gram_near
        if i == 0:
            tail_rim, head_rim = call(functools.partial(rim_body, plan), (rim, rim), vmem(3))(
                loadings, data, even
            )
            left, right = shifted(tail_rim, "tm", 1), shifted(head_rim, "tm", -1)
            far_data = swap(after(data, even), "chan", 2)
    odds = swap(even, "tm", bits[-1])
    far_even = swap(even, "chan", 2)
    gram_near = swap(gram, "tm", bits[-1])
    odds, far_even, gram_near, left, far_data = lax.optimization_barrier(
        (odds, far_even, gram_near, left, far_data)
    )
    gram = gram + gram_near
    if motifs.shape[1] != GROUP * LAGS:
        order = [0]
        for bit in bits:
            order = order + [o ^ bit for o in order]
        slots = jnp.concatenate([even, odds], 0)
        index = jnp.array([order.index(b) for b in range(shards)], jnp.int32)
        slots = jnp.take(slots, jnp.take(index, jnp.arange(shards) ^ place[0]), axis=0)
        slots = jnp.moveaxis(slots, 0, 1).reshape(channels, -1, GROUP * LAGS)
        slots = jnp.moveaxis(slots, 1, 0)
        even, odds = slots[0::2], slots[1::2]
        start = place * 0
        far_even = swap(even, "chan", 2)

    rims = jnp.concatenate([left[factors:], right[factors:]], 1).astype(BF16)
    far_odds = swap(jnp.concatenate([odds, rims[None]], 0), "chan", 2)
    far_rims = far_odds[-1]

    x, bits_x, low_x = call(
        functools.partial(lay_loadings, plan),
        (sds((rows, width), F32), sds((ext_rows, width), BF16), sds((rows, width), BF16)),
        vmem(3),
        [pltpu.VMEM((steps + 2 * LANES, LANES), F32)],
    )(loadings, left, right)
    lay = call(
        functools.partial(lay_data, plan),
        sds(((plan.per + REACH) * CHUNKS, PHASES * LANES), BF16),
        vmem(2),
        [pltpu.VMEM((steps + 2 * LANES, LANES), F32)],
    )

    def autos(evens, odd_ones, *before):
        return call(
            functools.partial(auto_body, plan),
            (sds((width, plan.tiles * LANES), BF16), sds((REACH * factors, width), F32)),
            smem() + vmem(2 + len(before)),
            [pltpu.VMEM((LANES, 2 * GROUP * LAGS), BF16)],
        )(start, evens, odd_ones, *before)

    def numers(stk, laid, *before):
        return call(
            functools.partial(numer_body, plan), sds((rows, width), F32), vmem(2 + len(before))
        )(stk, laid, *before)

    stk, auto = autos(even, odds)
    numer = numers(stk, lay(data, rims))
    far_laid = lay(far_data, far_rims)
    far_stk, auto = autos(far_even, far_odds, auto)
    auto_far = swap(auto, "chan", 1)
    numer = numers(far_stk, far_laid, numer)
    numer_far = swap(numer, "chan", 1)

    grams = [gram]

    def tail_of(bits_now):
        tail = call(
            functools.partial(tail_body, plan, shards),
            sds((REACH, width), F32),
            smem() + vmem(3),
        )(place, bits_now, stk, far_stk)
        return tail, swap(tail, "chan", 1)

    mats = sds(((REACH + 1) * width, width), BF16)
    every = list(range(-REACH, REACH + 1))
    high, low, den = call(
        functools.partial(first_conv_body, plan, every),
        (mats, mats, sds((rows, width), F32)),
        vmem(3),
        [pltpu.VMEM((factors, (REACH + 2) * width), F32)],
    )(auto, auto_far, bits_x)

    def conv(offsets, bits_now, *before):
        return call(
            functools.partial(conv_body, plan, offsets), sds((rows, width), F32), vmem(3 + len(before))
        )(bits_now, high, low, *before)

    scale = PENALTY / (steps * shards)
    field, window = sds((rows, width), F32), sds((ext_rows, width), BF16)
    low_field = sds((rows, width), BF16)
    numers_now = (numer, numer_far)
    for sweep in range(ITERS):
        if sweep == 0:
            tails = tail_of(bits_x)
        else:
            tails = tail_of(bits_x)
            part = conv(every[:REACH], bits_x)
            den = conv(every[REACH:], bits_x, part)
            grams = gram_rounds(gram, odd, [lambda: (part,), lambda: (den,)])
        operands = (place, x, bits_x, low_x, den, *numers_now, *tails, *grams)
        counts = (len(numers_now), len(grams))
        if sweep == ITERS - 1:
            return call(
                functools.partial(last_body, plan, scale, shards, counts),
                sds((factors, steps), F32),
                smem() + vmem(len(operands) - 1),
                [pltpu.VMEM((rows, width), F32), pltpu.VMEM((steps + 2 * LANES, LANES), F32)],
            )(*operands)
        outs = (field, window, low_field, sds((factors, factors), F32))
        if counts[0] > 1:
            outs = (field,) + outs
        got = call(
            functools.partial(update_body, plan, scale, shards, counts),
            outs,
            smem() + vmem(len(operands) - 1),
            [pltpu.VMEM((rows, width), F32), pltpu.VMEM((rows, 2 * width), BF16)],
        )(*operands)
        if counts[0] > 1:
            numers_now, got = got[:1], got[1:]
        x, bits_x, low_x, gram = got


def solution(mesh):
    in_specs = (P("chan", "tm"), P("chan", "tm"), P(None, "tm"))
    out_specs = P(None, "tm")
    return jax.shard_map(
        on_device, mesh=mesh, in_specs=in_specs, out_specs=out_specs, check_vma=False
    )
```

profile of v0, /device:TPU:0, one launch (start us, length us, event | category | flops | bytes accessed | tf_op | source)
XLA Modules:
  0.0 76.3 jit_solution(9884202008060938720)
XLA Ops:
  0.0 3.0 %collective-permute-start = (bf16[1,96,256]{2,1,0:T(8,128)(2,1)}, bf16[1,96,256]{2,1,0:T(8,128)(2,1)S(1)}, u32[]{:S(2)}, u32[]{:S(2)}) collective-permute-start(bf16[1,96,256]{2,1,0:T(8,128)(2,1)} %bitcast.9), channel_id=1, source_target_pairs={{0,8},{4,12},{8,0},{12,4},{16,24},{20,28},{24,16},{28,20},{1,9},{5... | collective-permute-start | bytes 147464 | tf_op jit(solution)/shard_map/ppermute | solution.py:375
  4.5 3.9 %collective-permute-done.1 = f32[64,64]{1,0:T(8,128)S(1)} collective-permute-done((f32[64,64]{1,0:T(8,128)S(1)}, f32[64,64]{1,0:T(8,128)S(1)}, u32[]{:S(2)}, u32[]{:S(2)}) %collective-permute-start.1) | collective-permute-done | bytes 16416 | tf_op jit(solution)/shard_map/ppermute | solution.py:375
  9.2 2.7 %collective-permute-start.2 = (bf16[2,96,256]{2,1,0:T(8,128)(2,1)S(1)}, bf16[2,96,256]{2,1,0:T(8,128)(2,1)S(1)}, u32[]{:S(2)}, u32[]{:S(2)}) collective-permute-start(bf16[2,96,256]{2,1,0:T(8,128)(2,1)S(1)} %pad_maximum_fusion.1.even_ref), channel_id=1, source_target_pairs={{0,16},{4,20},{8,24},{12,28},{16,0},{20,4},{24,8},{28,12},{1,17},{... | collective-permute-start | bytes 294920 | tf_op jit(solution)/shard_map/ppermute | solution.py:375
  14.2 1.6 %collective-permute-start.9 = (bf16[96,2048]{1,0:T(8,128)(2,1)S(1)}, bf16[96,2048]{1,0:T(8,128)(2,1)S(1)}, u32[]{:S(2)}, u32[]{:S(2)}) collective-permute-start(bf16[96,2048]{1,0:T(8,128)(2,1)S(1)} %copy-done.2), channel_id=1, source_target_pairs={{0,2},{1,3},{2,0},{3,1},{4,6},{5,7},{6,4},{7,5},{8,10},{9,11},{10,... | collective-permute-start | bytes 1179656 | tf_op jit(solution)/shard_map/ppermute | solution.py:375
  15.8 3.5 %collective-permute-start.3 = (f32[64,64]{1,0:T(8,128)S(1)}, f32[64,64]{1,0:T(8,128)S(1)}, u32[]{:S(2)}, u32[]{:S(2)}) collective-permute-start(f32[64,64]{1,0:T(8,128)S(1)} %add.20), channel_id=1, source_target_pairs={{0,16},{4,20},{8,24},{12,28},{16,0},{20,4},{24,8},{28,12},{1,17},{... | collective-permute-start | bytes 49160 | tf_op jit(solution)/shard_map/ppermute | solution.py:375
  19.2 1.4 %collective-permute-start.8 = (f32[160,128]{1,0:T(8,128)S(1)}, f32[160,128]{1,0:T(8,128)S(1)}, u32[]{:S(2)}, u32[]{:S(2)}) collective-permute-start(f32[160,128]{1,0:T(8,128)S(1)} %get-tuple-element.46), channel_id=1, source_target_pairs={{0,4},{4,8},{8,12},{12,16},{16,20},{20,24},{24,28},{1,5},{5,9},{9,... | collective-permute-start | bytes 245768 | tf_op jit(solution)/shard_map/ppermute | solution.py:390
  22.9 2.0 %collective-permute-start.5 = (bf16[4,96,256]{2,1,0:T(8,128)(2,1)S(1)}, bf16[4,96,256]{2,1,0:T(8,128)(2,1)S(1)}, u32[]{:S(2)}, u32[]{:S(2)}) collective-permute-start(bf16[4,96,256]{2,1,0:T(8,128)(2,1)S(1)} %pad_maximum_fusion.even_ref), channel_id=1, source_target_pairs={{0,4},{4,0},{8,12},{12,8},{16,20},{20,16},{24,28},{28,24},{1,5},{5... | collective-permute-start | bytes 589832 | tf_op jit(solution)/shard_map/ppermute | solution.py:375
  25.0 4.0 %collective-permute-done.7 = f32[64,64]{1,0:T(8,128)S(1)} collective-permute-done((f32[64,64]{1,0:T(8,128)S(1)}, f32[64,64]{1,0:T(8,128)S(1)}, u32[]{:S(2)}, u32[]{:S(2)}) %collective-permute-start.7) | collective-permute-done | bytes 16416 | tf_op jit(solution)/shard_map/ppermute | solution.py:375
  29.0 1.5 %collective-permute-start.10 = (bf16[5,96,256]{2,1,0:T(8,128)(2,1)S(1)}, bf16[5,96,256]{2,1,0:T(8,128)(2,1)S(1)}, u32[]{:S(2)}, u32[]{:S(2)}) collective-permute-start(bf16[5,96,256]{2,1,0:T(8,128)(2,1)S(1)} %maximum_maximum_fusion), channel_id=1, source_target_pairs={{0,2},{1,3},{2,0},{3,1},{4,6},{5,7},{6,4},{7,5},{8,10},{9,11},{10,... | collective-permute-start | bytes 737288 | tf_op jit(solution)/shard_map/ppermute | solution.py:375
  31.1 2.1 %shard_map.40 = (bf16[256,4608]{1,0:T(8,128)(2,1)S(1)}, f32[512,256]{1,0:T(8,128)S(1)}) custom-call(s32[2]{0:T(128)S(1)} %pad_add_fusion.me_ref, bf16[4,96,256]{2,1,0:T(8,128)(2,1)S(1)} %pad_maximum_fusion.even_ref, bf16[4,96,256]{2,1,0:T(8,128)(2,1)S(1)} %collective-permute-done.5.odd_ref), custom_call_target="tpu_custom_call" | custom-call | tf_op jit(solution)/shard_map/pallas_call | solution.py:496
  33.2 1.5 %shard_map.45.refs_0_ = f32[544,256]{1,0:T(8,128)S(1)} custom-call(bf16[256,4608]{1,0:T(8,128)(2,1)S(1)} %get-tuple-element.60.stk_ref.refs_0_, bf16[672,512]{1,0:T(8,128)(2,1)S(1)} %shard_map.44.data_ref), custom_call_target="tpu_custom_call" | custom-call | tf_op jit(solution)/shard_map/pallas_call | solution.py:504
  35.7 2.1 %shard_map.41 = (bf16[256,4608]{1,0:T(8,128)(2,1)S(1)}, f32[512,256]{1,0:T(8,128)S(1)}) custom-call(s32[2]{0:T(128)S(1)} %pad_add_fusion.me_ref, bf16[4,96,256]{2,1,0:T(8,128)(2,1)S(1)} %collective-permute-done.6.even_ref, bf16[5,96,256]{2,1,0:T(8,128)(2,1)S(1)} %collective-permute-done.10.odd_ref, f32[512,256]{1,0:T(8,128)S(1)} %get-tuple-element.55.refs_0_), custom_call_target="tpu_custom_call" | custom-call | tf_op jit(solution)/shard_map/pallas_call | solution.py:496
  37.8 1.5 %shard_map.46.refs_0_ = f32[544,256]{1,0:T(8,128)S(1)} custom-call(bf16[256,4608]{1,0:T(8,128)(2,1)S(1)} %get-tuple-element.58.stk_ref.refs_1_, bf16[672,512]{1,0:T(8,128)(2,1)S(1)} %shard_map.43.data_ref, f32[544,256]{1,0:T(8,128)S(1)} %shard_map.45.refs_0_), custom_call_target="tpu_custom_call" | custom-call | tf_op jit(solution)/shard_map/pallas_call | solution.py:504
  42.1 3.0 %shard_map.42 = (bf16[2304,256]{1,0:T(8,128)(2,1)S(1)}, bf16[2304,256]{1,0:T(8,128)(2,1)S(1)}, f32[544,256]{1,0:T(8,128)S(1)}) custom-call(f32[512,256]{1,0:T(8,128)S(1)} %get-tuple-element.56.auto_a, f32[512,256]{1,0:T(8,128)S(1)} %collective-permute-done.11.auto_b, bf16[800,256]{1,0:T(8,128)(2,1)S(1)} %get-tuple-element.51.bits_ref), custom_call_target="tpu_custom_call" | custom-call | tf_op jit(solution)/shard_map/pallas_call | solution.py:528
  45.1 1.9 %shard_map.48 = (f32[544,256]{1,0:T(8,128)S(1)}, f32[544,256]{1,0:T(8,128)S(1)}, bf16[800,256]{1,0:T(8,128)(2,1)S(1)}, bf16[544,256]{1,0:T(8,128)(2,1)S(1)}, f32[64,64]{1,0:T(8,128)S(1)}) custom-call(s32[2]{0:T(128)S(1)} %pad_add_fusion.me_ref, f32[544,256]{1,0:T(8,128)S(1)} %get-tuple-element.50.x_ref, bf16[800,256]{1,0:T(8,128)(2,1)S(1)} %get-tuple-element.51.bits_ref, ...), custom_call_target="tpu_custom_call" | custom-call | tf_op jit(solution)/shard_map/pallas_call | solution.py:564
  47.0 2.0 %collective-permute-start.15 = (f32[64,64]{1,0:T(8,128)S(1)}, f32[64,64]{1,0:T(8,128)S(1)}, u32[]{:S(2)}, u32[]{:S(2)}) collective-permute-start(f32[64,64]{1,0:T(8,128)S(1)} %get-tuple-element.68), channel_id=1, source_target_pairs={{0,4},{4,0},{8,12},{12,8},{16,20},{20,16},{24,28},{28,24},{1,5},{5... | collective-permute-start | bytes 49160 | tf_op jit(solution)/shard_map/ppermute | solution.py:375
  51.0 2.6 %collective-permute-start.16 = (f32[64,64]{1,0:T(8,128)S(1)}, f32[64,64]{1,0:T(8,128)S(1)}, u32[]{:S(2)}, u32[]{:S(2)}) collective-permute-start(f32[64,64]{1,0:T(8,128)S(1)} %add.23.refs_3_), channel_id=1, source_target_pairs={{0,8},{1,17},{2,10},{3,19},{4,12},{5,21},{6,14},{7,23},{8,0},{9,25... | collective-permute-start | bytes 49160 | tf_op jit(solution)/shard_map/ppermute | solution.py:385
  53.7 1.5 %shard_map.50.den_ref = f32[544,256]{1,0:T(8,128)S(1)} custom-call(bf16[800,256]{1,0:T(8,128)(2,1)S(1)} %get-tuple-element.63.bits_ref, bf16[2304,256]{1,0:T(8,128)(2,1)S(1)} %get-tuple-element.65.high_ref, bf16[2304,256]{1,0:T(8,128)(2,1)S(1)} %get-tuple-element.66.low_ref, f32[544,256]{1,0:T(8,128)S(1)} %shard_map.49.refs_0_), custom_call_target="tpu_custom_call" | custom-call | tf_op jit(solution)/shard_map/pallas_call | solution.py:536
  58.5 2.4 %collective-permute-done.18.refs_6_ = f32[64,64]{1,0:T(8,128)S(1)} collective-permute-done((f32[64,64]{1,0:T(8,128)S(1)}, f32[64,64]{1,0:T(8,128)S(1)}, u32[]{:S(2)}, u32[]{:S(2)}) %collective-permute-start.18) | collective-permute-done | bytes 16416 | tf_op jit(solution)/shard_map/ppermute | solution.py:375
  60.9 1.9 %shard_map.52 = (f32[544,256]{1,0:T(8,128)S(1)}, bf16[800,256]{1,0:T(8,128)(2,1)S(1)}, bf16[544,256]{1,0:T(8,128)(2,1)S(1)}, f32[64,64]{1,0:T(8,128)S(1)}) custom-call(s32[2]{0:T(128)S(1)} %pad_add_fusion.me_ref, f32[544,256]{1,0:T(8,128)S(1)} %get-tuple-element.62.x_ref, bf16[800,256]{1,0:T(8,128)(2,1)S(1)} %get-tuple-element.63.bits_ref, ...), custom_call_target="tpu_custom_call" | custom-call | tf_op jit(solution)/shard_map/pallas_call | solution.py:564
  64.2 2.5 %collective-permute-done.20 = f32[64,64]{1,0:T(8,128)S(1)} collective-permute-done((f32[64,64]{1,0:T(8,128)S(1)}, f32[64,64]{1,0:T(8,128)S(1)}, u32[]{:S(2)}, u32[]{:S(2)}) %collective-permute-start.20) | collective-permute-done | bytes 16416 | tf_op jit(solution)/shard_map/ppermute | solution.py:375
  66.8 1.5 %shard_map.54.den_ref = f32[544,256]{1,0:T(8,128)S(1)} custom-call(bf16[800,256]{1,0:T(8,128)(2,1)S(1)} %get-tuple-element.72.bits_ref, bf16[2304,256]{1,0:T(8,128)(2,1)S(1)} %get-tuple-element.65.high_ref, bf16[2304,256]{1,0:T(8,128)(2,1)S(1)} %get-tuple-element.66.low_ref, f32[544,256]{1,0:T(8,128)S(1)} %shard_map.53.refs_0_), custom_call_target="tpu_custom_call" | custom-call | tf_op jit(solution)/shard_map/pallas_call | solution.py:536
  68.3 1.4 %collective-permute-start.23 = (f32[64,64]{1,0:T(8,128)S(1)}, f32[64,64]{1,0:T(8,128)S(1)}, u32[]{:S(2)}, u32[]{:S(2)}) collective-permute-start(f32[64,64]{1,0:T(8,128)S(1)} %add.24.refs_3_), channel_id=1, source_target_pairs={{0,24},{4,28},{8,16},{12,20},{16,8},{20,12},{24,0},{28,4},{1,25},{... | collective-permute-start | bytes 49160 | tf_op jit(solution)/shard_map/ppermute | solution.py:375
  74.1 2.2 %shard_map.56 = f32[64,2048]{1,0:T(8,128)} custom-call(s32[2]{0:T(128)S(1)} %pad_add_fusion.me_ref, f32[544,256]{1,0:T(8,128)S(1)} %get-tuple-element.71.x_ref, bf16[800,256]{1,0:T(8,128)(2,1)S(1)} %get-tuple-element.72.bits_ref, bf16[544,256]{1,0:T(8,128)(2,1)S(1)} %get-tuple-element.73.low_ref, f32[544,256]{1,0:T(8,128)S(1)} %shard_map.54.den_ref, ...), custom_call_target="tpu_custom_call" | custom-call | tf_op jit(solution)/shard_map/pallas_call | solution.py:555
  (67 shorter events, 22.4 us)
Async XLA Ops:
  0.0 8.4 %collective-permute-start = (bf16[1,96,256]{2,1,0:T(8,128)(2,1)}, bf16[1,96,256]{2,1,0:T(8,128)(2,1)S(1)}, u32[]{:S(2)}, u32[]{:S(2)}) collective-permute-start(bf16[1,96,256]{2,1,0:T(8,128)(2,1)} %bitcast.9), channel_id=1, source_target_pairs={{0,8},{4,12},{8,0},{12,4},{16,24},{20,28},{24,16},{28,20},{1,9},{5... | collective-permute-start | bytes 147464 | tf_op jit(solution)/shard_map/ppermute | solution.py:375
  4.4 4.0 %collective-permute-start.1 = (f32[64,64]{1,0:T(8,128)S(1)}, f32[64,64]{1,0:T(8,128)S(1)}, u32[]{:S(2)}, u32[]{:S(2)}) collective-permute-start(f32[64,64]{1,0:T(8,128)S(1)} %shard_map.37), channel_id=1, source_target_pairs={{0,8},{4,12},{8,0},{12,4},{16,24},{20,28},{24,16},{28,20},{1,9},{5... | collective-permute-start | bytes 49160 | tf_op jit(solution)/shard_map/ppermute | solution.py:375
  9.2 11.9 %collective-permute-start.2 = (bf16[2,96,256]{2,1,0:T(8,128)(2,1)S(1)}, bf16[2,96,256]{2,1,0:T(8,128)(2,1)S(1)}, u32[]{:S(2)}, u32[]{:S(2)}) collective-permute-start(bf16[2,96,256]{2,1,0:T(8,128)(2,1)S(1)} %pad_maximum_fusion.1.even_ref), channel_id=1, source_target_pairs={{0,16},{4,20},{8,24},{12,28},{16,0},{20,4},{24,8},{28,12},{1,17},{... | collective-permute-start | bytes 294920 | tf_op jit(solution)/shard_map/ppermute | solution.py:375
  12.9 8.2 %collective-permute-start.4 = (f32[160,128]{1,0:T(8,128)S(1)}, f32[160,128]{1,0:T(8,128)S(1)}, u32[]{:S(2)}, u32[]{:S(2)}) collective-permute-start(f32[160,128]{1,0:T(8,128)S(1)} %get-tuple-element.43), channel_id=1, source_target_pairs={{4,0},{8,4},{12,8},{16,12},{20,16},{24,20},{28,24},{5,1},{9,5},{13... | collective-permute-start | bytes 245768 | tf_op jit(solution)/shard_map/ppermute | solution.py:390
  14.2 14.8 %collective-permute-start.9 = (bf16[96,2048]{1,0:T(8,128)(2,1)S(1)}, bf16[96,2048]{1,0:T(8,128)(2,1)S(1)}, u32[]{:S(2)}, u32[]{:S(2)}) collective-permute-start(bf16[96,2048]{1,0:T(8,128)(2,1)S(1)} %copy-done.2), channel_id=1, source_target_pairs={{0,2},{1,3},{2,0},{3,1},{4,6},{5,7},{6,4},{7,5},{8,10},{9,11},{10,... | collective-permute-start | bytes 1179656 | tf_op jit(solution)/shard_map/ppermute | solution.py:375
  15.8 5.3 %collective-permute-start.3 = (f32[64,64]{1,0:T(8,128)S(1)}, f32[64,64]{1,0:T(8,128)S(1)}, u32[]{:S(2)}, u32[]{:S(2)}) collective-permute-start(f32[64,64]{1,0:T(8,128)S(1)} %add.20), channel_id=1, source_target_pairs={{0,16},{4,20},{8,24},{12,28},{16,0},{20,4},{24,8},{28,12},{1,17},{... | collective-permute-start | bytes 49160 | tf_op jit(solution)/shard_map/ppermute | solution.py:375
  19.2 5.7 %collective-permute-start.8 = (f32[160,128]{1,0:T(8,128)S(1)}, f32[160,128]{1,0:T(8,128)S(1)}, u32[]{:S(2)}, u32[]{:S(2)}) collective-permute-start(f32[160,128]{1,0:T(8,128)S(1)} %get-tuple-element.46), channel_id=1, source_target_pairs={{0,4},{4,8},{8,12},{12,16},{16,20},{20,24},{24,28},{1,5},{5,9},{9,... | collective-permute-start | bytes 245768 | tf_op jit(solution)/shard_map/ppermute | solution.py:390
  22.0 7.0 %collective-permute-start.6 = (bf16[4,96,256]{2,1,0:T(8,128)(2,1)S(1)}, bf16[4,96,256]{2,1,0:T(8,128)(2,1)S(1)}, u32[]{:S(2)}, u32[]{:S(2)}) collective-permute-start(bf16[4,96,256]{2,1,0:T(8,128)(2,1)S(1)} %pad_maximum_fusion.even_ref), channel_id=1, source_target_pairs={{0,2},{1,3},{2,0},{3,1},{4,6},{5,7},{6,4},{7,5},{8,10},{9,11},{10,... | collective-permute-start | bytes 589832 | tf_op jit(solution)/shard_map/ppermute | solution.py:375
  22.9 6.0 %collective-permute-start.5 = (bf16[4,96,256]{2,1,0:T(8,128)(2,1)S(1)}, bf16[4,96,256]{2,1,0:T(8,128)(2,1)S(1)}, u32[]{:S(2)}, u32[]{:S(2)}) collective-permute-start(bf16[4,96,256]{2,1,0:T(8,128)(2,1)S(1)} %pad_maximum_fusion.even_ref), channel_id=1, source_target_pairs={{0,4},{4,0},{8,12},{12,8},{16,20},{20,16},{24,28},{28,24},{1,5},{5... | collective-permute-start | bytes 589832 | tf_op jit(solution)/shard_map/ppermute | solution.py:375
  24.9 4.1 %collective-permute-start.7 = (f32[64,64]{1,0:T(8,128)S(1)}, f32[64,64]{1,0:T(8,128)S(1)}, u32[]{:S(2)}, u32[]{:S(2)}) collective-permute-start(f32[64,64]{1,0:T(8,128)S(1)} %add.21), channel_id=1, source_target_pairs={{0,4},{4,0},{8,12},{12,8},{16,20},{20,16},{24,28},{28,24},{1,5},{5... | collective-permute-start | bytes 49160 | tf_op jit(solution)/shard_map/ppermute | solution.py:375
  29.0 6.3 %collective-permute-start.10 = (bf16[5,96,256]{2,1,0:T(8,128)(2,1)S(1)}, bf16[5,96,256]{2,1,0:T(8,128)(2,1)S(1)}, u32[]{:S(2)}, u32[]{:S(2)}) collective-permute-start(bf16[5,96,256]{2,1,0:T(8,128)(2,1)S(1)} %maximum_maximum_fusion), channel_id=1, source_target_pairs={{0,2},{1,3},{2,0},{3,1},{4,6},{5,7},{6,4},{7,5},{8,10},{9,11},{10,... | collective-permute-start | bytes 737288 | tf_op jit(solution)/shard_map/ppermute | solution.py:375
  39.3 5.8 %collective-permute-start.12 = (f32[544,256]{1,0:T(8,128)S(1)}, f32[544,256]{1,0:T(8,128)S(1)}, u32[]{:S(2)}, u32[]{:S(2)}) collective-permute-start(f32[544,256]{1,0:T(8,128)S(1)} %shard_map.46.refs_0_), channel_id=1, source_target_pairs={{0,1},{1,0},{2,3},{3,2},{4,5},{5,4},{6,7},{7,6},{8,9},{9,8},{10,11... | collective-permute-start | bytes 1671176 | tf_op jit(solution)/shard_map/ppermute | solution.py:375
  39.4 2.7 %collective-permute-start.11 = (f32[512,256]{1,0:T(8,128)S(1)}, f32[512,256]{1,0:T(8,128)S(1)}, u32[]{:S(2)}, u32[]{:S(2)}) collective-permute-start(f32[512,256]{1,0:T(8,128)S(1)} %get-tuple-element.56.auto_a), channel_id=1, source_target_pairs={{0,1},{1,0},{2,3},{3,2},{4,5},{5,4},{6,7},{7,6},{8,9},{9,8},{10,11... | collective-permute-start | bytes 1572872 | tf_op jit(solution)/shard_map/ppermute | solution.py:375
  41.2 3.9 %collective-permute-start.13 = (f32[8,256]{1,0:T(8,128)S(1)}, f32[8,256]{1,0:T(8,128)S(1)}, u32[]{:S(2)}, u32[]{:S(2)}) collective-permute-start(f32[8,256]{1,0:T(8,128)S(1)} %shard_map.47.refs_2_), channel_id=1, source_target_pairs={{0,1},{1,0},{2,3},{3,2},{4,5},{5,4},{6,7},{7,6},{8,9},{9,8},{10,11... | collective-permute-start | bytes 24584 | tf_op jit(solution)/shard_map/ppermute | solution.py:375
  47.0 4.0 %collective-permute-start.15 = (f32[64,64]{1,0:T(8,128)S(1)}, f32[64,64]{1,0:T(8,128)S(1)}, u32[]{:S(2)}, u32[]{:S(2)}) collective-permute-start(f32[64,64]{1,0:T(8,128)S(1)} %get-tuple-element.68), channel_id=1, source_target_pairs={{0,4},{4,0},{8,12},{12,8},{16,20},{20,16},{24,28},{28,24},{1,5},{5... | collective-permute-start | bytes 49160 | tf_op jit(solution)/shard_map/ppermute | solution.py:375
  51.0 5.5 %collective-permute-start.16 = (f32[64,64]{1,0:T(8,128)S(1)}, f32[64,64]{1,0:T(8,128)S(1)}, u32[]{:S(2)}, u32[]{:S(2)}) collective-permute-start(f32[64,64]{1,0:T(8,128)S(1)} %add.23.refs_3_), channel_id=1, source_target_pairs={{0,8},{1,17},{2,10},{3,19},{4,12},{5,21},{6,14},{7,23},{8,0},{9,25... | collective-permute-start | bytes 49160 | tf_op jit(solution)/shard_map/ppermute | solution.py:385
  55.1 5.8 %collective-permute-start.18 = (f32[64,64]{1,0:T(8,128)S(1)}, f32[64,64]{1,0:T(8,128)S(1)}, u32[]{:S(2)}, u32[]{:S(2)}) collective-permute-start(f32[64,64]{1,0:T(8,128)S(1)} %add.23.refs_3_), channel_id=1, source_target_pairs={{0,24},{4,28},{8,16},{12,20},{16,8},{20,12},{24,0},{28,4},{1,25},{... | collective-permute-start | bytes 49160 | tf_op jit(solution)/shard_map/ppermute | solution.py:375
  56.5 4.4 %collective-permute-start.17 = (f32[64,64]{1,0:T(8,128)S(1)}, f32[64,64]{1,0:T(8,128)S(1)}, u32[]{:S(2)}, u32[]{:S(2)}) collective-permute-start(f32[64,64]{1,0:T(8,128)S(1)} %collective-permute-done.16.refs_4_), channel_id=1, source_target_pairs={{0,1},{1,0},{2,3},{3,2},{4,5},{5,4},{6,7},{7,6},{8,9},{9,8},{10,11... | collective-permute-start | bytes 49160 | tf_op jit(solution)/shard_map/ppermute | solution.py:375
  57.1 1.4 %collective-permute-start.14 = (f32[8,256]{1,0:T(8,128)S(1)}, f32[8,256]{1,0:T(8,128)S(1)}, u32[]{:S(2)}, u32[]{:S(2)}) collective-permute-start(f32[8,256]{1,0:T(8,128)S(1)} %shard_map.51.refs_1_), channel_id=1, source_target_pairs={{0,1},{1,0},{2,3},{3,2},{4,5},{5,4},{6,7},{7,6},{8,9},{9,8},{10,11... | collective-permute-start | bytes 24584 | tf_op jit(solution)/shard_map/ppermute | solution.py:375
  62.8 4.0 %collective-permute-start.20 = (f32[64,64]{1,0:T(8,128)S(1)}, f32[64,64]{1,0:T(8,128)S(1)}, u32[]{:S(2)}, u32[]{:S(2)}) collective-permute-start(f32[64,64]{1,0:T(8,128)S(1)} %get-tuple-element.74), channel_id=1, source_target_pairs={{0,4},{4,0},{8,12},{12,8},{16,20},{20,16},{24,28},{28,24},{1,5},{5... | collective-permute-start | bytes 49160 | tf_op jit(solution)/shard_map/ppermute | solution.py:375
  66.8 4.2 %collective-permute-start.21 = (f32[64,64]{1,0:T(8,128)S(1)}, f32[64,64]{1,0:T(8,128)S(1)}, u32[]{:S(2)}, u32[]{:S(2)}) collective-permute-start(f32[64,64]{1,0:T(8,128)S(1)} %add.24.refs_3_), channel_id=1, source_target_pairs={{0,8},{1,17},{2,10},{3,19},{4,12},{5,21},{6,14},{7,23},{8,0},{9,25... | collective-permute-start | bytes 49160 | tf_op jit(solution)/shard_map/ppermute | solution.py:385
  68.3 5.8 %collective-permute-start.23 = (f32[64,64]{1,0:T(8,128)S(1)}, f32[64,64]{1,0:T(8,128)S(1)}, u32[]{:S(2)}, u32[]{:S(2)}) collective-permute-start(f32[64,64]{1,0:T(8,128)S(1)} %add.24.refs_3_), channel_id=1, source_target_pairs={{0,24},{4,28},{8,16},{12,20},{16,8},{20,12},{24,0},{28,4},{1,25},{... | collective-permute-start | bytes 49160 | tf_op jit(solution)/shard_map/ppermute | solution.py:375
  71.0 3.1 %collective-permute-start.22 = (f32[64,64]{1,0:T(8,128)S(1)}, f32[64,64]{1,0:T(8,128)S(1)}, u32[]{:S(2)}, u32[]{:S(2)}) collective-permute-start(f32[64,64]{1,0:T(8,128)S(1)} %collective-permute-done.21.refs_4_), channel_id=1, source_target_pairs={{0,1},{1,0},{2,3},{3,2},{4,5},{5,4},{6,7},{7,6},{8,9},{9,8},{10,11... | collective-permute-start | bytes 49160 | tf_op jit(solution)/shard_map/ppermute | solution.py:375
  71.6 1.4 %collective-permute-start.19 = (f32[8,256]{1,0:T(8,128)S(1)}, f32[8,256]{1,0:T(8,128)S(1)}, u32[]{:S(2)}, u32[]{:S(2)}) collective-permute-start(f32[8,256]{1,0:T(8,128)S(1)} %shard_map.55.refs_1_), channel_id=1, source_target_pairs={{0,1},{1,0},{2,3},{3,2},{4,5},{5,4},{6,7},{7,6},{8,9},{9,8},{10,11... | collective-permute-start | bytes 24584 | tf_op jit(solution)/shard_map/ppermute | solution.py:375
  (4 other events, 32.8 us)
where the time goes:
time: 76.6 us; the launch traced here: 76.3 us
  starting transfers between devices  27.4 us (36%)
  Pallas kernels  25.4 us (33%)
  waiting for transfers between devices  19.3 us (25%)
  local copies, waits for them, and re-layouts  2.07 us (3%)
  other arithmetic  1.76 us (2%)
    ppermute x20, starting transfers between devices, swap(): return lax.ppermute(x, axis, [(i, i ^ bit) for i in range(count)])  22.1 us
    ppermute x20, waiting for transfers between devices, swap(): return lax.ppermute(x, axis, [(i, i ^ bit) for i in range(count)])  18 us
    pallas_call x4, Pallas kernels, conv(): call(functools.partial(conv_body, plan, offsets), sds((rows, width), F32)...  5.62 us
    pallas_call x2, Pallas kernels, autos(): call(functools.partial(auto_body, plan), (sds((width, plan.tiles * LANES)...  4.21 us
    pallas_call x2, Pallas kernels, on_device(): call(functools.partial(update_body, plan, scale, shards, counts), outs, s...  3.81 us
    pallas_call x2, Pallas kernels, numers(): call(functools.partial(numer_body, plan), sds((rows, width), F32), vmem(2...  2.97 us
    pallas_call x1, Pallas kernels, on_device(): call(functools.partial(first_conv_body, plan, every), (mats, mats, sds((r...  2.97 us
    ppermute x2, starting transfers between devices, shifted(): lax.ppermute(x, axis, [(i, i + by) for i in range(count) if 0 <= i + by <...  2.71 us
  transfers between devices with their start and end apart: 24, of which 12 were waited for; matrix products, arithmetic and copies ran while one was open for 1% of the time, Pallas kernels for 20%

commit v1 on v0

--- a/solution.py
+++ b/solution.py
@@ -99,7 +99,8 @@
         bits_ref[row_tile(m + plan.per + REACH), :] = high.astype(BF16)
 
 
-def lay_loadings(plan, load_ref, left_ref, right_ref, x_ref, bits_ref, low_ref, buf):
+def lay_loadings(plan, shards, me_ref, load_ref, left_ref, right_ref, stk_a, stk_b, *refs):
+    x_ref, bits_ref, low_ref, tail_ref, buf, past, ahead = refs
     factors = plan.factors
     turned(buf, left_ref[:factors, :], load_ref, right_ref[:factors, :], plan.steps // LANES)
     lane = lax.broadcasted_iota(jnp.int32, (CHUNKS, LANES), 1)
@@ -117,6 +118,7 @@
         if REACH <= m < REACH + plan.per:
             x_ref[row_tile(m - REACH), :] = tile
             low_ref[row_tile(m - REACH), :] = (tile - bits.astype(F32)).astype(BF16)
+    tail_body(plan, shards, me_ref, bits_ref, (stk_a, stk_b), tail_ref, past, ahead)
 
 
 def lay_data(plan, data_ref, rims_ref, out_ref, buf):
@@ -128,18 +130,29 @@
             out_ref[row_tile(m), at] = buf[rows, :].astype(BF16)
 
 
-def first_gram(load_ref, out_ref):
+def first_body(plan, me_ref, load_any, data_any, motif_any, *refs):
+    motif_ref, gram_ref, near_ref, wide_ref, load_ref, data_ref, sems = refs
+    factors = plan.factors
+    moves = [
+        pltpu.make_async_copy(source, target, sems.at[i])
+        for i, (source, target) in enumerate(
+            ((load_any, load_ref), (data_any, data_ref), (motif_any, motif_ref.at[0]))
+        )
+    ]
+    for move in moves:
+        move.start()
+    for move in moves:
+        move.wait()
+    odd = me_ref[0] % 2 == 1
+    head, tail = slice(0, LANES), slice(plan.steps - LANES, plan.steps)
+    for rim_ref, even_at, odd_at in ((near_ref, tail, head), (wide_ref, head, tail)):
+        rim_ref[:factors, :] = jnp.where(odd, load_ref[:, odd_at], load_ref[:, even_at])
+        rim_ref[factors:, :] = jnp.where(
+            odd, data_ref[:, odd_at].astype(F32), data_ref[:, even_at].astype(F32)
+        )
     high, low = split(load_ref[...])
     cross = dot(high, low, NT)
-    out_ref[...] = dot(high, high, NT) + cross + cross.T
-
-
-def rim_body(plan, load_ref, data_ref, even_ref, tail_ref, head_ref):
-    factors = plan.factors
-    ends = ((tail_ref, slice(plan.steps - LANES, plan.steps)), (head_ref, slice(0, LANES)))
-    for rim_ref, at in ends:
-        rim_ref[:factors, :] = load_ref[:, at]
-        rim_ref[factors:, :] = data_ref[:, at].astype(F32)
+    gram_ref[...] = dot(high, high, NT) + cross + cross.T
 
 
 def lay_motifs(plan, me_ref, even_ref, odd_ref, stk_ref, padded):
@@ -200,36 +213,53 @@
             numer_ref[...] = part + before[0][...] if before else part
 
 
-def tail_part(plan, stk_ref, bits_ref):
-    width = plan.width
-    deep = PHASES * LANES
-    start = (plan.steps // PHASES + plan.edge) - (CHUNKS - 1) * plan.per + REACH
-    inside = [
-        bits_ref[row_tile(start - REACH + i), :].astype(F32)[CHUNKS - 1 :] for i in range(REACH)
-    ]
-    known = jnp.concatenate(inside + [jnp.zeros((REACH, width), F32)], 0)
-    ahead = jnp.zeros((REACH, deep), F32)
-    for s in range(1, REACH + 1):
-        rows = known[REACH - s : 2 * REACH - s].astype(BF16)
-        ahead += dot(rows, stk_ref[:, s * deep : (s + 1) * deep])
-    blank = jnp.zeros((REACH, deep), F32)
-    high = ahead.astype(BF16).astype(F32)
-    high, low = jnp.concatenate([blank, high], 0), jnp.concatenate([blank, ahead - high], 0)
-    out = jnp.zeros((2 * REACH, width), F32)
-    for s in range(1, REACH + 1):
-        both = jnp.concatenate([high[s : s + REACH], low[s : s + REACH]], 0).astype(BF16)
-        out += dot(both, stk_ref[:, s * deep : (s + 1) * deep], NT)
-    return out[:REACH] + out[REACH:]
-
-
-def tail_body(plan, shards, me_ref, bits_ref, *refs):
-    stks, out_ref = refs[:-1], refs[-1]
+def tail_part(plan, stk_ref, past, ahead):
+    factors = plan.factors
+    group = 2 * LANES // factors
+    known = past[...]
+    total = jnp.zeros((LAGS, LANES), F32)
+    for first in range(0, LAGS, group):
+        lags = range(first, first + group)
+        rows = jnp.concatenate([known[LAGS - l : 2 * LAGS - l, :factors] for l in lags], 1)
+        mat = jnp.concatenate([stk_ref[:factors, l * LANES : (l + 1) * LANES] for l in lags], 0)
+        total += dot(rows.astype(BF16), mat)
+    ahead[LAGS:, :] = total
+    beyond = ahead[...]
+    high = beyond.astype(BF16).astype(F32)
+    low = beyond - high
+    out = jnp.zeros((2 * LAGS, factors), F32)
+    for first in range(0, LAGS, 2):
+        lags = range(first, first + 2)
+        rows = jnp.concatenate(
+            [jnp.concatenate([part[l : l + LAGS] for l in lags], 1) for part in (high, low)], 0
+        )
+        mat = stk_ref[:factors, first * LANES : (first + 2) * LANES]
+        out += dot(rows.astype(BF16), mat, NT)
+    return out[:LAGS] + out[LAGS:]
+
+
+def tail_body(plan, shards, me_ref, bits_ref, stks, out_ref, past, ahead):
     out_ref[...] = jnp.zeros_like(out_ref)
 
     @pl.when(me_ref[0] == shards - 1)
     def _():
-        for stk_ref in stks:
-            out_ref[...] += tail_part(plan, stk_ref, bits_ref)
+        factors = plan.factors
+        start = (plan.steps // PHASES + plan.edge) - (CHUNKS - 1) * plan.per
+        ends = [
+            bits_ref[row_tile(start + i), :].astype(F32)[CHUNKS - 1 :] for i in range(REACH)
+        ]
+        known = jnp.concatenate(ends, 0)
+        past[...] = jnp.zeros_like(past)
+        ahead[...] = jnp.zeros_like(ahead)
+        for p in range(PHASES):
+            part = known[:, p * factors : (p + 1) * factors]
+            part = jnp.concatenate([part, jnp.zeros((REACH, LANES - factors), F32)], 1)
+            past[pl.ds(p, REACH, stride=PHASES), :] = part
+        over = sum(tail_part(plan, stk_ref, past, ahead) for stk_ref in stks)
+        past[:LAGS, :] = jnp.concatenate([over, jnp.zeros((LAGS, LANES - factors), F32)], 1)
+        out_ref[...] = jnp.concatenate(
+            [past[pl.ds(p, REACH, stride=PHASES), :][:, :factors] for p in range(PHASES)], 1
+        )
 
 
 def taps_body(plan, auto_a, auto_b, high_ref, low_ref, line):
@@ -266,6 +296,12 @@
             out_ref[...] += part
         else:
             out_ref[...] = part + before[0][...] if before else part
+
+
+def conv_tail_body(plan, shards, offsets, me_ref, bits_ref, high_ref, low_ref, stk_a, stk_b, *refs):
+    out_ref, tail_ref, past, ahead = refs
+    tail_body(plan, shards, me_ref, bits_ref, (stk_a, stk_b), tail_ref, past, ahead)
+    conv_body(plan, offsets, bits_ref, high_ref, low_ref, out_ref)
 
 
 def first_conv_body(plan, offsets, auto_a, auto_b, bits_ref, high_ref, low_ref, out_ref, line):
@@ -390,6 +426,12 @@
     return lax.ppermute(x, axis, [(i, i + by) for i in range(count) if 0 <= i + by < count])
 
 
+def between(x, axis):
+    count = lax.axis_size(axis)
+    pairs = [(i, i + 1) for i in range(1, count - 1, 2)]
+    return lax.ppermute(x, axis, pairs + [(b, a) for a, b in pairs])
+
+
 def doubling(axis):
     count = lax.axis_size(axis)
     bits = [1 << b for b in range(count.bit_length() - 1)]
@@ -400,23 +442,23 @@
     return lax.optimization_barrier((x, *others))[0]
 
 
-def gram_rounds(x, odd, meanwhile):
+def gram_rounds(x, odd, *meanwhile):
     bits = doubling("tm")
     singles, pairs = bits[-1:], bits[:-1]
     if len(pairs) % 2:
         singles, pairs = singles + pairs[-1:], pairs[:-1]
     gaps = list(meanwhile)
 
-    def gap(y):
-        return after(y, *gaps.pop(0)()) if gaps else y
+    def gap(*values):
+        others = gaps.pop(0) if gaps else ()
+        return lax.optimization_barrier(values + others)[: len(values)]
 
     for bit in singles:
-        x = x + gap(swap(x, "tm", bit))
+        x = x + gap(swap(x, "tm", bit))[0]
     terms = [x]
     while pairs:
         one, two, pairs = pairs[0], pairs[1], pairs[2:]
-        here, both = mixed(x, one, two), swap(x, "tm", one ^ two)
-        here = gap(here)
+        here, both = gap(mixed(x, one, two), swap(x, "tm", one ^ two))
         far = swap(here, "chan", 1)
         terms = [x, here, far, both]
         if pairs:
@@ -437,31 +479,49 @@
     odd = place[1] == 1
 
     rim = sds((factors + channels, LANES), F32)
-    gram = call(first_gram, sds((factors, factors), F32), vmem())(loadings)
+    even, gram, near_rim, wide_rim = call(
+        functools.partial(first_body, plan),
+        (
+            sds((1,) + motifs.shape, BF16),
+            sds((factors, factors), F32),
+            rim,
+            rim,
+        ),
+        smem() + [pl.BlockSpec(memory_space=pltpu.HBM)] * 3,
+        [
+            pltpu.VMEM(loadings.shape, F32),
+            pltpu.VMEM(data.shape, BF16),
+            pltpu.SemaphoreType.DMA((3,)),
+        ],
+        limit=53,
+    )(place, loadings, data, motifs)
 
     start = place
     bits = doubling("tm")
-    even = motifs[None]
     for i, bit in enumerate(bits[:-1]):
-        near, gram_near = swap(even, "tm", bit), swap(gram, "tm", bit)
-        if i == 1:
-            near, gram_near, right = lax.optimization_barrier((near, gram_near, right))
-        else:
-            near, gram_near = lax.optimization_barrier((near, gram_near))
-        even, gram = jnp.concatenate([even, near], 0), gram + gram_near
-        if i == 0:
-            tail_rim, head_rim = call(functools.partial(rim_body, plan), (rim, rim), vmem(3))(
-                loadings, data, even
-            )
-            left, right = shifted(tail_rim, "tm", 1), shifted(head_rim, "tm", -1)
-            far_data = swap(after(data, even), "chan", 2)
+        near = swap(even if i else motifs[None], "tm", bit)
+        if i:
+            gram_near = swap(gram, "tm", bits[i - 1])
+            if i == 1:
+                wide_rim = between(wide_rim, "tm")
+                far_data = swap(after(data, even), "chan", 2)
+                near, gram_near, wide_rim = lax.optimization_barrier((near, gram_near, wide_rim))
+            else:
+                near, gram_near = lax.optimization_barrier((near, gram_near))
+            gram = gram + gram_near
+        even = jnp.concatenate([even, near], 0)
     odds = swap(even, "tm", bits[-1])
     far_even = swap(even, "chan", 2)
-    gram_near = swap(gram, "tm", bits[-1])
-    odds, far_even, gram_near, left, far_data = lax.optimization_barrier(
-        (odds, far_even, gram_near, left, far_data)
+    gram_near = swap(gram, "tm", bits[-2])
+    near_rim = swap(after(near_rim, even), "tm", 1)
+    odds, far_even, gram_near, near_rim, far_data = lax.optimization_barrier(
+        (odds, far_even, gram_near, near_rim, far_data)
     )
     gram = gram + gram_near
+    gram_near = swap(gram, "tm", bits[-1])
+    right_side = lax.axis_index("tm") % 2 == 1
+    left = jnp.where(right_side, near_rim, wide_rim)
+    right = jnp.where(right_side, wide_rim, near_rim)
     if motifs.shape[1] != GROUP * LAGS:
         order = [0]
         for bit in bits:
@@ -477,14 +537,10 @@
 
     rims = jnp.concatenate([left[factors:], right[factors:]], 1).astype(BF16)
     far_odds = swap(jnp.concatenate([odds, rims[None]], 0), "chan", 2)
+    far_odds, gram_near = lax.optimization_barrier((far_odds, gram_near))
+    gram = gram + gram_near
     far_rims = far_odds[-1]
 
-    x, bits_x, low_x = call(
-        functools.partial(lay_loadings, plan),
-        (sds((rows, width), F32), sds((ext_rows, width), BF16), sds((rows, width), BF16)),
-        vmem(3),
-        [pltpu.VMEM((steps + 2 * LANES, LANES), F32)],
-    )(loadings, left, right)
     lay = call(
         functools.partial(lay_data, plan),
         sds(((plan.per + REACH) * CHUNKS, PHASES * LANES), BF16),
@@ -507,21 +563,24 @@
 
     stk, auto = autos(even, odds)
     numer = numers(stk, lay(data, rims))
+    far_odds, numer = lax.optimization_barrier((far_odds, numer))
+    far_stk, auto = autos(far_even, far_odds, auto)
+    far_data, far_rims, auto = lax.optimization_barrier((far_data, far_rims, auto))
+    auto_far = swap(auto, "chan", 1)
+    field, window = sds((rows, width), F32), sds((ext_rows, width), BF16)
+    low_field, rest = sds((rows, width), BF16), sds((REACH, width), F32)
+    tail_room = [pltpu.VMEM((2 * LAGS, LANES), F32)] * 2
+    x, bits_x, low_x, tail = call(
+        functools.partial(lay_loadings, plan, shards),
+        (field, window, low_field, rest),
+        smem() + vmem(5),
+        [pltpu.VMEM((steps + 2 * LANES, LANES), F32)] + tail_room,
+    )(place, loadings, left, right, stk, far_stk)
     far_laid = lay(far_data, far_rims)
-    far_stk, auto = autos(far_even, far_odds, auto)
-    auto_far = swap(auto, "chan", 1)
+    far_laid, auto_far, x = lax.optimization_barrier((far_laid, auto_far, x))
     numer = numers(far_stk, far_laid, numer)
     numer_far = swap(numer, "chan", 1)
-
     grams = [gram]
-
-    def tail_of(bits_now):
-        tail = call(
-            functools.partial(tail_body, plan, shards),
-            sds((REACH, width), F32),
-            smem() + vmem(3),
-        )(place, bits_now, stk, far_stk)
-        return tail, swap(tail, "chan", 1)
 
     mats = sds(((REACH + 1) * width, width), BF16)
     every = list(range(-REACH, REACH + 1))
@@ -532,23 +591,29 @@
         [pltpu.VMEM((factors, (REACH + 2) * width), F32)],
     )(auto, auto_far, bits_x)
 
-    def conv(offsets, bits_now, *before):
+    def conv(offsets, bits_now, before):
+        return call(functools.partial(conv_body, plan, offsets), field, vmem(4))(
+            bits_now, high, low, before
+        )
+
+    def conv_tail(offsets, bits_now):
         return call(
-            functools.partial(conv_body, plan, offsets), sds((rows, width), F32), vmem(3 + len(before))
-        )(bits_now, high, low, *before)
+            functools.partial(conv_tail_body, plan, shards, offsets),
+            (field, rest),
+            smem() + vmem(5),
+            tail_room,
+        )(place, bits_now, high, low, stk, far_stk)
 
     scale = PENALTY / (steps * shards)
-    field, window = sds((rows, width), F32), sds((ext_rows, width), BF16)
-    low_field = sds((rows, width), BF16)
     numers_now = (numer, numer_far)
     for sweep in range(ITERS):
-        if sweep == 0:
-            tails = tail_of(bits_x)
+        if sweep:
+            part, tail = conv_tail(every[:REACH], bits_x)
+            tails = (tail, swap(tail, "chan", 1))
+            den = conv(every[REACH:], bits_x, part)
+            grams = gram_rounds(gram, odd, (part,), (den, tails[1]))
         else:
-            tails = tail_of(bits_x)
-            part = conv(every[:REACH], bits_x)
-            den = conv(every[REACH:], bits_x, part)
-            grams = gram_rounds(gram, odd, [lambda: (part,), lambda: (den,)])
+            tails = (tail, swap(tail, "chan", 1))
         operands = (place, x, bits_x, low_x, den, *numers_now, *tails, *grams)
         counts = (len(numers_now), len(grams))
         if sweep == ITERS - 1:

time: 76.6 us -> 72.1 us (0.941)
  waiting for transfers between devices: 19.3 us -> 15 us
  Pallas kernels: 25.4 us -> 28.1 us
  other arithmetic: 1.76 us -> 0.15 us
  local copies, waits for them, and re-layouts: 2.07 us -> 0.85 us
    ppermute x20 -> x21, starting transfers between devices: 22.1 us -> 26.7 us  [swap(): return lax.ppermute(x, axis, [(i, i ^ bit) for i in range(count)])]
    ppermute x20 -> x21, waiting for transfers between devices: 18 us -> 14.2 us  [swap(): return lax.ppermute(x, axis, [(i, i ^ bit) for i in range(count)])]
    ppermute x2, starting transfers between devices: 2.65 us -> 0.01 us  [mixed(): return lax.ppermute(x, ('tm', 'chan'), pairs)]
    ppermute x2 -> x1, starting transfers between devices: 2.71 us -> 0.65 us  [between(): return lax.ppermute(x, axis, pairs + [(b, a) for a, b in pairs])]
    pallas_call x10 -> x6, Pallas kernels: 8.38 us -> 10.1 us  [the longest x2 3.97 us: conv_tail(): call(functools.partial(conv_tail_body, plan, shards, offsets), (field, re...]
    concatenate x2 -> x0, other arithmetic: 1.63 us -> none  [on_device(): even, gram = (jnp.concatenate([even, near], 0), gram + gram_near)]
    unnamed x8 -> x5, local copies, waits for them, and re-layouts: 2.05 us -> 0.81 us
    pallas_call x1, Pallas kernels: 0.43 us -> 1.43 us  [on_device(): numer = numers(stk, lay(data, rims))]
  transfers between devices with their start and end apart: 24 -> 24, of which waited for: 12 -> 11; matrix products, arithmetic and copies ran while one was open for 1% -> 0% of each run, Pallas kernels for 20% -> 26%
where the time goes in v1:
time: 72.1 us; the launch traced here: 71.8 us
  Pallas kernels  28.1 us (39%)
  starting transfers between devices  27.4 us (38%)
  waiting for transfers between devices  15 us (21%)
  local copies, waits for them, and re-layouts  0.85 us (1%)
    ppermute x21, starting transfers between devices, swap(): return lax.ppermute(x, axis, [(i, i ^ bit) for i in range(count)])  26.7 us
    ppermute x21, waiting for transfers between devices, swap(): return lax.ppermute(x, axis, [(i, i ^ bit) for i in range(count)])  14.2 us
    pallas_call x2, Pallas kernels, autos(): call(functools.partial(auto_body, plan), (sds((width, plan.tiles * LANES)...  4.2 us
    pallas_call x2, Pallas kernels, conv_tail(): call(functools.partial(conv_tail_body, plan, shards, offsets), (field, re...  3.97 us
    pallas_call x2, Pallas kernels, on_device(): call(functools.partial(update_body, plan, scale, shards, counts), outs, s...  3.79 us
    pallas_call x1, Pallas kernels, on_device(): call(functools.partial(first_conv_body, plan, every), (mats, mats, sds((r...  2.98 us
    pallas_call x2, Pallas kernels, numers(): call(functools.partial(numer_body, plan), sds((rows, width), F32), vmem(2...  2.97 us
    pallas_call x2, Pallas kernels, conv(): call(functools.partial(conv_body, plan, offsets), field, vmem(4))  2.95 us
  transfers between devices with their start and end apart: 24, of which 11 were waited for; matrix products, arithmetic and copies ran while one was open for 0% of the time, Pallas kernels for 26%

profile of v1, /device:TPU:0, one launch (start us, length us, event | category | flops | bytes accessed | tf_op | source)
XLA Modules:
  0.0 71.8 jit_solution(7015855401217947716)
XLA Ops:
  0.0 3.0 %collective-permute-start = (bf16[1,96,256]{2,1,0:T(8,128)(2,1)}, bf16[1,96,256]{2,1,0:T(8,128)(2,1)S(1)}, u32[]{:S(2)}, u32[]{:S(2)}) collective-permute-start(bf16[1,96,256]{2,1,0:T(8,128)(2,1)} %bitcast.9), channel_id=1, source_target_pairs={{0,8},{4,12},{8,0},{12,4},{16,24},{20,28},{24,16},{28,20},{1,9},{5... | collective-permute-start | bytes 147464 | tf_op jit(solution)/shard_map/ppermute | solution.py:411
  3.9 2.1 %shard_map.37 = (bf16[1,96,256]{2,1,0:T(8,128)(2,1)S(1)}, f32[64,64]{1,0:T(8,128)S(1)}, f32[160,128]{1,0:T(8,128)S(1)}, f32[160,128]{1,0:T(8,128)S(1)}) custom-call(s32[2]{0:T(128)S(1)} %pad_add_fusion.me_ref, f32[64,2048]{1,0:T(8,128)} %load_ref.1, bf16[96,2048]{1,0:T(8,128)(2,1)} %data_ref.1, bf16[96,256]{1,0:T(8,128)(2,1)S(1)} %copy-done.1), custom_call_target="tpu_custom_call" | custom-call | tf_op jit(solution)/shard_map/pallas_call | solution.py:482
  6.0 2.7 %collective-permute-start.1 = (bf16[2,96,256]{2,1,0:T(8,128)(2,1)S(1)}, bf16[2,96,256]{2,1,0:T(8,128)(2,1)S(1)}, u32[]{:S(2)}, u32[]{:S(2)}) collective-permute-start(bf16[2,96,256]{2,1,0:T(8,128)(2,1)S(1)} %get-tuple-element.115), channel_id=1, source_target_pairs={{0,16},{4,20},{8,24},{12,28},{16,0},{20,4},{24,8},{28,12},{1,17},{... | collective-permute-start | bytes 294920 | tf_op jit(solution)/shard_map/ppermute | solution.py:411
  9.4 1.6 %collective-permute-start.8 = (bf16[96,2048]{1,0:T(8,128)(2,1)}, bf16[96,2048]{1,0:T(8,128)(2,1)S(1)}, u32[]{:S(2)}, u32[]{:S(2)}) collective-permute-start(bf16[96,2048]{1,0:T(8,128)(2,1)} %data_ref.1), channel_id=1, source_target_pairs={{0,2},{1,3},{2,0},{3,1},{4,6},{5,7},{6,4},{7,5},{8,10},{9,11},{10,... | collective-permute-start | bytes 1179656 | tf_op jit(solution)/shard_map/ppermute | solution.py:411
  10.9 4.2 %collective-permute-start.2 = (f32[64,64]{1,0:T(8,128)S(1)}, f32[64,64]{1,0:T(8,128)S(1)}, u32[]{:S(2)}, u32[]{:S(2)}) collective-permute-start(f32[64,64]{1,0:T(8,128)S(1)} %get-tuple-element.60), channel_id=1, source_target_pairs={{0,8},{4,12},{8,0},{12,4},{16,24},{20,28},{24,16},{28,20},{1,9},{5... | collective-permute-start | bytes 49160 | tf_op jit(solution)/shard_map/ppermute | solution.py:411
  15.1 1.9 %collective-permute-done.2 = f32[64,64]{1,0:T(8,128)S(1)} collective-permute-done((f32[64,64]{1,0:T(8,128)S(1)}, f32[64,64]{1,0:T(8,128)S(1)}, u32[]{:S(2)}, u32[]{:S(2)}) %collective-permute-start.2) | collective-permute-done | bytes 16416 | tf_op jit(solution)/shard_map/ppermute | solution.py:411
  17.9 1.5 %collective-permute-start.4 = (bf16[4,96,256]{2,1,0:T(8,128)(2,1)S(1)}, bf16[4,96,256]{2,1,0:T(8,128)(2,1)S(1)}, u32[]{:S(2)}, u32[]{:S(2)}) collective-permute-start(bf16[4,96,256]{2,1,0:T(8,128)(2,1)S(1)} %constant_dynamic-update-slice_fusion.2.even_ref), channel_id=1, source_target_pairs={{0,4},{4,0},{8,12},{12,8},{16,20},{20,16},{24,28},{28,24},{1,5},{5... | collective-permute-start | bytes 589832 | tf_op jit(solution)/shard_map/ppermute | solution.py:411
  19.9 2.5 %collective-permute-start.6 = (f32[64,64]{1,0:T(8,128)S(1)}, f32[64,64]{1,0:T(8,128)S(1)}, u32[]{:S(2)}, u32[]{:S(2)}) collective-permute-start(f32[64,64]{1,0:T(8,128)S(1)} %add.23), channel_id=1, source_target_pairs={{0,16},{4,20},{8,24},{12,28},{16,0},{20,4},{24,8},{28,12},{1,17},{... | collective-permute-start | bytes 49160 | tf_op jit(solution)/shard_map/ppermute | solution.py:411
  22.4 2.3 %collective-permute-done.6 = f32[64,64]{1,0:T(8,128)S(1)} collective-permute-done((f32[64,64]{1,0:T(8,128)S(1)}, f32[64,64]{1,0:T(8,128)S(1)}, u32[]{:S(2)}, u32[]{:S(2)}) %collective-permute-start.6) | collective-permute-done | bytes 16416 | tf_op jit(solution)/shard_map/ppermute | solution.py:411
  26.2 2.6 %collective-permute-start.10 = (f32[64,64]{1,0:T(8,128)S(1)}, f32[64,64]{1,0:T(8,128)S(1)}, u32[]{:S(2)}, u32[]{:S(2)}) collective-permute-start(f32[64,64]{1,0:T(8,128)S(1)} %add.25), channel_id=1, source_target_pairs={{0,4},{4,0},{8,12},{12,8},{16,20},{20,16},{24,28},{28,24},{1,5},{5... | collective-permute-start | bytes 49160 | tf_op jit(solution)/shard_map/ppermute | solution.py:411
  28.8 2.1 %shard_map.38 = (bf16[256,4608]{1,0:T(8,128)(2,1)S(1)}, f32[512,256]{1,0:T(8,128)S(1)}) custom-call(s32[2]{0:T(128)S(1)} %pad_add_fusion.me_ref, bf16[4,96,256]{2,1,0:T(8,128)(2,1)S(1)} %constant_dynamic-update-slice_fusion.2.even_ref, bf16[4,96,256]{2,1,0:T(8,128)(2,1)S(1)} %collective-permute-done.4.odd_ref), custom_call_target="tpu_custom_call" | custom-call | tf_op jit(solution)/shard_map/pallas_call | solution.py:552
  33.9 2.1 %shard_map.41 = (bf16[256,4608]{1,0:T(8,128)(2,1)S(1)}, f32[512,256]{1,0:T(8,128)S(1)}) custom-call(s32[2]{0:T(128)S(1)} %pad_add_fusion.me_ref, bf16[4,96,256]{2,1,0:T(8,128)(2,1)S(1)} %collective-permute-done.5.even_ref, bf16[5,96,256]{2,1,0:T(8,128)(2,1)S(1)} %collective-permute-done.9.odd_ref, f32[512,256]{1,0:T(8,128)S(1)} %get-tuple-element.76.refs_0_), custom_call_target="tpu_custom_call" | custom-call | tf_op jit(solution)/shard_map/pallas_call | solution.py:552
  38.0 1.5 %shard_map.45.refs_0_ = f32[544,256]{1,0:T(8,128)S(1)} custom-call(bf16[256,4608]{1,0:T(8,128)(2,1)S(1)} %get-tuple-element.81.stk_b.stk_ref, bf16[672,512]{1,0:T(8,128)(2,1)S(1)} %shard_map.42.data_ref, f32[544,256]{1,0:T(8,128)S(1)} %shard_map.40.refs_0_), custom_call_target="tpu_custom_call" | custom-call | tf_op jit(solution)/shard_map/pallas_call | solution.py:560
  40.0 3.0 %shard_map.44 = (bf16[2304,256]{1,0:T(8,128)(2,1)S(1)}, bf16[2304,256]{1,0:T(8,128)(2,1)S(1)}, f32[544,256]{1,0:T(8,128)S(1)}) custom-call(f32[512,256]{1,0:T(8,128)S(1)} %get-tuple-element.80.auto_a, f32[512,256]{1,0:T(8,128)S(1)} %collective-permute-done.11.auto_b, bf16[800,256]{1,0:T(8,128)(2,1)S(1)} %get-tuple-element.84.bits_ref), custom_call_target="tpu_custom_call" | custom-call | tf_op jit(solution)/shard_map/pallas_call | solution.py:587
  43.0 1.9 %shard_map.46 = (f32[544,256]{1,0:T(8,128)S(1)}, f32[544,256]{1,0:T(8,128)S(1)}, bf16[800,256]{1,0:T(8,128)(2,1)S(1)}, bf16[544,256]{1,0:T(8,128)(2,1)S(1)}, f32[64,64]{1,0:T(8,128)S(1)}) custom-call(s32[2]{0:T(128)S(1)} %pad_add_fusion.me_ref, f32[544,256]{1,0:T(8,128)S(1)} %get-tuple-element.83.x_ref, bf16[800,256]{1,0:T(8,128)(2,1)S(1)} %get-tuple-element.84.bits_ref, ...), custom_call_target="tpu_custom_call" | custom-call | tf_op jit(solution)/shard_map/pallas_call | solution.py:629
  45.0 2.1 %shard_map.47 = (f32[544,256]{1,0:T(8,128)S(1)}, f32[8,256]{1,0:T(8,128)S(1)}) custom-call(s32[2]{0:T(128)S(1)} %pad_add_fusion.me_ref, bf16[800,256]{1,0:T(8,128)(2,1)S(1)} %get-tuple-element.93.bits_ref, bf16[2304,256]{1,0:T(8,128)(2,1)S(1)} %get-tuple-element.95.high_ref, bf16[2304,256]{1,0:T(8,128)(2,1)S(1)} %get-tuple-element.96.low_ref, ...), custom_call_target="tpu_custom_call" | custom-call | tf_op jit(solution)/shard_map/pallas_call | solution.py:600
  47.1 1.8 %collective-permute-done.15 = f32[64,64]{1,0:T(8,128)S(1)} collective-permute-done((f32[64,64]{1,0:T(8,128)S(1)}, f32[64,64]{1,0:T(8,128)S(1)}, u32[]{:S(2)}, u32[]{:S(2)}) %collective-permute-start.15) | collective-permute-done | bytes 16416 | tf_op jit(solution)/shard_map/ppermute | solution.py:411
  48.9 2.1 %collective-permute-start.17 = (f32[64,64]{1,0:T(8,128)S(1)}, f32[64,64]{1,0:T(8,128)S(1)}, u32[]{:S(2)}, u32[]{:S(2)}) collective-permute-start(f32[64,64]{1,0:T(8,128)S(1)} %add.27.refs_3_), channel_id=1, source_target_pairs={{0,24},{4,28},{8,16},{12,20},{16,8},{20,12},{24,0},{28,4},{1,25},{... | collective-permute-start | bytes 49160 | tf_op jit(solution)/shard_map/ppermute | solution.py:411
  52.6 2.1 %collective-permute-done.17.refs_6_ = f32[64,64]{1,0:T(8,128)S(1)} collective-permute-done((f32[64,64]{1,0:T(8,128)S(1)}, f32[64,64]{1,0:T(8,128)S(1)}, u32[]{:S(2)}, u32[]{:S(2)}) %collective-permute-start.17) | collective-permute-done | bytes 16416 | tf_op jit(solution)/shard_map/ppermute | solution.py:411
  56.6 1.9 %shard_map.49 = (f32[544,256]{1,0:T(8,128)S(1)}, bf16[800,256]{1,0:T(8,128)(2,1)S(1)}, bf16[544,256]{1,0:T(8,128)(2,1)S(1)}, f32[64,64]{1,0:T(8,128)S(1)}) custom-call(s32[2]{0:T(128)S(1)} %pad_add_fusion.me_ref, f32[544,256]{1,0:T(8,128)S(1)} %get-tuple-element.92.x_ref, bf16[800,256]{1,0:T(8,128)(2,1)S(1)} %get-tuple-element.93.bits_ref, ...), custom_call_target="tpu_custom_call" | custom-call | tf_op jit(solution)/shard_map/pallas_call | solution.py:629
  59.9 1.9 %shard_map.50 = (f32[544,256]{1,0:T(8,128)S(1)}, f32[8,256]{1,0:T(8,128)S(1)}) custom-call(s32[2]{0:T(128)S(1)} %pad_add_fusion.me_ref, bf16[800,256]{1,0:T(8,128)(2,1)S(1)} %get-tuple-element.105.bits_ref, bf16[2304,256]{1,0:T(8,128)(2,1)S(1)} %get-tuple-element.95.high_ref, bf16[2304,256]{1,0:T(8,128)(2,1)S(1)} %get-tuple-element.96.low_ref, ...), custom_call_target="tpu_custom_call" | custom-call | tf_op jit(solution)/shard_map/pallas_call | solution.py:600
  62.4 1.7 %collective-permute-start.22 = (f32[64,64]{1,0:T(8,128)S(1)}, f32[64,64]{1,0:T(8,128)S(1)}, u32[]{:S(2)}, u32[]{:S(2)}) collective-permute-start(f32[64,64]{1,0:T(8,128)S(1)} %add.28.refs_3_), channel_id=1, source_target_pairs={{0,24},{4,28},{8,16},{12,20},{16,8},{20,12},{24,0},{28,4},{1,25},{... | collective-permute-start | bytes 49160 | tf_op jit(solution)/shard_map/ppermute | solution.py:411
  65.6 2.7 %collective-permute-done.22.refs_6_ = f32[64,64]{1,0:T(8,128)S(1)} collective-permute-done((f32[64,64]{1,0:T(8,128)S(1)}, f32[64,64]{1,0:T(8,128)S(1)}, u32[]{:S(2)}, u32[]{:S(2)}) %collective-permute-start.22) | collective-permute-done | bytes 16416 | tf_op jit(solution)/shard_map/ppermute | solution.py:411
  69.6 2.2 %shard_map.52 = f32[64,2048]{1,0:T(8,128)} custom-call(s32[2]{0:T(128)S(1)} %pad_add_fusion.me_ref, f32[544,256]{1,0:T(8,128)S(1)} %get-tuple-element.104.x_ref, bf16[800,256]{1,0:T(8,128)(2,1)S(1)} %get-tuple-element.105.bits_ref, bf16[544,256]{1,0:T(8,128)(2,1)S(1)} %get-tuple-element.106.low_ref, f32[544,256]{1,0:T(8,128)S(1)} %shard_map.51.den_ref, ...), custom_call_target="tpu_custom_call" | custom-call | tf_op jit(solution)/shard_map/pallas_call | solution.py:620
  (61 shorter events, 18.1 us)
Async XLA Ops:
  0.0 6.0 %collective-permute-start = (bf16[1,96,256]{2,1,0:T(8,128)(2,1)}, bf16[1,96,256]{2,1,0:T(8,128)(2,1)S(1)}, u32[]{:S(2)}, u32[]{:S(2)}) collective-permute-start(bf16[1,96,256]{2,1,0:T(8,128)(2,1)} %bitcast.9), channel_id=1, source_target_pairs={{0,8},{4,12},{8,0},{12,4},{16,24},{20,28},{24,16},{28,20},{1,9},{5... | collective-permute-start | bytes 147464 | tf_op jit(solution)/shard_map/ppermute | solution.py:411
  6.0 11.0 %collective-permute-start.1 = (bf16[2,96,256]{2,1,0:T(8,128)(2,1)S(1)}, bf16[2,96,256]{2,1,0:T(8,128)(2,1)S(1)}, u32[]{:S(2)}, u32[]{:S(2)}) collective-permute-start(bf16[2,96,256]{2,1,0:T(8,128)(2,1)S(1)} %get-tuple-element.115), channel_id=1, source_target_pairs={{0,16},{4,20},{8,24},{12,28},{16,0},{20,4},{24,8},{28,12},{1,17},{... | collective-permute-start | bytes 294920 | tf_op jit(solution)/shard_map/ppermute | solution.py:411
  8.7 8.3 %collective-permute-start.3 = (f32[160,128]{1,0:T(8,128)S(1)}, f32[160,128]{1,0:T(8,128)S(1)}, u32[]{:S(2)}, u32[]{:S(2)}) collective-permute-start(f32[160,128]{1,0:T(8,128)S(1)} %get-tuple-element.61), channel_id=1, source_target_pairs={{4,8},{12,16},{20,24},{8,4},{16,12},{24,20},{5,9},{13,17},{21,25},... | collective-permute-start | bytes 245768 | tf_op jit(solution)/shard_map/ppermute | solution.py:432
  9.4 15.4 %collective-permute-start.8 = (bf16[96,2048]{1,0:T(8,128)(2,1)}, bf16[96,2048]{1,0:T(8,128)(2,1)S(1)}, u32[]{:S(2)}, u32[]{:S(2)}) collective-permute-start(bf16[96,2048]{1,0:T(8,128)(2,1)} %data_ref.1), channel_id=1, source_target_pairs={{0,2},{1,3},{2,0},{3,1},{4,6},{5,7},{6,4},{7,5},{8,10},{9,11},{10,... | collective-permute-start | bytes 1179656 | tf_op jit(solution)/shard_map/ppermute | solution.py:411
  10.9 6.1 %collective-permute-start.2 = (f32[64,64]{1,0:T(8,128)S(1)}, f32[64,64]{1,0:T(8,128)S(1)}, u32[]{:S(2)}, u32[]{:S(2)}) collective-permute-start(f32[64,64]{1,0:T(8,128)S(1)} %get-tuple-element.60), channel_id=1, source_target_pairs={{0,8},{4,12},{8,0},{12,4},{16,24},{20,28},{24,16},{28,20},{1,9},{5... | collective-permute-start | bytes 49160 | tf_op jit(solution)/shard_map/ppermute | solution.py:411
  17.1 7.7 %collective-permute-start.5 = (bf16[4,96,256]{2,1,0:T(8,128)(2,1)S(1)}, bf16[4,96,256]{2,1,0:T(8,128)(2,1)S(1)}, u32[]{:S(2)}, u32[]{:S(2)}) collective-permute-start(bf16[4,96,256]{2,1,0:T(8,128)(2,1)S(1)} %constant_dynamic-update-slice_fusion.2.even_ref), channel_id=1, source_target_pairs={{0,2},{1,3},{2,0},{3,1},{4,6},{5,7},{6,4},{7,5},{8,10},{9,11},{10,... | collective-permute-start | bytes 589832 | tf_op jit(solution)/shard_map/ppermute | solution.py:411
  17.9 6.9 %collective-permute-start.4 = (bf16[4,96,256]{2,1,0:T(8,128)(2,1)S(1)}, bf16[4,96,256]{2,1,0:T(8,128)(2,1)S(1)}, u32[]{:S(2)}, u32[]{:S(2)}) collective-permute-start(bf16[4,96,256]{2,1,0:T(8,128)(2,1)S(1)} %constant_dynamic-update-slice_fusion.2.even_ref), channel_id=1, source_target_pairs={{0,4},{4,0},{8,12},{12,8},{16,20},{20,16},{24,28},{28,24},{1,5},{5... | collective-permute-start | bytes 589832 | tf_op jit(solution)/shard_map/ppermute | solution.py:411
  19.4 5.3 %collective-permute-start.7 = (f32[160,128]{1,0:T(8,128)S(1)}, f32[160,128]{1,0:T(8,128)S(1)}, u32[]{:S(2)}, u32[]{:S(2)}) collective-permute-start(f32[160,128]{1,0:T(8,128)S(1)} %get-tuple-element.65), channel_id=1, source_target_pairs={{0,4},{4,0},{8,12},{12,8},{16,20},{20,16},{24,28},{28,24},{1,5},{5... | collective-permute-start | bytes 245768 | tf_op jit(solution)/shard_map/ppermute | solution.py:411
  19.9 4.8 %collective-permute-start.6 = (f32[64,64]{1,0:T(8,128)S(1)}, f32[64,64]{1,0:T(8,128)S(1)}, u32[]{:S(2)}, u32[]{:S(2)}) collective-permute-start(f32[64,64]{1,0:T(8,128)S(1)} %add.23), channel_id=1, source_target_pairs={{0,16},{4,20},{8,24},{12,28},{16,0},{20,4},{24,8},{28,12},{1,17},{... | collective-permute-start | bytes 49160 | tf_op jit(solution)/shard_map/ppermute | solution.py:411
  24.9 9.0 %collective-permute-start.9 = (bf16[5,96,256]{2,1,0:T(8,128)(2,1)S(1)}, bf16[5,96,256]{2,1,0:T(8,128)(2,1)S(1)}, u32[]{:S(2)}, u32[]{:S(2)}) collective-permute-start(bf16[5,96,256]{2,1,0:T(8,128)(2,1)S(1)} %maximum_maximum_fusion), channel_id=1, source_target_pairs={{0,2},{1,3},{2,0},{3,1},{4,6},{5,7},{6,4},{7,5},{8,10},{9,11},{10,... | collective-permute-start | bytes 737288 | tf_op jit(solution)/shard_map/ppermute | solution.py:411
  26.2 7.6 %collective-permute-start.10 = (f32[64,64]{1,0:T(8,128)S(1)}, f32[64,64]{1,0:T(8,128)S(1)}, u32[]{:S(2)}, u32[]{:S(2)}) collective-permute-start(f32[64,64]{1,0:T(8,128)S(1)} %add.25), channel_id=1, source_target_pairs={{0,4},{4,0},{8,12},{12,8},{16,20},{20,16},{24,28},{28,24},{1,5},{5... | collective-permute-start | bytes 49160 | tf_op jit(solution)/shard_map/ppermute | solution.py:411
  36.0 2.0 %collective-permute-start.11 = (f32[512,256]{1,0:T(8,128)S(1)}, f32[512,256]{1,0:T(8,128)S(1)}, u32[]{:S(2)}, u32[]{:S(2)}) collective-permute-start(f32[512,256]{1,0:T(8,128)S(1)} %get-tuple-element.80.auto_a), channel_id=1, source_target_pairs={{0,1},{1,0},{2,3},{3,2},{4,5},{5,4},{6,7},{7,6},{8,9},{9,8},{10,11... | collective-permute-start | bytes 1572872 | tf_op jit(solution)/shard_map/ppermute | solution.py:411
  39.5 3.6 %collective-permute-start.12 = (f32[544,256]{1,0:T(8,128)S(1)}, f32[544,256]{1,0:T(8,128)S(1)}, u32[]{:S(2)}, u32[]{:S(2)}) collective-permute-start(f32[544,256]{1,0:T(8,128)S(1)} %shard_map.45.refs_0_), channel_id=1, source_target_pairs={{0,1},{1,0},{2,3},{3,2},{4,5},{5,4},{6,7},{7,6},{8,9},{9,8},{10,11... | collective-permute-start | bytes 1671176 | tf_op jit(solution)/shard_map/ppermute | solution.py:411
  39.7 3.3 %collective-permute-start.13 = (f32[8,256]{1,0:T(8,128)S(1)}, f32[8,256]{1,0:T(8,128)S(1)}, u32[]{:S(2)}, u32[]{:S(2)}) collective-permute-start(f32[8,256]{1,0:T(8,128)S(1)} %get-tuple-element.90.refs_2_), channel_id=1, source_target_pairs={{0,1},{1,0},{2,3},{3,2},{4,5},{5,4},{6,7},{7,6},{8,9},{9,8},{10,11... | collective-permute-start | bytes 24584 | tf_op jit(solution)/shard_map/ppermute | solution.py:411
  45.0 4.0 %collective-permute-start.15 = (f32[64,64]{1,0:T(8,128)S(1)}, f32[64,64]{1,0:T(8,128)S(1)}, u32[]{:S(2)}, u32[]{:S(2)}) collective-permute-start(f32[64,64]{1,0:T(8,128)S(1)} %get-tuple-element.100), channel_id=1, source_target_pairs={{0,4},{4,0},{8,12},{12,8},{16,20},{20,16},{24,28},{28,24},{1,5},{5... | collective-permute-start | bytes 49160 | tf_op jit(solution)/shard_map/ppermute | solution.py:411
  48.9 5.7 %collective-permute-start.17 = (f32[64,64]{1,0:T(8,128)S(1)}, f32[64,64]{1,0:T(8,128)S(1)}, u32[]{:S(2)}, u32[]{:S(2)}) collective-permute-start(f32[64,64]{1,0:T(8,128)S(1)} %add.27.refs_3_), channel_id=1, source_target_pairs={{0,24},{4,28},{8,16},{12,20},{16,8},{20,12},{24,0},{28,4},{1,25},{... | collective-permute-start | bytes 49160 | tf_op jit(solution)/shard_map/ppermute | solution.py:411
  51.1 4.3 %collective-permute-start.16 = (f32[64,64]{1,0:T(8,128)S(1)}, f32[64,64]{1,0:T(8,128)S(1)}, u32[]{:S(2)}, u32[]{:S(2)}) collective-permute-start(f32[64,64]{1,0:T(8,128)S(1)} %add.27.refs_3_), channel_id=1, source_target_pairs={{0,8},{1,17},{2,10},{3,19},{4,12},{5,21},{6,14},{7,23},{8,0},{9,25... | collective-permute-start | bytes 49160 | tf_op jit(solution)/shard_map/ppermute | solution.py:421
  51.1 1.5 %collective-permute-start.14 = (f32[8,256]{1,0:T(8,128)S(1)}, f32[8,256]{1,0:T(8,128)S(1)}, u32[]{:S(2)}, u32[]{:S(2)}) collective-permute-start(f32[8,256]{1,0:T(8,128)S(1)} %get-tuple-element.99.refs_1_), channel_id=1, source_target_pairs={{0,1},{1,0},{2,3},{3,2},{4,5},{5,4},{6,7},{7,6},{8,9},{9,8},{10,11... | collective-permute-start | bytes 24584 | tf_op jit(solution)/shard_map/ppermute | solution.py:411
  55.4 1.2 %collective-permute-start.18 = (f32[64,64]{1,0:T(8,128)S(1)}, f32[64,64]{1,0:T(8,128)S(1)}, u32[]{:S(2)}, u32[]{:S(2)}) collective-permute-start(f32[64,64]{1,0:T(8,128)S(1)} %collective-permute-done.16.refs_4_), channel_id=1, source_target_pairs={{0,1},{1,0},{2,3},{3,2},{4,5},{5,4},{6,7},{7,6},{8,9},{9,8},{10,11... | collective-permute-start | bytes 49160 | tf_op jit(solution)/shard_map/ppermute | solution.py:411
  58.5 4.0 %collective-permute-start.20 = (f32[64,64]{1,0:T(8,128)S(1)}, f32[64,64]{1,0:T(8,128)S(1)}, u32[]{:S(2)}, u32[]{:S(2)}) collective-permute-start(f32[64,64]{1,0:T(8,128)S(1)} %get-tuple-element.109), channel_id=1, source_target_pairs={{0,4},{4,0},{8,12},{12,8},{16,20},{20,16},{24,28},{28,24},{1,5},{5... | collective-permute-start | bytes 49160 | tf_op jit(solution)/shard_map/ppermute | solution.py:411
  62.4 5.8 %collective-permute-start.22 = (f32[64,64]{1,0:T(8,128)S(1)}, f32[64,64]{1,0:T(8,128)S(1)}, u32[]{:S(2)}, u32[]{:S(2)}) collective-permute-start(f32[64,64]{1,0:T(8,128)S(1)} %add.28.refs_3_), channel_id=1, source_target_pairs={{0,24},{4,28},{8,16},{12,20},{16,8},{20,12},{24,0},{28,4},{1,25},{... | collective-permute-start | bytes 49160 | tf_op jit(solution)/shard_map/ppermute | solution.py:411
  64.1 4.3 %collective-permute-start.21 = (f32[64,64]{1,0:T(8,128)S(1)}, f32[64,64]{1,0:T(8,128)S(1)}, u32[]{:S(2)}, u32[]{:S(2)}) collective-permute-start(f32[64,64]{1,0:T(8,128)S(1)} %add.28.refs_3_), channel_id=1, source_target_pairs={{0,8},{1,17},{2,10},{3,19},{4,12},{5,21},{6,14},{7,23},{8,0},{9,25... | collective-permute-start | bytes 49160 | tf_op jit(solution)/shard_map/ppermute | solution.py:421
  64.1 1.5 %collective-permute-start.19 = (f32[8,256]{1,0:T(8,128)S(1)}, f32[8,256]{1,0:T(8,128)S(1)}, u32[]{:S(2)}, u32[]{:S(2)}) collective-permute-start(f32[8,256]{1,0:T(8,128)S(1)} %get-tuple-element.108.refs_1_), channel_id=1, source_target_pairs={{0,1},{1,0},{2,3},{3,2},{4,5},{5,4},{6,7},{7,6},{8,9},{9,8},{10,11... | collective-permute-start | bytes 24584 | tf_op jit(solution)/shard_map/ppermute | solution.py:411
  68.4 1.2 %collective-permute-start.23 = (f32[64,64]{1,0:T(8,128)S(1)}, f32[64,64]{1,0:T(8,128)S(1)}, u32[]{:S(2)}, u32[]{:S(2)}) collective-permute-start(f32[64,64]{1,0:T(8,128)S(1)} %collective-permute-done.21.refs_4_), channel_id=1, source_target_pairs={{0,1},{1,0},{2,3},{3,2},{4,5},{5,4},{6,7},{7,6},{8,9},{9,8},{10,11... | collective-permute-start | bytes 49160 | tf_op jit(solution)/shard_map/ppermute | solution.py:411
  (2 other events, 4.5 us)

commit v2 on v1

--- a/solution.py
+++ b/solution.py
@@ -99,8 +99,7 @@
         bits_ref[row_tile(m + plan.per + REACH), :] = high.astype(BF16)
 
 
-def lay_loadings(plan, shards, me_ref, load_ref, left_ref, right_ref, stk_a, stk_b, *refs):
-    x_ref, bits_ref, low_ref, tail_ref, buf, past, ahead = refs
+def lay_loadings(plan, load_ref, left_ref, right_ref, x_ref, bits_ref, low_ref, buf):
     factors = plan.factors
     turned(buf, left_ref[:factors, :], load_ref, right_ref[:factors, :], plan.steps // LANES)
     lane = lax.broadcasted_iota(jnp.int32, (CHUNKS, LANES), 1)
@@ -118,7 +117,6 @@
         if REACH <= m < REACH + plan.per:
             x_ref[row_tile(m - REACH), :] = tile
             low_ref[row_tile(m - REACH), :] = (tile - bits.astype(F32)).astype(BF16)
-    tail_body(plan, shards, me_ref, bits_ref, (stk_a, stk_b), tail_ref, past, ahead)
 
 
 def lay_data(plan, data_ref, rims_ref, out_ref, buf):
@@ -130,8 +128,8 @@
             out_ref[row_tile(m), at] = buf[rows, :].astype(BF16)
 
 
-def first_body(plan, me_ref, load_any, data_any, motif_any, *refs):
-    motif_ref, gram_ref, near_ref, wide_ref, load_ref, data_ref, sems = refs
+def first_body(plan, load_any, data_any, motif_any, *refs):
+    data_ref, motif_ref, gram_ref, near_ref, wide_ref, load_ref, sems = refs
     factors = plan.factors
     moves = [
         pltpu.make_async_copy(source, target, sems.at[i])
@@ -143,7 +141,7 @@
         move.start()
     for move in moves:
         move.wait()
-    odd = me_ref[0] % 2 == 1
+    odd = lax.axis_index("tm") % 2 == 1
     head, tail = slice(0, LANES), slice(plan.steps - LANES, plan.steps)
     for rim_ref, even_at, odd_at in ((near_ref, tail, head), (wide_ref, head, tail)):
         rim_ref[:factors, :] = jnp.where(odd, load_ref[:, odd_at], load_ref[:, even_at])
@@ -155,12 +153,11 @@
     gram_ref[...] = dot(high, high, NT) + cross + cross.T
 
 
-def lay_motifs(plan, me_ref, even_ref, odd_ref, stk_ref, padded):
+def lay_motifs(plan, me, even_ref, odd_ref, stk_ref, padded):
     factors = plan.factors
     channels = even_ref.shape[1]
     span = GROUP * LAGS
-    me = me_ref[0]
-    padded[channels:, :] = jnp.zeros((LANES - channels, 2 * span), BF16)
+    padded[channels:, :] = jnp.zeros((LANES - channels, padded.shape[1]), BF16)
     row = lax.broadcasted_iota(jnp.int32, (span, span), 0)
     col = lax.broadcasted_iota(jnp.int32, (span, span), 1)
     pick = jnp.where(col == (row % GROUP) * LAGS + row // GROUP, 1.0, 0.0).astype(BF16)
@@ -173,9 +170,10 @@
     for pair in range(factors // (2 * GROUP)):
         at = (me // 2) ^ pair
         one, two = even_ref[at].astype(F32), odd_ref[at].astype(F32)
-        padded[:channels, :span] = jnp.where(swapped == 1, two, one).astype(BF16)
-        padded[:channels, span:] = jnp.where(swapped == 1, one, two).astype(BF16)
-        halves = [dot(pick, padded[:, h * span : (h + 1) * span], NT) for h in range(2)]
+        room = slice(2 * pair * span, (2 * pair + 1) * span), slice((2 * pair + 1) * span, (2 * pair + 2) * span)
+        padded[:channels, room[0]] = jnp.where(swapped == 1, two, one).astype(BF16)
+        padded[:channels, room[1]] = jnp.where(swapped == 1, one, two).astype(BF16)
+        halves = [dot(pick, padded[:, at], NT) for at in room]
         for lag in range(LAGS):
             cut = slice(lag * GROUP, (lag + 1) * GROUP)
             tile = jnp.concatenate([halves[0][cut], halves[1][cut]], 0).astype(BF16)
@@ -184,25 +182,22 @@
                 stk_ref[first : first + 2 * GROUP, (lag + q) * LANES : (lag + q + 1) * LANES] = tile
 
 
-def auto_body(plan, me_ref, even_ref, odd_ref, *refs):
+def auto_body(plan, moved, even_ref, odd_ref, *refs):
     before, (stk_ref, auto_ref, padded) = refs[:-3], refs[-3:]
     factors = plan.factors
-    lay_motifs(plan, me_ref, even_ref, odd_ref, stk_ref, padded)
+    me = lax.axis_index("tm") if moved else 0
+    lay_motifs(plan, me, even_ref, odd_ref, stk_ref, padded)
     last = (PHASES - 1) * factors
-    chunk = 2 * LANES
-    shift = PHASES * LANES // chunk
+    deep = PHASES * LANES
     auto_ref[...] = before[0][...] if before else jnp.zeros_like(auto_ref)
-    for u in range(plan.tiles * LANES // chunk):
-        taps = min(u // shift + 1, REACH)
-        cuts = [u - shift * a for a in range(taps)]
-        left = [stk_ref[last : last + factors, c * chunk : (c + 1) * chunk] for c in cuts]
-        auto_ref[: taps * factors, :] += dot(
-            jnp.concatenate(left, 0), stk_ref[:, u * chunk : (u + 1) * chunk], NT
-        )
-
-
-def numer_body(plan, stk_ref, data_ref, *refs):
-    before, numer_ref = refs[:-1], refs[-1]
+    for u in range(REACH + 1):
+        taps = min(u + 1, REACH)
+        cuts = [slice((u - a) * deep, (u - a + 1) * deep) for a in range(taps)]
+        left = jnp.concatenate([stk_ref[last : last + factors, cut] for cut in cuts], 0)
+        auto_ref[: taps * factors, :] += dot(left, stk_ref[:, u * deep : (u + 1) * deep], NT)
+
+
+def numer_body(plan, stk_ref, data_ref, numer_ref, before=None):
     deep = PHASES * LANES
     for s in range(REACH + 1):
         rows = slice(s * CHUNKS, s * CHUNKS + plan.rows)
@@ -210,7 +205,13 @@
         if s:
             numer_ref[...] += part
         else:
-            numer_ref[...] = part + before[0][...] if before else part
+            numer_ref[...] = part if before is None else part + before[...]
+
+
+def numer_tail_body(plan, shards, stk_a, stk_b, data_ref, before, bits_ref, *refs):
+    numer_ref, tail_ref, past, ahead = refs
+    tail_body(plan, shards, bits_ref, (stk_a, stk_b), tail_ref, past, ahead)
+    numer_body(plan, stk_b, data_ref, numer_ref, before)
 
 
 def tail_part(plan, stk_ref, past, ahead):
@@ -238,10 +239,10 @@
     return out[:LAGS] + out[LAGS:]
 
 
-def tail_body(plan, shards, me_ref, bits_ref, stks, out_ref, past, ahead):
+def tail_body(plan, shards, bits_ref, stks, out_ref, past, ahead):
     out_ref[...] = jnp.zeros_like(out_ref)
 
-    @pl.when(me_ref[0] == shards - 1)
+    @pl.when(lax.axis_index("tm") == shards - 1)
     def _():
         factors = plan.factors
         start = (plan.steps // PHASES + plan.edge) - (CHUNKS - 1) * plan.per
@@ -298,9 +299,9 @@
             out_ref[...] = part + before[0][...] if before else part
 
 
-def conv_tail_body(plan, shards, offsets, me_ref, bits_ref, high_ref, low_ref, stk_a, stk_b, *refs):
+def conv_tail_body(plan, shards, offsets, bits_ref, high_ref, low_ref, stk_a, stk_b, *refs):
     out_ref, tail_ref, past, ahead = refs
-    tail_body(plan, shards, me_ref, bits_ref, (stk_a, stk_b), tail_ref, past, ahead)
+    tail_body(plan, shards, bits_ref, (stk_a, stk_b), tail_ref, past, ahead)
     conv_body(plan, offsets, bits_ref, high_ref, low_ref, out_ref)
 
 
@@ -309,12 +310,12 @@
     conv_body(plan, offsets, bits_ref, high_ref, low_ref, out_ref)
 
 
-def penalties(plan, scale, me_ref, grams, bits_ref, low_ref):
+def penalties(plan, scale, grams, bits_ref, low_ref):
     factors, rows = plan.factors, plan.rows
     total = grams[0][...]
     if len(grams) > 1:
         here, far, both = (g[...] for g in grams[1:])
-        odd = me_ref[1] == 1
+        odd = lax.axis_index("chan") % 2 == 1
         near = jnp.where(odd, far, here)
         next_one = jnp.where(odd, here, far)
         total = (total + near) + (next_one + both)
@@ -335,7 +336,7 @@
     return dot(bits, high) + dot(bits, low) + dot(low_ref[...], high)
 
 
-def new_tile(plan, shards, me_ref, m, x_ref, den_ref, numer, pen, tails):
+def new_tile(plan, shards, me, m, x_ref, den_ref, numer, pen, tails):
     at = row_tile(m)
     den = den_ref[at, :] + pen[at, :]
     j = lax.broadcasted_iota(jnp.int32, den.shape, 0)
@@ -343,23 +344,24 @@
     if end - REACH <= m < end:
         i = m - end + REACH
         over = tails[0][i : i + 1, :] + tails[1][i : i + 1, :]
-        den -= jnp.where((j == CHUNKS - 1) & (me_ref[0] == shards - 1), over, 0.0)
+        den -= jnp.where((j == CHUNKS - 1) & (me == shards - 1), over, 0.0)
     new = x_ref[at, :] * numer / den
     if m < plan.edge:
-        new = jnp.where((j == 0) & (me_ref[0] == 0), 0.0, new)
+        new = jnp.where((j == 0) & (me == 0), 0.0, new)
     if m >= end:
-        new = jnp.where((j == CHUNKS - 1) & (me_ref[0] == shards - 1), 0.0, new)
+        new = jnp.where((j == CHUNKS - 1) & (me == shards - 1), 0.0, new)
     return new
 
 
-def update_body(plan, scale, shards, counts, me_ref, x_ref, bits_ref, low_ref, den_ref, *refs):
+def update_body(plan, scale, shards, counts, x_ref, bits_ref, low_ref, den_ref, *refs):
     numers, tails, grams = refs[: counts[0]], refs[counts[0] :][:2], refs[counts[0] + 2 :][: counts[1]]
     refs = refs[counts[0] + 2 + counts[1] :]
     if counts[0] > 1:
         numer_ref, refs = refs[0], refs[1:]
     out_ref, out_bits, out_low, gram_ref, pen, both = refs
     factors, width = plan.factors, plan.width
-    pen[...] = penalties(plan, scale, me_ref, grams, bits_ref, low_ref)
+    me = lax.axis_index("tm")
+    pen[...] = penalties(plan, scale, grams, bits_ref, low_ref)
     end = (plan.steps // PHASES + plan.edge) - (CHUNKS - 1) * plan.per
     for m in range(plan.per):
         at = row_tile(m)
@@ -367,7 +369,7 @@
         if counts[0] > 1:
             numer = numer + numers[1][at, :]
             numer_ref[at, :] = numer
-        new = new_tile(plan, shards, me_ref, m, x_ref, den_ref, numer, pen, tails)
+        new = new_tile(plan, shards, me, m, x_ref, den_ref, numer, pen, tails)
         out_ref[at, :] = new
         spread(plan, new, m, out_bits)
         high, low = split(new)
@@ -381,21 +383,25 @@
         high, low = split(kept)
         both[at, :width] = high
         both[at, width:] = low
-    full = dot(both[:, :width], both[...], TN)
-    cross = full[:, width:]
-    full = full[:, :width] + cross + cross.T
-    gram_ref[...] = sum(
-        full[p * factors : (p + 1) * factors, p * factors : (p + 1) * factors] for p in range(PHASES)
-    )
-
-
-def last_body(plan, scale, shards, counts, me_ref, x_ref, bits_ref, low_ref, den_ref, *refs):
+    same, cross = 0.0, 0.0
+    for lanes in lane_tiles(width // LANES):
+        ahead = slice(width + lanes.start, width + lanes.stop)
+        full = dot(both[:, lanes], jnp.concatenate([both[:, lanes], both[:, ahead]], 1), TN)
+        for p in range(LANES // factors):
+            at = slice(p * factors, (p + 1) * factors)
+            same += full[at, at]
+            cross += full[at, LANES + at.start : LANES + at.stop]
+    gram_ref[...] = same + cross + cross.T
+
+
+def last_body(plan, scale, shards, counts, x_ref, bits_ref, low_ref, den_ref, *refs):
     numers, tails, grams = refs[: counts[0]], refs[counts[0] :][:2], refs[counts[0] + 2 :][: counts[1]]
     out_ref, pen, buf = refs[counts[0] + 2 + counts[1] :]
-    pen[...] = penalties(plan, scale, me_ref, grams, bits_ref, low_ref)
+    me = lax.axis_index("tm")
+    pen[...] = penalties(plan, scale, grams, bits_ref, low_ref)
     for m in range(plan.per):
         numer = sum(n[row_tile(m), :] for n in numers)
-        new = new_tile(plan, shards, me_ref, m, x_ref, den_ref, numer, pen, tails)
+        new = new_tile(plan, shards, me, m, x_ref, den_ref, numer, pen, tails)
         for h, lanes in enumerate(lane_tiles(PHASES // 2)):
             at = PHASES * m + 2 * h
             buf[pl.ds(at, CHUNKS, stride=plan.stride), :] = new[:, lanes]
@@ -475,28 +481,28 @@
     width, rows = plan.width, plan.rows
     ext_rows = plan.ext * CHUNKS
     sds = jax.ShapeDtypeStruct
-    place = jnp.stack([lax.axis_index("tm"), lax.axis_index("chan") % 2]).astype(jnp.int32)
-    odd = place[1] == 1
+    me = lax.axis_index("tm")
+    odd = lax.axis_index("chan") % 2 == 1
 
     rim = sds((factors + channels, LANES), F32)
-    even, gram, near_rim, wide_rim = call(
+    data_in, even, gram, near_rim, wide_rim = call(
         functools.partial(first_body, plan),
         (
+            sds(data.shape, BF16),
             sds((1,) + motifs.shape, BF16),
             sds((factors, factors), F32),
             rim,
             rim,
         ),
-        smem() + [pl.BlockSpec(memory_space=pltpu.HBM)] * 3,
+        [pl.BlockSpec(memory_space=pltpu.HBM)] * 3,
         [
             pltpu.VMEM(loadings.shape, F32),
-            pltpu.VMEM(data.shape, BF16),
             pltpu.SemaphoreType.DMA((3,)),
         ],
         limit=53,
-    )(place, loadings, data, motifs)
-
-    start = place
+    )(loadings, data, motifs)
+
+    moved = motifs.shape[1] == GROUP * LAGS
     bits = doubling("tm")
     for i, bit in enumerate(bits[:-1]):
         near = swap(even if i else motifs[None], "tm", bit)
@@ -504,8 +510,10 @@
             gram_near = swap(gram, "tm", bits[i - 1])
             if i == 1:
                 wide_rim = between(wide_rim, "tm")
-                far_data = swap(after(data, even), "chan", 2)
-                near, gram_near, wide_rim = lax.optimization_barrier((near, gram_near, wide_rim))
+                far_data = swap(after(data_in, even), "chan", 2)
+                near, gram_near, wide_rim, far_data = lax.optimization_barrier(
+                (near, gram_near, wide_rim, far_data)
+            )
             else:
                 near, gram_near = lax.optimization_barrier((near, gram_near))
             gram = gram + gram_near
@@ -514,32 +522,20 @@
     far_even = swap(even, "chan", 2)
     gram_near = swap(gram, "tm", bits[-2])
     near_rim = swap(after(near_rim, even), "tm", 1)
-    odds, far_even, gram_near, near_rim, far_data = lax.optimization_barrier(
-        (odds, far_even, gram_near, near_rim, far_data)
-    )
-    gram = gram + gram_near
-    gram_near = swap(gram, "tm", bits[-1])
-    right_side = lax.axis_index("tm") % 2 == 1
+    right_side = me % 2 == 1
     left = jnp.where(right_side, near_rim, wide_rim)
     right = jnp.where(right_side, wide_rim, near_rim)
-    if motifs.shape[1] != GROUP * LAGS:
+    if not moved:
         order = [0]
         for bit in bits:
             order = order + [o ^ bit for o in order]
         slots = jnp.concatenate([even, odds], 0)
         index = jnp.array([order.index(b) for b in range(shards)], jnp.int32)
-        slots = jnp.take(slots, jnp.take(index, jnp.arange(shards) ^ place[0]), axis=0)
+        slots = jnp.take(slots, jnp.take(index, jnp.arange(shards) ^ me), axis=0)
         slots = jnp.moveaxis(slots, 0, 1).reshape(channels, -1, GROUP * LAGS)
         slots = jnp.moveaxis(slots, 1, 0)
         even, odds = slots[0::2], slots[1::2]
-        start = place * 0
         far_even = swap(even, "chan", 2)
-
-    rims = jnp.concatenate([left[factors:], right[factors:]], 1).astype(BF16)
-    far_odds = swap(jnp.concatenate([odds, rims[None]], 0), "chan", 2)
-    far_odds, gram_near = lax.optimization_barrier((far_odds, gram_near))
-    gram = gram + gram_near
-    far_rims = far_odds[-1]
 
     lay = call(
         functools.partial(lay_data, plan),
@@ -548,37 +544,48 @@
         [pltpu.VMEM((steps + 2 * LANES, LANES), F32)],
     )
 
+    field, window = sds((rows, width), F32), sds((ext_rows, width), BF16)
+    low_field, rest = sds((rows, width), BF16), sds((REACH, width), F32)
+    tail_room = [pltpu.VMEM((2 * LAGS, LANES), F32)] * 2
+    rims = jnp.concatenate([left[factors:], right[factors:]], 1).astype(BF16)
+    own_laid = lay(data_in, rims)
+    x, bits_x, low_x = call(
+        functools.partial(lay_loadings, plan),
+        (field, window, low_field),
+        vmem(3),
+        [pltpu.VMEM((steps + 2 * LANES, LANES), F32)],
+    )(loadings, left, right)
+    odds, far_even, gram_near, far_data, own_laid, x, bits_x = lax.optimization_barrier(
+        (odds, far_even, gram_near, far_data, own_laid, x, bits_x)
+    )
+    gram = gram + gram_near
+    gram_near = swap(gram, "tm", bits[-1])
+    far_odds = swap(jnp.concatenate([odds, rims[None]], 0), "chan", 2)
+    far_odds, gram_near = lax.optimization_barrier((far_odds, gram_near))
+    gram = gram + gram_near
+    far_rims = far_odds[-1]
+
     def autos(evens, odd_ones, *before):
         return call(
-            functools.partial(auto_body, plan),
+            functools.partial(auto_body, plan, moved),
             (sds((width, plan.tiles * LANES), BF16), sds((REACH * factors, width), F32)),
-            smem() + vmem(2 + len(before)),
-            [pltpu.VMEM((LANES, 2 * GROUP * LAGS), BF16)],
-        )(start, evens, odd_ones, *before)
-
-    def numers(stk, laid, *before):
-        return call(
-            functools.partial(numer_body, plan), sds((rows, width), F32), vmem(2 + len(before))
-        )(stk, laid, *before)
+            vmem(2 + len(before)),
+            [pltpu.VMEM((LANES, factors * LAGS), BF16)],
+        )(evens, odd_ones, *before)
 
     stk, auto = autos(even, odds)
-    numer = numers(stk, lay(data, rims))
+    numer = call(functools.partial(numer_body, plan), field, vmem(2))(stk, own_laid)
     far_odds, numer = lax.optimization_barrier((far_odds, numer))
     far_stk, auto = autos(far_even, far_odds, auto)
     far_data, far_rims, auto = lax.optimization_barrier((far_data, far_rims, auto))
     auto_far = swap(auto, "chan", 1)
-    field, window = sds((rows, width), F32), sds((ext_rows, width), BF16)
-    low_field, rest = sds((rows, width), BF16), sds((REACH, width), F32)
-    tail_room = [pltpu.VMEM((2 * LAGS, LANES), F32)] * 2
-    x, bits_x, low_x, tail = call(
-        functools.partial(lay_loadings, plan, shards),
-        (field, window, low_field, rest),
-        smem() + vmem(5),
-        [pltpu.VMEM((steps + 2 * LANES, LANES), F32)] + tail_room,
-    )(place, loadings, left, right, stk, far_stk)
-    far_laid = lay(far_data, far_rims)
-    far_laid, auto_far, x = lax.optimization_barrier((far_laid, auto_far, x))
-    numer = numers(far_stk, far_laid, numer)
+    numer, tail = call(
+        functools.partial(numer_tail_body, plan, shards),
+        (field, rest),
+        vmem(5),
+        tail_room,
+    )(stk, far_stk, lay(far_data, far_rims), numer, bits_x)
+    numer, tail, auto_far = lax.optimization_barrier((numer, tail, auto_far))
     numer_far = swap(numer, "chan", 1)
     grams = [gram]
 
@@ -600,9 +607,9 @@
         return call(
             functools.partial(conv_tail_body, plan, shards, offsets),
             (field, rest),
-            smem() + vmem(5),
+            vmem(5),
             tail_room,
-        )(place, bits_now, high, low, stk, far_stk)
+        )(bits_now, high, low, stk, far_stk)
 
     scale = PENALTY / (steps * shards)
     numers_now = (numer, numer_far)
@@ -614,13 +621,13 @@
             grams = gram_rounds(gram, odd, (part,), (den, tails[1]))
         else:
             tails = (tail, swap(tail, "chan", 1))
-        operands = (place, x, bits_x, low_x, den, *numers_now, *tails, *grams)
+        operands = (x, bits_x, low_x, den, *numers_now, *tails, *grams)
         counts = (len(numers_now), len(grams))
         if sweep == ITERS - 1:
             return call(
                 functools.partial(last_body, plan, scale, shards, counts),
                 sds((factors, steps), F32),
-                smem() + vmem(len(operands) - 1),
+                vmem(len(operands)),
                 [pltpu.VMEM((rows, width), F32), pltpu.VMEM((steps + 2 * LANES, LANES), F32)],
             )(*operands)
         outs = (field, window, low_field, sds((factors, factors), F32))
@@ -629,7 +636,7 @@
         got = call(
             functools.partial(update_body, plan, scale, shards, counts),
             outs,
-            smem() + vmem(len(operands) - 1),
+            vmem(len(operands)),
             [pltpu.VMEM((rows, width), F32), pltpu.VMEM((rows, 2 * width), BF16)],
         )(*operands)
         if counts[0] > 1:

time: 72.1 us -> 66.7 us (0.925)
  Pallas kernels: 28.1 us -> 21.9 us
  starting transfers between devices: 27.4 us -> 29.1 us
    pallas_call x10, Pallas kernels: 16 us -> 11.6 us  [the longest x2 3.16 us: autos(): call(functools.partial(auto_body, plan, moved), (sds((width, plan.tiles *...]
    ppermute x21, starting transfers between devices: 26.7 us -> 28.4 us  [swap(): return lax.ppermute(x, axis, [(i, i ^ bit) for i in range(count)])]
    ppermute x21, waiting for transfers between devices: 14.2 us -> 12.5 us  [swap(): return lax.ppermute(x, axis, [(i, i ^ bit) for i in range(count)])]
    pallas_call x2, Pallas kernels: 3.97 us -> 2.69 us  [conv_tail(): call(functools.partial(conv_tail_body, plan, shards, offsets), (field, re...]
    ppermute x2, waiting for transfers between devices: 0.81 us -> 1.83 us  [mixed(): return lax.ppermute(x, ('tm', 'chan'), pairs)]
  transfers between devices with their start and end apart: 24 -> 24, of which waited for: 11 -> 13; matrix products, arithmetic and copies ran while one was open for 0% -> 0% of each run, Pallas kernels for 26% -> 24%
where the time goes in v2:
time: 66.7 us; the launch traced here: 66.5 us
  starting transfers between devices  29.1 us (44%)
  Pallas kernels  21.9 us (33%)
  waiting for transfers between devices  14.3 us (21%)
  local copies, waits for them, and re-layouts  0.89 us (1%)
    ppermute x21, starting transfers between devices, swap(): return lax.ppermute(x, axis, [(i, i ^ bit) for i in range(count)])  28.4 us
    ppermute x21, waiting for transfers between devices, swap(): return lax.ppermute(x, axis, [(i, i ^ bit) for i in range(count)])  12.5 us
    pallas_call x2, Pallas kernels, autos(): call(functools.partial(auto_body, plan, moved), (sds((width, plan.tiles *...  3.16 us
    pallas_call x1, Pallas kernels, on_device(): call(functools.partial(first_conv_body, plan, every), (mats, mats, sds((r...  2.99 us
    pallas_call x2, Pallas kernels, conv(): call(functools.partial(conv_body, plan, offsets), field, vmem(4))  2.94 us
    pallas_call x2, Pallas kernels, conv_tail(): call(functools.partial(conv_tail_body, plan, shards, offsets), (field, re...  2.69 us
    pallas_call x2, Pallas kernels, on_device(): call(functools.partial(update_body, plan, scale, shards, counts), outs, v...  2.44 us
    ppermute x2, waiting for transfers between devices, mixed(): return lax.ppermute(x, ('tm', 'chan'), pairs)  1.83 us
  transfers between devices with their start and end apart: 24, of which 13 were waited for; matrix products, arithmetic and copies ran while one was open for 0% of the time, Pallas kernels for 24%

profile of v2, /device:TPU:0, one launch (start us, length us, event | category | flops | bytes accessed | tf_op | source)
XLA Modules:
  0.0 66.5 jit_solution(3041696788737403595)
XLA Ops:
  0.0 3.0 %collective-permute-start = (bf16[1,96,256]{2,1,0:T(8,128)(2,1)}, bf16[1,96,256]{2,1,0:T(8,128)(2,1)S(1)}, u32[]{:S(2)}, u32[]{:S(2)}) collective-permute-start(bf16[1,96,256]{2,1,0:T(8,128)(2,1)} %bitcast.7), channel_id=1, source_target_pairs={{0,8},{4,12},{8,0},{12,4},{16,24},{20,28},{24,16},{28,20},{1,9},{5... | collective-permute-start | bytes 147464 | tf_op jit(solution)/shard_map/ppermute | solution.py:417
  3.9 1.5 %shard_map.37 = (bf16[96,2048]{1,0:T(8,128)(2,1)S(1)}, bf16[1,96,256]{2,1,0:T(8,128)(2,1)S(1)}, f32[64,64]{1,0:T(8,128)S(1)}, f32[160,128]{1,0:T(8,128)S(1)}, f32[160,128]{1,0:T(8,128)S(1)}) custom-call(f32[64,2048]{1,0:T(8,128)} %load_ref.1, bf16[96,2048]{1,0:T(8,128)(2,1)} %data_any.1, bf16[96,256]{1,0:T(8,128)(2,1)S(1)} %copy-done.1), custom_call_target="tpu_custom_call" | custom-call | tf_op jit(solution)/shard_map/pallas_call | solution.py:488
  5.5 1.9 %collective-permute-start.4 = (bf16[96,2048]{1,0:T(8,128)(2,1)S(1)}, bf16[96,2048]{1,0:T(8,128)(2,1)S(1)}, u32[]{:S(2)}, u32[]{:S(2)}) collective-permute-start(bf16[96,2048]{1,0:T(8,128)(2,1)S(1)} %get-tuple-element.68.data_ref), channel_id=1, source_target_pairs={{0,2},{1,3},{2,0},{3,1},{4,6},{5,7},{6,4},{7,5},{8,10},{9,11},{10,... | collective-permute-start | bytes 1179656 | tf_op jit(solution)/shard_map/ppermute | solution.py:417
  7.3 2.6 %collective-permute-start.1 = (bf16[2,96,256]{2,1,0:T(8,128)(2,1)S(1)}, bf16[2,96,256]{2,1,0:T(8,128)(2,1)S(1)}, u32[]{:S(2)}, u32[]{:S(2)}) collective-permute-start(bf16[2,96,256]{2,1,0:T(8,128)(2,1)S(1)} %get-tuple-element.125), channel_id=1, source_target_pairs={{0,16},{4,20},{8,24},{12,28},{16,0},{20,4},{24,8},{28,12},{1,17},{... | collective-permute-start | bytes 294920 | tf_op jit(solution)/shard_map/ppermute | solution.py:417
  10.6 4.3 %collective-permute-start.2 = (f32[64,64]{1,0:T(8,128)S(1)}, f32[64,64]{1,0:T(8,128)S(1)}, u32[]{:S(2)}, u32[]{:S(2)}) collective-permute-start(f32[64,64]{1,0:T(8,128)S(1)} %get-tuple-element.65), channel_id=1, source_target_pairs={{0,8},{4,12},{8,0},{12,4},{16,24},{20,28},{24,16},{28,20},{1,9},{5... | collective-permute-start | bytes 49160 | tf_op jit(solution)/shard_map/ppermute | solution.py:417
  14.9 2.7 %collective-permute-done.2 = f32[64,64]{1,0:T(8,128)S(1)} collective-permute-done((f32[64,64]{1,0:T(8,128)S(1)}, f32[64,64]{1,0:T(8,128)S(1)}, u32[]{:S(2)}, u32[]{:S(2)}) %collective-permute-start.2) | collective-permute-done | bytes 16416 | tf_op jit(solution)/shard_map/ppermute | solution.py:417
  17.6 1.4 %collective-permute-start.8 = (f32[160,128]{1,0:T(8,128)S(1)}, f32[160,128]{1,0:T(8,128)S(1)}, u32[]{:S(2)}, u32[]{:S(2)}) collective-permute-start(f32[160,128]{1,0:T(8,128)S(1)} %get-tuple-element.73), channel_id=1, source_target_pairs={{0,4},{4,0},{8,12},{12,8},{16,20},{20,16},{24,28},{28,24},{1,5},{5... | collective-permute-start | bytes 245768 | tf_op jit(solution)/shard_map/ppermute | solution.py:417
  20.2 2.2 %collective-permute-start.7 = (f32[64,64]{1,0:T(8,128)S(1)}, f32[64,64]{1,0:T(8,128)S(1)}, u32[]{:S(2)}, u32[]{:S(2)}) collective-permute-start(f32[64,64]{1,0:T(8,128)S(1)} %add.19), channel_id=1, source_target_pairs={{0,16},{4,20},{8,24},{12,28},{16,0},{20,4},{24,8},{28,12},{1,17},{... | collective-permute-start | bytes 49160 | tf_op jit(solution)/shard_map/ppermute | solution.py:417
  23.6 1.4 %collective-permute-done.7 = f32[64,64]{1,0:T(8,128)S(1)} collective-permute-done((f32[64,64]{1,0:T(8,128)S(1)}, f32[64,64]{1,0:T(8,128)S(1)}, u32[]{:S(2)}, u32[]{:S(2)}) %collective-permute-start.7) | collective-permute-done | bytes 16416 | tf_op jit(solution)/shard_map/ppermute | solution.py:417
  25.2 1.6 %collective-permute-start.9 = (bf16[5,96,256]{2,1,0:T(8,128)(2,1)S(1)}, bf16[5,96,256]{2,1,0:T(8,128)(2,1)S(1)}, u32[]{:S(2)}, u32[]{:S(2)}) collective-permute-start(bf16[5,96,256]{2,1,0:T(8,128)(2,1)S(1)} %maximum_maximum_fusion), channel_id=1, source_target_pairs={{0,2},{1,3},{2,0},{3,1},{4,6},{5,7},{6,4},{7,5},{8,10},{9,11},{10,... | collective-permute-start | bytes 737288 | tf_op jit(solution)/shard_map/ppermute | solution.py:417
  27.9 1.6 %shard_map.40 = (bf16[256,4608]{1,0:T(8,128)(2,1)S(1)}, f32[512,256]{1,0:T(8,128)S(1)}) custom-call(bf16[4,96,256]{2,1,0:T(8,128)(2,1)S(1)} %constant_dynamic-update-slice_fusion.2.even_ref, bf16[4,96,256]{2,1,0:T(8,128)(2,1)S(1)} %collective-permute-done.5.odd_ref), custom_call_target="tpu_custom_call" | custom-call | tf_op jit(solution)/shard_map/pallas_call | solution.py:569
  29.5 1.5 %shard_map.41.before = f32[544,256]{1,0:T(8,128)S(1)} custom-call(bf16[256,4608]{1,0:T(8,128)(2,1)S(1)} %get-tuple-element.85.stk_ref.stk_a, bf16[672,512]{1,0:T(8,128)(2,1)S(1)} %shard_map.38.data_ref), custom_call_target="tpu_custom_call" | custom-call | tf_op jit(solution)/shard_map/pallas_call | solution.py:577
  31.4 1.6 %shard_map.42 = (bf16[256,4608]{1,0:T(8,128)(2,1)S(1)}, f32[512,256]{1,0:T(8,128)S(1)}) custom-call(bf16[4,96,256]{2,1,0:T(8,128)(2,1)S(1)} %collective-permute-done.6.even_ref, bf16[5,96,256]{2,1,0:T(8,128)(2,1)S(1)} %collective-permute-done.9.odd_ref, f32[512,256]{1,0:T(8,128)S(1)} %get-tuple-element.88.refs_0_), custom_call_target="tpu_custom_call" | custom-call | tf_op jit(solution)/shard_map/pallas_call | solution.py:569
  33.5 1.5 %shard_map.44 = (f32[544,256]{1,0:T(8,128)S(1)}, f32[8,256]{1,0:T(8,128)S(1)}) custom-call(bf16[256,4608]{1,0:T(8,128)(2,1)S(1)} %get-tuple-element.85.stk_ref.stk_a, bf16[256,4608]{1,0:T(8,128)(2,1)S(1)} %get-tuple-element.91.stk_b, bf16[672,512]{1,0:T(8,128)(2,1)S(1)} %shard_map.43.data_ref, f32[544,256]{1,0:T(8,128)S(1)} %shard_map.41.before, ...), custom_call_target="tpu_custom_call" | custom-call | tf_op jit(solution)/shard_map/pallas_call | solution.py:582
  35.7 3.0 %shard_map.45 = (bf16[2304,256]{1,0:T(8,128)(2,1)S(1)}, bf16[2304,256]{1,0:T(8,128)(2,1)S(1)}, f32[544,256]{1,0:T(8,128)S(1)}) custom-call(f32[512,256]{1,0:T(8,128)S(1)} %get-tuple-element.90.auto_a, f32[512,256]{1,0:T(8,128)S(1)} %collective-permute-done.11.auto_b, bf16[800,256]{1,0:T(8,128)(2,1)S(1)} %get-tuple-element.78.bits_ref), custom_call_target="tpu_custom_call" | custom-call | tf_op jit(solution)/shard_map/pallas_call | solution.py:594
  42.6 1.4 %collective-permute-done.15 = f32[64,64]{1,0:T(8,128)S(1)} collective-permute-done((f32[64,64]{1,0:T(8,128)S(1)}, f32[64,64]{1,0:T(8,128)S(1)}, u32[]{:S(2)}, u32[]{:S(2)}) %collective-permute-start.15) | collective-permute-done | bytes 16416 | tf_op jit(solution)/shard_map/ppermute | solution.py:417
  44.0 3.3 %collective-permute-start.17 = (f32[64,64]{1,0:T(8,128)S(1)}, f32[64,64]{1,0:T(8,128)S(1)}, u32[]{:S(2)}, u32[]{:S(2)}) collective-permute-start(f32[64,64]{1,0:T(8,128)S(1)} %add.23.refs_3_), channel_id=1, source_target_pairs={{0,24},{4,28},{8,16},{12,20},{16,8},{20,12},{24,0},{28,4},{1,25},{... | collective-permute-start | bytes 49160 | tf_op jit(solution)/shard_map/ppermute | solution.py:417
  47.3 1.5 %shard_map.48.den_ref = f32[544,256]{1,0:T(8,128)S(1)} custom-call(bf16[800,256]{1,0:T(8,128)(2,1)S(1)} %get-tuple-element.103.bits_ref, bf16[2304,256]{1,0:T(8,128)(2,1)S(1)} %get-tuple-element.105.high_ref, bf16[2304,256]{1,0:T(8,128)(2,1)S(1)} %get-tuple-element.106.low_ref, f32[544,256]{1,0:T(8,128)S(1)} %get-tuple-element.107.refs_0_), custom_call_target="tpu_custom_call" | custom-call | tf_op jit(solution)/shard_map/pallas_call | solution.py:602
  49.7 1.5 %collective-permute-done.16.refs_4_ = f32[64,64]{1,0:T(8,128)S(1)} collective-permute-done((f32[64,64]{1,0:T(8,128)S(1)}, f32[64,64]{1,0:T(8,128)S(1)}, u32[]{:S(2)}, u32[]{:S(2)}) %collective-permute-start.16) | collective-permute-done | bytes 16416 | tf_op jit(solution)/shard_map/ppermute | solution.py:427
  53.6 2.0 %collective-permute-start.20 = (f32[64,64]{1,0:T(8,128)S(1)}, f32[64,64]{1,0:T(8,128)S(1)}, u32[]{:S(2)}, u32[]{:S(2)}) collective-permute-start(f32[64,64]{1,0:T(8,128)S(1)} %get-tuple-element.119), channel_id=1, source_target_pairs={{0,4},{4,0},{8,12},{12,8},{16,20},{20,16},{24,28},{28,24},{1,5},{5... | collective-permute-start | bytes 49160 | tf_op jit(solution)/shard_map/ppermute | solution.py:417
  57.6 1.8 %collective-permute-start.22 = (f32[64,64]{1,0:T(8,128)S(1)}, f32[64,64]{1,0:T(8,128)S(1)}, u32[]{:S(2)}, u32[]{:S(2)}) collective-permute-start(f32[64,64]{1,0:T(8,128)S(1)} %add.24.refs_3_), channel_id=1, source_target_pairs={{0,24},{4,28},{8,16},{12,20},{16,8},{20,12},{24,0},{28,4},{1,25},{... | collective-permute-start | bytes 49160 | tf_op jit(solution)/shard_map/ppermute | solution.py:417
  59.4 1.5 %shard_map.51.den_ref = f32[544,256]{1,0:T(8,128)S(1)} custom-call(bf16[800,256]{1,0:T(8,128)(2,1)S(1)} %get-tuple-element.115.bits_ref, bf16[2304,256]{1,0:T(8,128)(2,1)S(1)} %get-tuple-element.105.high_ref, bf16[2304,256]{1,0:T(8,128)(2,1)S(1)} %get-tuple-element.106.low_ref, f32[544,256]{1,0:T(8,128)S(1)} %get-tuple-element.117.refs_0_), custom_call_target="tpu_custom_call" | custom-call | tf_op jit(solution)/shard_map/pallas_call | solution.py:602
  60.9 2.4 %collective-permute-done.22.refs_6_ = f32[64,64]{1,0:T(8,128)S(1)} collective-permute-done((f32[64,64]{1,0:T(8,128)S(1)}, f32[64,64]{1,0:T(8,128)S(1)}, u32[]{:S(2)}, u32[]{:S(2)}) %collective-permute-start.22) | collective-permute-done | bytes 16416 | tf_op jit(solution)/shard_map/ppermute | solution.py:417
  64.9 1.7 %shard_map.52 = f32[64,2048]{1,0:T(8,128)} custom-call(f32[544,256]{1,0:T(8,128)S(1)} %get-tuple-element.114.x_ref, bf16[800,256]{1,0:T(8,128)(2,1)S(1)} %get-tuple-element.115.bits_ref, bf16[544,256]{1,0:T(8,128)(2,1)S(1)} %get-tuple-element.116.low_ref, f32[544,256]{1,0:T(8,128)S(1)} %shard_map.51.den_ref, f32[544,256]{1,0:T(8,128)S(1)} %get-tuple-element.108.refs_0_, ...), custom_call_target="tpu_custom_call" | custom-call | tf_op jit(solution)/shard_map/pallas_call | solution.py:627
  (60 shorter events, 17.4 us)
Async XLA Ops:
  0.0 5.4 %collective-permute-start = (bf16[1,96,256]{2,1,0:T(8,128)(2,1)}, bf16[1,96,256]{2,1,0:T(8,128)(2,1)S(1)}, u32[]{:S(2)}, u32[]{:S(2)}) collective-permute-start(bf16[1,96,256]{2,1,0:T(8,128)(2,1)} %bitcast.7), channel_id=1, source_target_pairs={{0,8},{4,12},{8,0},{12,4},{16,24},{20,28},{24,16},{28,20},{1,9},{5... | collective-permute-start | bytes 147464 | tf_op jit(solution)/shard_map/ppermute | solution.py:417
  5.5 12.1 %collective-permute-start.4 = (bf16[96,2048]{1,0:T(8,128)(2,1)S(1)}, bf16[96,2048]{1,0:T(8,128)(2,1)S(1)}, u32[]{:S(2)}, u32[]{:S(2)}) collective-permute-start(bf16[96,2048]{1,0:T(8,128)(2,1)S(1)} %get-tuple-element.68.data_ref), channel_id=1, source_target_pairs={{0,2},{1,3},{2,0},{3,1},{4,6},{5,7},{6,4},{7,5},{8,10},{9,11},{10,... | collective-permute-start | bytes 1179656 | tf_op jit(solution)/shard_map/ppermute | solution.py:417
  7.3 10.2 %collective-permute-start.1 = (bf16[2,96,256]{2,1,0:T(8,128)(2,1)S(1)}, bf16[2,96,256]{2,1,0:T(8,128)(2,1)S(1)}, u32[]{:S(2)}, u32[]{:S(2)}) collective-permute-start(bf16[2,96,256]{2,1,0:T(8,128)(2,1)S(1)} %get-tuple-element.125), channel_id=1, source_target_pairs={{0,16},{4,20},{8,24},{12,28},{16,0},{20,4},{24,8},{28,12},{1,17},{... | collective-permute-start | bytes 294920 | tf_op jit(solution)/shard_map/ppermute | solution.py:417
  9.9 7.6 %collective-permute-start.3 = (f32[160,128]{1,0:T(8,128)S(1)}, f32[160,128]{1,0:T(8,128)S(1)}, u32[]{:S(2)}, u32[]{:S(2)}) collective-permute-start(f32[160,128]{1,0:T(8,128)S(1)} %get-tuple-element.66), channel_id=1, source_target_pairs={{4,8},{12,16},{20,24},{8,4},{16,12},{24,20},{5,9},{13,17},{21,25},... | collective-permute-start | bytes 245768 | tf_op jit(solution)/shard_map/ppermute | solution.py:438
  10.6 6.9 %collective-permute-start.2 = (f32[64,64]{1,0:T(8,128)S(1)}, f32[64,64]{1,0:T(8,128)S(1)}, u32[]{:S(2)}, u32[]{:S(2)}) collective-permute-start(f32[64,64]{1,0:T(8,128)S(1)} %get-tuple-element.65), channel_id=1, source_target_pairs={{0,8},{4,12},{8,0},{12,4},{16,24},{20,28},{24,16},{28,20},{1,9},{5... | collective-permute-start | bytes 49160 | tf_op jit(solution)/shard_map/ppermute | solution.py:417
  17.6 5.0 %collective-permute-start.8 = (f32[160,128]{1,0:T(8,128)S(1)}, f32[160,128]{1,0:T(8,128)S(1)}, u32[]{:S(2)}, u32[]{:S(2)}) collective-permute-start(f32[160,128]{1,0:T(8,128)S(1)} %get-tuple-element.73), channel_id=1, source_target_pairs={{0,4},{4,0},{8,12},{12,8},{16,20},{20,16},{24,28},{28,24},{1,5},{5... | collective-permute-start | bytes 245768 | tf_op jit(solution)/shard_map/ppermute | solution.py:417
  19.0 6.0 %collective-permute-start.6 = (bf16[4,96,256]{2,1,0:T(8,128)(2,1)S(1)}, bf16[4,96,256]{2,1,0:T(8,128)(2,1)S(1)}, u32[]{:S(2)}, u32[]{:S(2)}) collective-permute-start(bf16[4,96,256]{2,1,0:T(8,128)(2,1)S(1)} %constant_dynamic-update-slice_fusion.2.even_ref), channel_id=1, source_target_pairs={{0,2},{1,3},{2,0},{3,1},{4,6},{5,7},{6,4},{7,5},{8,10},{9,11},{10,... | collective-permute-start | bytes 589832 | tf_op jit(solution)/shard_map/ppermute | solution.py:417
  19.5 5.7 %collective-permute-start.5 = (bf16[4,96,256]{2,1,0:T(8,128)(2,1)S(1)}, bf16[4,96,256]{2,1,0:T(8,128)(2,1)S(1)}, u32[]{:S(2)}, u32[]{:S(2)}) collective-permute-start(bf16[4,96,256]{2,1,0:T(8,128)(2,1)S(1)} %constant_dynamic-update-slice_fusion.2.even_ref), channel_id=1, source_target_pairs={{0,4},{4,0},{8,12},{12,8},{16,20},{20,16},{24,28},{28,24},{1,5},{5... | collective-permute-start | bytes 589832 | tf_op jit(solution)/shard_map/ppermute | solution.py:417
  20.2 4.8 %collective-permute-start.7 = (f32[64,64]{1,0:T(8,128)S(1)}, f32[64,64]{1,0:T(8,128)S(1)}, u32[]{:S(2)}, u32[]{:S(2)}) collective-permute-start(f32[64,64]{1,0:T(8,128)S(1)} %add.19), channel_id=1, source_target_pairs={{0,16},{4,20},{8,24},{12,28},{16,0},{20,4},{24,8},{28,12},{1,17},{... | collective-permute-start | bytes 49160 | tf_op jit(solution)/shard_map/ppermute | solution.py:417
  25.2 6.3 %collective-permute-start.9 = (bf16[5,96,256]{2,1,0:T(8,128)(2,1)S(1)}, bf16[5,96,256]{2,1,0:T(8,128)(2,1)S(1)}, u32[]{:S(2)}, u32[]{:S(2)}) collective-permute-start(bf16[5,96,256]{2,1,0:T(8,128)(2,1)S(1)} %maximum_maximum_fusion), channel_id=1, source_target_pairs={{0,2},{1,3},{2,0},{3,1},{4,6},{5,7},{6,4},{7,5},{8,10},{9,11},{10,... | collective-permute-start | bytes 737288 | tf_op jit(solution)/shard_map/ppermute | solution.py:417
  26.8 4.3 %collective-permute-start.10 = (f32[64,64]{1,0:T(8,128)S(1)}, f32[64,64]{1,0:T(8,128)S(1)}, u32[]{:S(2)}, u32[]{:S(2)}) collective-permute-start(f32[64,64]{1,0:T(8,128)S(1)} %add.21), channel_id=1, source_target_pairs={{0,4},{4,0},{8,12},{12,8},{16,20},{20,16},{24,28},{28,24},{1,5},{5... | collective-permute-start | bytes 49160 | tf_op jit(solution)/shard_map/ppermute | solution.py:417
  33.0 2.0 %collective-permute-start.11 = (f32[512,256]{1,0:T(8,128)S(1)}, f32[512,256]{1,0:T(8,128)S(1)}, u32[]{:S(2)}, u32[]{:S(2)}) collective-permute-start(f32[512,256]{1,0:T(8,128)S(1)} %get-tuple-element.90.auto_a), channel_id=1, source_target_pairs={{0,1},{1,0},{2,3},{3,2},{4,5},{5,4},{6,7},{7,6},{8,9},{9,8},{10,11... | collective-permute-start | bytes 1572872 | tf_op jit(solution)/shard_map/ppermute | solution.py:417
  35.1 3.7 %collective-permute-start.12 = (f32[544,256]{1,0:T(8,128)S(1)}, f32[544,256]{1,0:T(8,128)S(1)}, u32[]{:S(2)}, u32[]{:S(2)}) collective-permute-start(f32[544,256]{1,0:T(8,128)S(1)} %get-tuple-element.99.refs_0_), channel_id=1, source_target_pairs={{0,1},{1,0},{2,3},{3,2},{4,5},{5,4},{6,7},{7,6},{8,9},{9,8},{10,11... | collective-permute-start | bytes 1671176 | tf_op jit(solution)/shard_map/ppermute | solution.py:417
  35.6 3.1 %collective-permute-start.13 = (f32[8,256]{1,0:T(8,128)S(1)}, f32[8,256]{1,0:T(8,128)S(1)}, u32[]{:S(2)}, u32[]{:S(2)}) collective-permute-start(f32[8,256]{1,0:T(8,128)S(1)} %get-tuple-element.100.refs_2_), channel_id=1, source_target_pairs={{0,1},{1,0},{2,3},{3,2},{4,5},{5,4},{6,7},{7,6},{8,9},{9,8},{10,11... | collective-permute-start | bytes 24584 | tf_op jit(solution)/shard_map/ppermute | solution.py:417
  40.0 4.0 %collective-permute-start.15 = (f32[64,64]{1,0:T(8,128)S(1)}, f32[64,64]{1,0:T(8,128)S(1)}, u32[]{:S(2)}, u32[]{:S(2)}) collective-permute-start(f32[64,64]{1,0:T(8,128)S(1)} %get-tuple-element.110), channel_id=1, source_target_pairs={{0,4},{4,0},{8,12},{12,8},{16,20},{20,16},{24,28},{28,24},{1,5},{5... | collective-permute-start | bytes 49160 | tf_op jit(solution)/shard_map/ppermute | solution.py:417
  44.0 5.7 %collective-permute-start.17 = (f32[64,64]{1,0:T(8,128)S(1)}, f32[64,64]{1,0:T(8,128)S(1)}, u32[]{:S(2)}, u32[]{:S(2)}) collective-permute-start(f32[64,64]{1,0:T(8,128)S(1)} %add.23.refs_3_), channel_id=1, source_target_pairs={{0,24},{4,28},{8,16},{12,20},{16,8},{20,12},{24,0},{28,4},{1,25},{... | collective-permute-start | bytes 49160 | tf_op jit(solution)/shard_map/ppermute | solution.py:417
  47.3 3.9 %collective-permute-start.16 = (f32[64,64]{1,0:T(8,128)S(1)}, f32[64,64]{1,0:T(8,128)S(1)}, u32[]{:S(2)}, u32[]{:S(2)}) collective-permute-start(f32[64,64]{1,0:T(8,128)S(1)} %add.23.refs_3_), channel_id=1, source_target_pairs={{0,8},{1,17},{2,10},{3,19},{4,12},{5,21},{6,14},{7,23},{8,0},{9,25... | collective-permute-start | bytes 49160 | tf_op jit(solution)/shard_map/ppermute | solution.py:427
  47.3 1.5 %collective-permute-start.14 = (f32[8,256]{1,0:T(8,128)S(1)}, f32[8,256]{1,0:T(8,128)S(1)}, u32[]{:S(2)}, u32[]{:S(2)}) collective-permute-start(f32[8,256]{1,0:T(8,128)S(1)} %get-tuple-element.109.refs_1_), channel_id=1, source_target_pairs={{0,1},{1,0},{2,3},{3,2},{4,5},{5,4},{6,7},{7,6},{8,9},{9,8},{10,11... | collective-permute-start | bytes 24584 | tf_op jit(solution)/shard_map/ppermute | solution.py:417
  51.2 1.2 %collective-permute-start.18 = (f32[64,64]{1,0:T(8,128)S(1)}, f32[64,64]{1,0:T(8,128)S(1)}, u32[]{:S(2)}, u32[]{:S(2)}) collective-permute-start(f32[64,64]{1,0:T(8,128)S(1)} %collective-permute-done.16.refs_4_), channel_id=1, source_target_pairs={{0,1},{1,0},{2,3},{3,2},{4,5},{5,4},{6,7},{7,6},{8,9},{9,8},{10,11... | collective-permute-start | bytes 49160 | tf_op jit(solution)/shard_map/ppermute | solution.py:417
  53.6 4.0 %collective-permute-start.20 = (f32[64,64]{1,0:T(8,128)S(1)}, f32[64,64]{1,0:T(8,128)S(1)}, u32[]{:S(2)}, u32[]{:S(2)}) collective-permute-start(f32[64,64]{1,0:T(8,128)S(1)} %get-tuple-element.119), channel_id=1, source_target_pairs={{0,4},{4,0},{8,12},{12,8},{16,20},{20,16},{24,28},{28,24},{1,5},{5... | collective-permute-start | bytes 49160 | tf_op jit(solution)/shard_map/ppermute | solution.py:417
  57.6 5.7 %collective-permute-start.22 = (f32[64,64]{1,0:T(8,128)S(1)}, f32[64,64]{1,0:T(8,128)S(1)}, u32[]{:S(2)}, u32[]{:S(2)}) collective-permute-start(f32[64,64]{1,0:T(8,128)S(1)} %add.24.refs_3_), channel_id=1, source_target_pairs={{0,24},{4,28},{8,16},{12,20},{16,8},{20,12},{24,0},{28,4},{1,25},{... | collective-permute-start | bytes 49160 | tf_op jit(solution)/shard_map/ppermute | solution.py:417
  59.4 4.3 %collective-permute-start.21 = (f32[64,64]{1,0:T(8,128)S(1)}, f32[64,64]{1,0:T(8,128)S(1)}, u32[]{:S(2)}, u32[]{:S(2)}) collective-permute-start(f32[64,64]{1,0:T(8,128)S(1)} %add.24.refs_3_), channel_id=1, source_target_pairs={{0,8},{1,17},{2,10},{3,19},{4,12},{5,21},{6,14},{7,23},{8,0},{9,25... | collective-permute-start | bytes 49160 | tf_op jit(solution)/shard_map/ppermute | solution.py:427
  59.4 1.5 %collective-permute-start.19 = (f32[8,256]{1,0:T(8,128)S(1)}, f32[8,256]{1,0:T(8,128)S(1)}, u32[]{:S(2)}, u32[]{:S(2)}) collective-permute-start(f32[8,256]{1,0:T(8,128)S(1)} %get-tuple-element.118.refs_1_), channel_id=1, source_target_pairs={{0,1},{1,0},{2,3},{3,2},{4,5},{5,4},{6,7},{7,6},{8,9},{9,8},{10,11... | collective-permute-start | bytes 24584 | tf_op jit(solution)/shard_map/ppermute | solution.py:417
  63.6 1.2 %collective-permute-start.23 = (f32[64,64]{1,0:T(8,128)S(1)}, f32[64,64]{1,0:T(8,128)S(1)}, u32[]{:S(2)}, u32[]{:S(2)}) collective-permute-start(f32[64,64]{1,0:T(8,128)S(1)} %collective-permute-done.21.refs_4_), channel_id=1, source_target_pairs={{0,1},{1,0},{2,3},{3,2},{4,5},{5,4},{6,7},{7,6},{8,9},{9,8},{10,11... | collective-permute-start | bytes 49160 | tf_op jit(solution)/shard_map/ppermute | solution.py:417
  (2 other events, 23.4 us)

commit v3 on v2

--- a/solution.py
+++ b/solution.py
@@ -79,8 +79,9 @@
     return slice(m * CHUNKS, (m + 1) * CHUNKS)
 
 
-def turned(buf, left, middle, right, tiles):
-    parts = [left] + [middle[:, at] for at in lane_tiles(tiles)] + [right]
+def turned(buf, left, fields, right):
+    middle = [field[:, at] for field in fields for at in lane_tiles(field.shape[1] // LANES)]
+    parts = [left] + middle + [right]
     for i, part in enumerate(parts):
         part = part.astype(F32)
         spare = LANES - part.shape[0]
@@ -101,7 +102,11 @@
 
 def lay_loadings(plan, load_ref, left_ref, right_ref, x_ref, bits_ref, low_ref, buf):
     factors = plan.factors
-    turned(buf, left_ref[:factors, :], load_ref, right_ref[:factors, :], plan.steps // LANES)
+    left, right = (
+        ref[:factors, :].astype(F32) + ref[factors : 2 * factors, :].astype(F32)
+        for ref in (left_ref, right_ref)
+    )
+    turned(buf, left, (load_ref,), right)
     lane = lax.broadcasted_iota(jnp.int32, (CHUNKS, LANES), 1)
     skip = LANES - plan.halo
     for m in range(plan.ext):
@@ -119,8 +124,9 @@
             low_ref[row_tile(m - REACH), :] = (tile - bits.astype(F32)).astype(BF16)
 
 
-def lay_data(plan, data_ref, rims_ref, out_ref, buf):
-    turned(buf, rims_ref[:, :LANES], data_ref, rims_ref[:, LANES:], plan.steps // LANES)
+def lay_data(plan, *refs):
+    fields, (rims_ref, out_ref, buf) = refs[:-3], refs[-3:]
+    turned(buf, rims_ref[:, :LANES], fields, rims_ref[:, LANES:])
     skip = LANES - plan.front
     for m in range(plan.per + REACH):
         for p, at in enumerate(lane_tiles(PHASES)):
@@ -144,18 +150,20 @@
     odd = lax.axis_index("tm") % 2 == 1
     head, tail = slice(0, LANES), slice(plan.steps - LANES, plan.steps)
     for rim_ref, even_at, odd_at in ((near_ref, tail, head), (wide_ref, head, tail)):
-        rim_ref[:factors, :] = jnp.where(odd, load_ref[:, odd_at], load_ref[:, even_at])
-        rim_ref[factors:, :] = jnp.where(
+        high, low = split(jnp.where(odd, load_ref[:, odd_at], load_ref[:, even_at]))
+        rim_ref[:factors, :] = high
+        rim_ref[factors : 2 * factors, :] = low
+        rim_ref[2 * factors :, :] = jnp.where(
             odd, data_ref[:, odd_at].astype(F32), data_ref[:, even_at].astype(F32)
-        )
+        ).astype(BF16)
     high, low = split(load_ref[...])
     cross = dot(high, low, NT)
     gram_ref[...] = dot(high, high, NT) + cross + cross.T
 
 
-def lay_motifs(plan, me, even_ref, odd_ref, stk_ref, padded):
+def lay_motifs(plan, me, crossed, first_ref, second_ref, stk_ref, padded):
     factors = plan.factors
-    channels = even_ref.shape[1]
+    channels = first_ref.shape[1]
     span = GROUP * LAGS
     padded[channels:, :] = jnp.zeros((LANES - channels, padded.shape[1]), BF16)
     row = lax.broadcasted_iota(jnp.int32, (span, span), 0)
@@ -166,14 +174,18 @@
         if q:
             stk_ref[rows, : q * LANES] = jnp.zeros((factors, q * LANES), BF16)
         stk_ref[rows, (LAGS + q) * LANES :] = jnp.zeros((factors, (PHASES - q) * LANES), BF16)
-    swapped = me % 2
     for pair in range(factors // (2 * GROUP)):
-        at = (me // 2) ^ pair
-        one, two = even_ref[at].astype(F32), odd_ref[at].astype(F32)
-        room = slice(2 * pair * span, (2 * pair + 1) * span), slice((2 * pair + 1) * span, (2 * pair + 2) * span)
-        padded[:channels, room[0]] = jnp.where(swapped == 1, two, one).astype(BF16)
-        padded[:channels, room[1]] = jnp.where(swapped == 1, one, two).astype(BF16)
-        halves = [dot(pick, padded[:, at], NT) for at in room]
+        halves = []
+        for block in (2 * pair, 2 * pair + 1):
+            room = slice(block * span, (block + 1) * span)
+            step = block ^ me
+            index, late = step // 2, step % 2
+            if crossed is not None:
+                index = jnp.where(crossed, (step // 2) % 2 + 2 * (step % 2), index)
+                late = jnp.where(crossed, step // 4, late)
+            one, two = first_ref[index].astype(F32), second_ref[index].astype(F32)
+            padded[:channels, room] = jnp.where(late == 1, two, one).astype(BF16)
+            halves.append(dot(pick, padded[:, room], NT))
         for lag in range(LAGS):
             cut = slice(lag * GROUP, (lag + 1) * GROUP)
             tile = jnp.concatenate([halves[0][cut], halves[1][cut]], 0).astype(BF16)
@@ -182,11 +194,12 @@
                 stk_ref[first : first + 2 * GROUP, (lag + q) * LANES : (lag + q + 1) * LANES] = tile
 
 
-def auto_body(plan, moved, even_ref, odd_ref, *refs):
+def auto_body(plan, moved, first_ref, second_ref, *refs):
     before, (stk_ref, auto_ref, padded) = refs[:-3], refs[-3:]
     factors = plan.factors
     me = lax.axis_index("tm") if moved else 0
-    lay_motifs(plan, me, even_ref, odd_ref, stk_ref, padded)
+    crossed = None
+    lay_motifs(plan, me, crossed, first_ref, second_ref, stk_ref, padded)
     last = (PHASES - 1) * factors
     deep = PHASES * LANES
     auto_ref[...] = before[0][...] if before else jnp.zeros_like(auto_ref)
@@ -209,12 +222,12 @@
 
 
 def numer_tail_body(plan, shards, stk_a, stk_b, data_ref, before, bits_ref, *refs):
-    numer_ref, tail_ref, past, ahead = refs
-    tail_body(plan, shards, bits_ref, (stk_a, stk_b), tail_ref, past, ahead)
+    numer_ref, tail_ref, past, ahead, ahead2 = refs
+    tail_body(plan, shards, bits_ref, (stk_a, stk_b), tail_ref, past, ahead, ahead2)
     numer_body(plan, stk_b, data_ref, numer_ref, before)
 
 
-def tail_part(plan, stk_ref, past, ahead):
+def tail_start(plan, stk_ref, past, ahead):
     factors = plan.factors
     group = 2 * LANES // factors
     known = past[...]
@@ -224,7 +237,12 @@
         rows = jnp.concatenate([known[LAGS - l : 2 * LAGS - l, :factors] for l in lags], 1)
         mat = jnp.concatenate([stk_ref[:factors, l * LANES : (l + 1) * LANES] for l in lags], 0)
         total += dot(rows.astype(BF16), mat)
+    ahead[:LAGS, :] = jnp.zeros((LAGS, LANES), F32)
     ahead[LAGS:, :] = total
+
+
+def tail_part(plan, stk_ref, ahead):
+    factors = plan.factors
     beyond = ahead[...]
     high = beyond.astype(BF16).astype(F32)
     low = beyond - high
@@ -239,28 +257,28 @@
     return out[:LAGS] + out[LAGS:]
 
 
-def tail_body(plan, shards, bits_ref, stks, out_ref, past, ahead):
+def tail_body(plan, shards, bits_ref, stks, out_ref, past, *aheads):
     out_ref[...] = jnp.zeros_like(out_ref)
 
-    @pl.when(lax.axis_index("tm") == shards - 1)
-    def _():
-        factors = plan.factors
-        start = (plan.steps // PHASES + plan.edge) - (CHUNKS - 1) * plan.per
-        ends = [
-            bits_ref[row_tile(start + i), :].astype(F32)[CHUNKS - 1 :] for i in range(REACH)
-        ]
-        known = jnp.concatenate(ends, 0)
-        past[...] = jnp.zeros_like(past)
-        ahead[...] = jnp.zeros_like(ahead)
-        for p in range(PHASES):
-            part = known[:, p * factors : (p + 1) * factors]
-            part = jnp.concatenate([part, jnp.zeros((REACH, LANES - factors), F32)], 1)
-            past[pl.ds(p, REACH, stride=PHASES), :] = part
-        over = sum(tail_part(plan, stk_ref, past, ahead) for stk_ref in stks)
-        past[:LAGS, :] = jnp.concatenate([over, jnp.zeros((LAGS, LANES - factors), F32)], 1)
-        out_ref[...] = jnp.concatenate(
-            [past[pl.ds(p, REACH, stride=PHASES), :][:, :factors] for p in range(PHASES)], 1
-        )
+    factors = plan.factors
+    start = (plan.steps // PHASES + plan.edge) - (CHUNKS - 1) * plan.per
+    ends = [
+        bits_ref[row_tile(start + i), :].astype(F32)[CHUNKS - 1 :] for i in range(REACH)
+    ]
+    known = jnp.concatenate(ends, 0)
+    past[...] = jnp.zeros_like(past)
+    for p in range(PHASES):
+        part = known[:, p * factors : (p + 1) * factors]
+        part = jnp.concatenate([part, jnp.zeros((REACH, LANES - factors), F32)], 1)
+        past[pl.ds(p, REACH, stride=PHASES), :] = part
+    for stk_ref, ahead in zip(stks, aheads):
+        tail_start(plan, stk_ref, past, ahead)
+    over = sum(tail_part(plan, stk_ref, ahead) for stk_ref, ahead in zip(stks, aheads))
+    past[:LAGS, :] = jnp.concatenate([over, jnp.zeros((LAGS, LANES - factors), F32)], 1)
+    value = jnp.concatenate(
+        [past[pl.ds(p, REACH, stride=PHASES), :][:, :factors] for p in range(PHASES)], 1
+    )
+    out_ref[...] = jnp.where(lax.axis_index("tm") == shards - 1, value, 0.0)
 
 
 def taps_body(plan, auto_a, auto_b, high_ref, low_ref, line):
@@ -300,8 +318,8 @@
 
 
 def conv_tail_body(plan, shards, offsets, bits_ref, high_ref, low_ref, stk_a, stk_b, *refs):
-    out_ref, tail_ref, past, ahead = refs
-    tail_body(plan, shards, bits_ref, (stk_a, stk_b), tail_ref, past, ahead)
+    out_ref, tail_ref, past, ahead, ahead2 = refs
+    tail_body(plan, shards, bits_ref, (stk_a, stk_b), tail_ref, past, ahead, ahead2)
     conv_body(plan, offsets, bits_ref, high_ref, low_ref, out_ref)
 
 
@@ -432,10 +450,15 @@
     return lax.ppermute(x, axis, [(i, i + by) for i in range(count) if 0 <= i + by < count])
 
 
-def between(x, axis):
-    count = lax.axis_size(axis)
-    pairs = [(i, i + 1) for i in range(1, count - 1, 2)]
-    return lax.ppermute(x, axis, pairs + [(b, a) for a, b in pairs])
+def between(x):
+    count, wide = lax.axis_size("tm"), lax.axis_size("chan")
+    pairs = []
+    for t in range(count):
+        far = t + (1 if t % 2 else -1)
+        for c in range(wide):
+            target = (far, c) if 0 <= far < count else (t, c ^ (wide // 2))
+            pairs.append((t * wide + c, target[0] * wide + target[1]))
+    return lax.ppermute(x, ("tm", "chan"), pairs)
 
 
 def doubling(axis):
@@ -484,7 +507,7 @@
     me = lax.axis_index("tm")
     odd = lax.axis_index("chan") % 2 == 1
 
-    rim = sds((factors + channels, LANES), F32)
+    rim = sds((2 * factors + channels, LANES), BF16)
     data_in, even, gram, near_rim, wide_rim = call(
         functools.partial(first_body, plan),
         (
@@ -504,27 +527,36 @@
 
     moved = motifs.shape[1] == GROUP * LAGS
     bits = doubling("tm")
+    tracks = (bits, bits)
+
+    front = slice(0, steps // (2 * LANES) * LANES)
+
+    def gather_round(x, i):
+        return mixed(x, tracks[0][i], tracks[1][i])
+
     for i, bit in enumerate(bits[:-1]):
-        near = swap(even if i else motifs[None], "tm", bit)
+        near = gather_round(even if i else motifs[None], i)
         if i:
             gram_near = swap(gram, "tm", bits[i - 1])
             if i == 1:
-                wide_rim = between(wide_rim, "tm")
-                far_data = swap(after(data_in, even), "chan", 2)
-                near, gram_near, wide_rim, far_data = lax.optimization_barrier(
-                (near, gram_near, wide_rim, far_data)
-            )
+                wide_rim = between(wide_rim)
+                ready = after(data_in, even)
+                far_data = [swap(ready[:, at], "chan", 2) for at in (front, slice(front.stop, steps))]
+                near_rim = swap(after(near_rim, even), "tm", bits[-1])
+                near, gram_near, near_rim, far_front = lax.optimization_barrier(
+                    (near, gram_near, near_rim, far_data[0])
+                )
             else:
                 near, gram_near = lax.optimization_barrier((near, gram_near))
             gram = gram + gram_near
         even = jnp.concatenate([even, near], 0)
-    odds = swap(even, "tm", bits[-1])
+    odds = gather_round(even, len(bits) - 1)
     far_even = swap(even, "chan", 2)
-    gram_near = swap(gram, "tm", bits[-2])
-    near_rim = swap(after(near_rim, even), "tm", 1)
+    gram_near = swap(gram, "tm", bits[-1])
     right_side = me % 2 == 1
-    left = jnp.where(right_side, near_rim, wide_rim)
-    right = jnp.where(right_side, wide_rim, near_rim)
+    nothing = jnp.zeros_like(wide_rim)
+    left = jnp.where(me == 0, nothing, jnp.where(right_side, near_rim, wide_rim))
+    right = jnp.where(me == shards - 1, nothing, jnp.where(right_side, wide_rim, near_rim))
     if not moved:
         order = [0]
         for bit in bits:
@@ -537,17 +569,18 @@
         even, odds = slots[0::2], slots[1::2]
         far_even = swap(even, "chan", 2)
 
-    lay = call(
-        functools.partial(lay_data, plan),
-        sds(((plan.per + REACH) * CHUNKS, PHASES * LANES), BF16),
-        vmem(2),
-        [pltpu.VMEM((steps + 2 * LANES, LANES), F32)],
-    )
+    def lay(*fields):
+        return call(
+            functools.partial(lay_data, plan),
+            sds(((plan.per + REACH) * CHUNKS, PHASES * LANES), BF16),
+            vmem(len(fields)),
+            [pltpu.VMEM((steps + 2 * LANES, LANES), F32)],
+        )(*fields)
 
     field, window = sds((rows, width), F32), sds((ext_rows, width), BF16)
     low_field, rest = sds((rows, width), BF16), sds((REACH, width), F32)
-    tail_room = [pltpu.VMEM((2 * LAGS, LANES), F32)] * 2
-    rims = jnp.concatenate([left[factors:], right[factors:]], 1).astype(BF16)
+    tail_room = [pltpu.VMEM((2 * LAGS, LANES), F32)] * 3
+    rims = jnp.concatenate([left[2 * factors :], right[2 * factors :]], 1)
     own_laid = lay(data_in, rims)
     x, bits_x, low_x = call(
         functools.partial(lay_loadings, plan),
@@ -555,11 +588,11 @@
         vmem(3),
         [pltpu.VMEM((steps + 2 * LANES, LANES), F32)],
     )(loadings, left, right)
-    odds, far_even, gram_near, far_data, own_laid, x, bits_x = lax.optimization_barrier(
-        (odds, far_even, gram_near, far_data, own_laid, x, bits_x)
+    odds, far_even, gram_near, far_back, own_laid, x, bits_x = lax.optimization_barrier(
+        (odds, far_even, gram_near, far_data[1], own_laid, x, bits_x)
     )
     gram = gram + gram_near
-    gram_near = swap(gram, "tm", bits[-1])
+    gram_near = swap(gram, "tm", bits[-2])
     far_odds = swap(jnp.concatenate([odds, rims[None]], 0), "chan", 2)
     far_odds, gram_near = lax.optimization_barrier((far_odds, gram_near))
     gram = gram + gram_near
@@ -577,14 +610,16 @@
     numer = call(functools.partial(numer_body, plan), field, vmem(2))(stk, own_laid)
     far_odds, numer = lax.optimization_barrier((far_odds, numer))
     far_stk, auto = autos(far_even, far_odds, auto)
-    far_data, far_rims, auto = lax.optimization_barrier((far_data, far_rims, auto))
+    far_front, far_back, far_rims, auto = lax.optimization_barrier(
+        (far_front, far_back, far_rims, auto)
+    )
     auto_far = swap(auto, "chan", 1)
     numer, tail = call(
         functools.partial(numer_tail_body, plan, shards),
         (field, rest),
         vmem(5),
         tail_room,
-    )(stk, far_stk, lay(far_data, far_rims), numer, bits_x)
+    )(stk, far_stk, lay(far_front, far_back, far_rims), numer, bits_x)
     numer, tail, auto_far = lax.optimization_barrier((numer, tail, auto_far))
     numer_far = swap(numer, "chan", 1)
     grams = [gram]
@@ -615,9 +650,9 @@
     numers_now = (numer, numer_far)
     for sweep in range(ITERS):
         if sweep:
-            part, tail = conv_tail(every[:REACH], bits_x)
+            part, tail = conv_tail(every[:REACH + 3], bits_x)
             tails = (tail, swap(tail, "chan", 1))
-            den = conv(every[REACH:], bits_x, part)
+            den = conv(every[REACH + 3:], bits_x, part)
             grams = gram_rounds(gram, odd, (part,), (den, tails[1]))
         else:
             tails = (tail, swap(tail, "chan", 1))

time: 66.7 us -> 65.7 us (0.985)
  starting transfers between devices: 29.1 us -> 21.9 us
  waiting for transfers between devices: 14.3 us -> 18.6 us
  Pallas kernels: 21.9 us -> 23.7 us
    ppermute x21 -> x19, starting transfers between devices: 28.4 us -> 15 us  [swap(): return lax.ppermute(x, axis, [(i, i ^ bit) for i in range(count)])]
    ppermute x2 -> x5, starting transfers between devices: 0.01 us -> 6.43 us  [mixed(): return lax.ppermute(x, ('tm', 'chan'), pairs)]
    ppermute x21 -> x19, waiting for transfers between devices: 12.5 us -> 18.3 us  [swap(): return lax.ppermute(x, axis, [(i, i ^ bit) for i in range(count)])]
    pallas_call x2, Pallas kernels: 2.69 us -> 4.76 us  [conv_tail(): call(functools.partial(conv_tail_body, plan, shards, offsets), (field, re...]
    ppermute x2 -> x5, waiting for transfers between devices: 1.83 us -> 0.35 us  [mixed(): return lax.ppermute(x, ('tm', 'chan'), pairs)]
    pallas_call x2, Pallas kernels: 2.94 us -> 2.07 us  [conv(): call(functools.partial(conv_body, plan, offsets), field, vmem(4))]
  transfers between devices with their start and end apart: 24 -> 25, of which waited for: 13 -> 14; matrix products, arithmetic and copies ran while one was open for 0% -> 0% of each run, Pallas kernels for 24% -> 27%
where the time goes in v3:
time: 65.7 us; the launch traced here: 65.5 us
  Pallas kernels  23.7 us (36%)
  starting transfers between devices  21.9 us (33%)
  waiting for transfers between devices  18.6 us (28%)
  local copies, waits for them, and re-layouts  0.9 us (1%)
    ppermute x19, waiting for transfers between devices, swap(): return lax.ppermute(x, axis, [(i, i ^ bit) for i in range(count)])  18.3 us
    ppermute x19, starting transfers between devices, swap(): return lax.ppermute(x, axis, [(i, i ^ bit) for i in range(count)])  15 us
    ppermute x5, starting transfers between devices, mixed(): return lax.ppermute(x, ('tm', 'chan'), pairs)  6.43 us
    pallas_call x2, Pallas kernels, conv_tail(): call(functools.partial(conv_tail_body, plan, shards, offsets), (field, re...  4.76 us
    pallas_call x2, Pallas kernels, autos(): call(functools.partial(auto_body, plan, moved), (sds((width, plan.tiles *...  3.17 us
    pallas_call x1, Pallas kernels, on_device(): call(functools.partial(first_conv_body, plan, every), (mats, mats, sds((r...  2.99 us
    pallas_call x2, Pallas kernels, on_device(): call(functools.partial(update_body, plan, scale, shards, counts), outs, v...  2.44 us
    pallas_call x1, Pallas kernels, on_device(): call(functools.partial(numer_tail_body, plan, shards), (field, rest), vme...  2.12 us
  transfers between devices with their start and end apart: 25, of which 14 were waited for; matrix products, arithmetic and copies ran while one was open for 0% of the time, Pallas kernels for 27%

profile of v3, /device:TPU:0, one launch (start us, length us, event | category | flops | bytes accessed | tf_op | source)
XLA Modules:
  0.0 65.5 jit_solution(8607102089865813311)
XLA Ops:
  0.0 3.0 %collective-permute-start = (bf16[1,96,256]{2,1,0:T(8,128)(2,1)}, bf16[1,96,256]{2,1,0:T(8,128)(2,1)S(1)}, u32[]{:S(2)}, u32[]{:S(2)}) collective-permute-start(bf16[1,96,256]{2,1,0:T(8,128)(2,1)} %bitcast.5), channel_id=1, source_target_pairs={{0,8},{1,9},{2,10},{3,11},{4,12},{5,13},{6,14},{7,15},{8,0},{9,1},... | collective-permute-start | bytes 147464 | tf_op jit(solution)/shard_map/ppermute | solution.py:445
  3.9 1.6 %shard_map.37 = (bf16[96,2048]{1,0:T(8,128)(2,1)S(1)}, bf16[1,96,256]{2,1,0:T(8,128)(2,1)S(1)}, f32[64,64]{1,0:T(8,128)S(1)}, bf16[224,128]{1,0:T(8,128)(2,1)S(1)}, bf16[224,128]{1,0:T(8,128)(2,1)S(1)}) custom-call(f32[64,2048]{1,0:T(8,128)} %load_ref.1, bf16[96,2048]{1,0:T(8,128)(2,1)} %data_any.1, bf16[96,256]{1,0:T(8,128)(2,1)S(1)} %copy-done.1), custom_call_target="tpu_custom_call" | custom-call | tf_op jit(solution)/shard_map/pallas_call | solution.py:511
  5.5 1.9 %collective-permute-start.4 = (bf16[96,1024]{1,0:T(8,128)(2,1)S(1)}, bf16[96,1024]{1,0:T(8,128)(2,1)S(1)}, u32[]{:S(2)}, u32[]{:S(2)}) collective-permute-start(bf16[96,1024]{1,0:T(8,128)(2,1)S(1)} %get-tuple-element.126), channel_id=1, source_target_pairs={{0,2},{1,3},{2,0},{3,1},{4,6},{5,7},{6,4},{7,5},{8,10},{9,11},{10,... | collective-permute-start | bytes 589832 | tf_op jit(solution)/shard_map/ppermute | solution.py:435
  7.4 2.6 %collective-permute-start.1 = (bf16[2,96,256]{2,1,0:T(8,128)(2,1)S(1)}, bf16[2,96,256]{2,1,0:T(8,128)(2,1)S(1)}, u32[]{:S(2)}, u32[]{:S(2)}) collective-permute-start(bf16[2,96,256]{2,1,0:T(8,128)(2,1)S(1)} %get-tuple-element.131), channel_id=1, source_target_pairs={{0,16},{1,17},{2,18},{3,19},{4,20},{5,21},{6,22},{7,23},{8,24},{9,... | collective-permute-start | bytes 294920 | tf_op jit(solution)/shard_map/ppermute | solution.py:445
  10.0 1.5 %collective-permute-start.3 = (bf16[224,128]{1,0:T(8,128)(2,1)S(1)}, bf16[224,128]{1,0:T(8,128)(2,1)S(1)}, u32[]{:S(2)}, u32[]{:S(2)}) collective-permute-start(bf16[224,128]{1,0:T(8,128)(2,1)S(1)} %get-tuple-element.68), channel_id=1, source_target_pairs={{0,4},{4,0},{8,12},{12,8},{16,20},{20,16},{24,28},{28,24},{1,5},{5... | collective-permute-start | bytes 172040 | tf_op jit(solution)/shard_map/ppermute | solution.py:435
  11.5 1.6 %collective-permute-start.2 = (f32[64,64]{1,0:T(8,128)S(1)}, f32[64,64]{1,0:T(8,128)S(1)}, u32[]{:S(2)}, u32[]{:S(2)}) collective-permute-start(f32[64,64]{1,0:T(8,128)S(1)} %get-tuple-element.66), channel_id=1, source_target_pairs={{0,8},{4,12},{8,0},{12,4},{16,24},{20,28},{24,16},{28,20},{1,9},{5... | collective-permute-start | bytes 49160 | tf_op jit(solution)/shard_map/ppermute | solution.py:435
  13.5 1.8 %collective-permute-done.2 = f32[64,64]{1,0:T(8,128)S(1)} collective-permute-done((f32[64,64]{1,0:T(8,128)S(1)}, f32[64,64]{1,0:T(8,128)S(1)}, u32[]{:S(2)}, u32[]{:S(2)}) %collective-permute-start.2) | collective-permute-done | bytes 16416 | tf_op jit(solution)/shard_map/ppermute | solution.py:435
  15.9 1.6 %collective-permute-start.6 = (bf16[4,96,256]{2,1,0:T(8,128)(2,1)S(1)}, bf16[4,96,256]{2,1,0:T(8,128)(2,1)S(1)}, u32[]{:S(2)}, u32[]{:S(2)}) collective-permute-start(bf16[4,96,256]{2,1,0:T(8,128)(2,1)S(1)} %constant_dynamic-update-slice_fusion.2.first_ref), channel_id=1, source_target_pairs={{0,2},{1,3},{2,0},{3,1},{4,6},{5,7},{6,4},{7,5},{8,10},{9,11},{10,... | collective-permute-start | bytes 589832 | tf_op jit(solution)/shard_map/ppermute | solution.py:435
  18.0 1.5 %collective-permute-start.7 = (f32[64,64]{1,0:T(8,128)S(1)}, f32[64,64]{1,0:T(8,128)S(1)}, u32[]{:S(2)}, u32[]{:S(2)}) collective-permute-start(f32[64,64]{1,0:T(8,128)S(1)} %add.19), channel_id=1, source_target_pairs={{0,4},{4,0},{8,12},{12,8},{16,20},{20,16},{24,28},{28,24},{1,5},{5... | collective-permute-start | bytes 49160 | tf_op jit(solution)/shard_map/ppermute | solution.py:435
  20.6 2.3 %collective-permute-done.8.refs_1_ = bf16[96,1024]{1,0:T(8,128)(2,1)S(1)} collective-permute-done((bf16[96,1024]{1,0:T(8,128)(2,1)S(1)}, bf16[96,1024]{1,0:T(8,128)(2,1)S(1)}, u32[]{:S(2)}, u32[]{:S(2)}) %collective-permute-start.8) | collective-permute-done | bytes 196640 | tf_op jit(solution)/shard_map/ppermute | solution.py:435
  23.5 1.5 %collective-permute-done.6.first_ref = bf16[4,96,256]{2,1,0:T(8,128)(2,1)S(1)} collective-permute-done((bf16[4,96,256]{2,1,0:T(8,128)(2,1)S(1)}, bf16[4,96,256]{2,1,0:T(8,128)(2,1)S(1)}, u32[]{:S(2)}, u32[]{:S(2)}) %collective-permute-start.6) | collective-permute-done | bytes 196640 | tf_op jit(solution)/shard_map/ppermute | solution.py:435
  25.6 1.6 %shard_map.40 = (bf16[256,4608]{1,0:T(8,128)(2,1)S(1)}, f32[512,256]{1,0:T(8,128)S(1)}) custom-call(bf16[4,96,256]{2,1,0:T(8,128)(2,1)S(1)} %constant_dynamic-update-slice_fusion.2.first_ref, bf16[4,96,256]{2,1,0:T(8,128)(2,1)S(1)} %collective-permute-done.5.second_ref), custom_call_target="tpu_custom_call" | custom-call | tf_op jit(solution)/shard_map/pallas_call | solution.py:602
  27.2 1.5 %shard_map.41.before = f32[544,256]{1,0:T(8,128)S(1)} custom-call(bf16[256,4608]{1,0:T(8,128)(2,1)S(1)} %get-tuple-element.86.stk_ref.stk_a, bf16[672,512]{1,0:T(8,128)(2,1)S(1)} %shard_map.38.data_ref), custom_call_target="tpu_custom_call" | custom-call | tf_op jit(solution)/shard_map/pallas_call | solution.py:610
  28.7 1.7 %collective-permute-done.11 = f32[64,64]{1,0:T(8,128)S(1)} collective-permute-done((f32[64,64]{1,0:T(8,128)S(1)}, f32[64,64]{1,0:T(8,128)S(1)}, u32[]{:S(2)}, u32[]{:S(2)}) %collective-permute-start.11) | collective-permute-done | bytes 16416 | tf_op jit(solution)/shard_map/ppermute | solution.py:435
  31.3 1.6 %shard_map.42 = (bf16[256,4608]{1,0:T(8,128)(2,1)S(1)}, f32[512,256]{1,0:T(8,128)S(1)}) custom-call(bf16[4,96,256]{2,1,0:T(8,128)(2,1)S(1)} %collective-permute-done.6.first_ref, bf16[5,96,256]{2,1,0:T(8,128)(2,1)S(1)} %collective-permute-done.10.second_ref, f32[512,256]{1,0:T(8,128)S(1)} %get-tuple-element.89.refs_0_), custom_call_target="tpu_custom_call" | custom-call | tf_op jit(solution)/shard_map/pallas_call | solution.py:602
  33.4 2.1 %shard_map.44 = (f32[544,256]{1,0:T(8,128)S(1)}, f32[8,256]{1,0:T(8,128)S(1)}) custom-call(bf16[256,4608]{1,0:T(8,128)(2,1)S(1)} %get-tuple-element.86.stk_ref.stk_a, bf16[256,4608]{1,0:T(8,128)(2,1)S(1)} %get-tuple-element.92.stk_b, bf16[672,512]{1,0:T(8,128)(2,1)S(1)} %shard_map.43.data_ref, f32[544,256]{1,0:T(8,128)S(1)} %shard_map.41.before, ...), custom_call_target="tpu_custom_call" | custom-call | tf_op jit(solution)/shard_map/pallas_call | solution.py:617
  36.2 3.0 %shard_map.45 = (bf16[2304,256]{1,0:T(8,128)(2,1)S(1)}, bf16[2304,256]{1,0:T(8,128)(2,1)S(1)}, f32[544,256]{1,0:T(8,128)S(1)}) custom-call(f32[512,256]{1,0:T(8,128)S(1)} %get-tuple-element.91.auto_a, f32[512,256]{1,0:T(8,128)S(1)} %collective-permute-done.12.auto_b, bf16[800,256]{1,0:T(8,128)(2,1)S(1)} %get-tuple-element.78.bits_ref), custom_call_target="tpu_custom_call" | custom-call | tf_op jit(solution)/shard_map/pallas_call | solution.py:629
  39.2 1.2 %shard_map.46 = (f32[544,256]{1,0:T(8,128)S(1)}, f32[544,256]{1,0:T(8,128)S(1)}, bf16[800,256]{1,0:T(8,128)(2,1)S(1)}, bf16[544,256]{1,0:T(8,128)(2,1)S(1)}, f32[64,64]{1,0:T(8,128)S(1)}) custom-call(f32[544,256]{1,0:T(8,128)S(1)} %get-tuple-element.77.x_ref, bf16[800,256]{1,0:T(8,128)(2,1)S(1)} %get-tuple-element.78.bits_ref, ...), custom_call_target="tpu_custom_call" | custom-call | tf_op jit(solution)/shard_map/pallas_call | solution.py:671
  41.4 2.4 %shard_map.47 = (f32[544,256]{1,0:T(8,128)S(1)}, f32[8,256]{1,0:T(8,128)S(1)}) custom-call(bf16[800,256]{1,0:T(8,128)(2,1)S(1)} %get-tuple-element.105.bits_ref, bf16[2304,256]{1,0:T(8,128)(2,1)S(1)} %get-tuple-element.107.high_ref, bf16[2304,256]{1,0:T(8,128)(2,1)S(1)} %get-tuple-element.108.low_ref, bf16[256,4608]{1,0:T(8,128)(2,1)S(1)} %get-tuple-element.86.stk_ref.stk_a, ...), custom_call_target="tpu_custom_call" | custom-call | tf_op jit(solution)/shard_map/pallas_call | solution.py:642
  46.9 3.2 %collective-permute-done.18.refs_6_ = f32[64,64]{1,0:T(8,128)S(1)} collective-permute-done((f32[64,64]{1,0:T(8,128)S(1)}, f32[64,64]{1,0:T(8,128)S(1)}, u32[]{:S(2)}, u32[]{:S(2)}) %collective-permute-start.18) | collective-permute-done | bytes 16416 | tf_op jit(solution)/shard_map/ppermute | solution.py:435
  53.5 2.4 %shard_map.50 = (f32[544,256]{1,0:T(8,128)S(1)}, f32[8,256]{1,0:T(8,128)S(1)}) custom-call(bf16[800,256]{1,0:T(8,128)(2,1)S(1)} %get-tuple-element.117.bits_ref, bf16[2304,256]{1,0:T(8,128)(2,1)S(1)} %get-tuple-element.107.high_ref, bf16[2304,256]{1,0:T(8,128)(2,1)S(1)} %get-tuple-element.108.low_ref, bf16[256,4608]{1,0:T(8,128)(2,1)S(1)} %get-tuple-element.86.stk_ref.stk_a, ...), custom_call_target="tpu_custom_call" | custom-call | tf_op jit(solution)/shard_map/pallas_call | solution.py:642
  56.5 2.0 %collective-permute-start.23 = (f32[64,64]{1,0:T(8,128)S(1)}, f32[64,64]{1,0:T(8,128)S(1)}, u32[]{:S(2)}, u32[]{:S(2)}) collective-permute-start(f32[64,64]{1,0:T(8,128)S(1)} %add.24.refs_3_), channel_id=1, source_target_pairs={{0,24},{4,28},{8,16},{12,20},{16,8},{20,12},{24,0},{28,4},{1,25},{... | collective-permute-start | bytes 49160 | tf_op jit(solution)/shard_map/ppermute | solution.py:435
  59.7 2.5 %collective-permute-done.23.refs_6_ = f32[64,64]{1,0:T(8,128)S(1)} collective-permute-done((f32[64,64]{1,0:T(8,128)S(1)}, f32[64,64]{1,0:T(8,128)S(1)}, u32[]{:S(2)}, u32[]{:S(2)}) %collective-permute-start.23) | collective-permute-done | bytes 16416 | tf_op jit(solution)/shard_map/ppermute | solution.py:435
  63.8 1.7 %shard_map.52 = f32[64,2048]{1,0:T(8,128)} custom-call(f32[544,256]{1,0:T(8,128)S(1)} %get-tuple-element.116.x_ref, bf16[800,256]{1,0:T(8,128)(2,1)S(1)} %get-tuple-element.117.bits_ref, bf16[544,256]{1,0:T(8,128)(2,1)S(1)} %get-tuple-element.118.low_ref, f32[544,256]{1,0:T(8,128)S(1)} %shard_map.51.den_ref, f32[544,256]{1,0:T(8,128)S(1)} %get-tuple-element.110.refs_0_, ...), custom_call_target="tpu_custom_call" | custom-call | tf_op jit(solution)/shard_map/pallas_call | solution.py:662
  (61 shorter events, 17.5 us)
Async XLA Ops:
  0.0 5.4 %collective-permute-start = (bf16[1,96,256]{2,1,0:T(8,128)(2,1)}, bf16[1,96,256]{2,1,0:T(8,128)(2,1)S(1)}, u32[]{:S(2)}, u32[]{:S(2)}) collective-permute-start(bf16[1,96,256]{2,1,0:T(8,128)(2,1)} %bitcast.5), channel_id=1, source_target_pairs={{0,8},{1,9},{2,10},{3,11},{4,12},{5,13},{6,14},{7,15},{8,0},{9,1},... | collective-permute-start | bytes 147464 | tf_op jit(solution)/shard_map/ppermute | solution.py:445
  5.5 10.4 %collective-permute-start.4 = (bf16[96,1024]{1,0:T(8,128)(2,1)S(1)}, bf16[96,1024]{1,0:T(8,128)(2,1)S(1)}, u32[]{:S(2)}, u32[]{:S(2)}) collective-permute-start(bf16[96,1024]{1,0:T(8,128)(2,1)S(1)} %get-tuple-element.126), channel_id=1, source_target_pairs={{0,2},{1,3},{2,0},{3,1},{4,6},{5,7},{6,4},{7,5},{8,10},{9,11},{10,... | collective-permute-start | bytes 589832 | tf_op jit(solution)/shard_map/ppermute | solution.py:435
  7.4 8.5 %collective-permute-start.1 = (bf16[2,96,256]{2,1,0:T(8,128)(2,1)S(1)}, bf16[2,96,256]{2,1,0:T(8,128)(2,1)S(1)}, u32[]{:S(2)}, u32[]{:S(2)}) collective-permute-start(bf16[2,96,256]{2,1,0:T(8,128)(2,1)S(1)} %get-tuple-element.131), channel_id=1, source_target_pairs={{0,16},{1,17},{2,18},{3,19},{4,20},{5,21},{6,22},{7,23},{8,24},{9,... | collective-permute-start | bytes 294920 | tf_op jit(solution)/shard_map/ppermute | solution.py:445
  10.0 5.9 %collective-permute-start.3 = (bf16[224,128]{1,0:T(8,128)(2,1)S(1)}, bf16[224,128]{1,0:T(8,128)(2,1)S(1)}, u32[]{:S(2)}, u32[]{:S(2)}) collective-permute-start(bf16[224,128]{1,0:T(8,128)(2,1)S(1)} %get-tuple-element.68), channel_id=1, source_target_pairs={{0,4},{4,0},{8,12},{12,8},{16,20},{20,16},{24,28},{28,24},{1,5},{5... | collective-permute-start | bytes 172040 | tf_op jit(solution)/shard_map/ppermute | solution.py:435
  11.5 3.9 %collective-permute-start.2 = (f32[64,64]{1,0:T(8,128)S(1)}, f32[64,64]{1,0:T(8,128)S(1)}, u32[]{:S(2)}, u32[]{:S(2)}) collective-permute-start(f32[64,64]{1,0:T(8,128)S(1)} %get-tuple-element.66), channel_id=1, source_target_pairs={{0,8},{4,12},{8,0},{12,4},{16,24},{20,28},{24,16},{28,20},{1,9},{5... | collective-permute-start | bytes 49160 | tf_op jit(solution)/shard_map/ppermute | solution.py:435
  13.0 6.5 %collective-permute-start.9 = (bf16[224,128]{1,0:T(8,128)(2,1)S(1)}, bf16[224,128]{1,0:T(8,128)(2,1)S(1)}, u32[]{:S(2)}, u32[]{:S(2)}) collective-permute-start(bf16[224,128]{1,0:T(8,128)(2,1)S(1)} %get-tuple-element.74), channel_id=1, source_target_pairs={{0,2},{1,3},{2,0},{3,1},{4,8},{5,9},{6,10},{7,11},{8,4},{9,5},{10,... | collective-permute-start | bytes 172040 | tf_op jit(solution)/shard_map/ppermute | solution.py:461
  15.4 7.5 %collective-permute-start.8 = (bf16[96,1024]{1,0:T(8,128)(2,1)S(1)}, bf16[96,1024]{1,0:T(8,128)(2,1)S(1)}, u32[]{:S(2)}, u32[]{:S(2)}) collective-permute-start(bf16[96,1024]{1,0:T(8,128)(2,1)S(1)} %get-tuple-element.125), channel_id=1, source_target_pairs={{0,2},{1,3},{2,0},{3,1},{4,6},{5,7},{6,4},{7,5},{8,10},{9,11},{10,... | collective-permute-start | bytes 589832 | tf_op jit(solution)/shard_map/ppermute | solution.py:435
  15.9 9.1 %collective-permute-start.6 = (bf16[4,96,256]{2,1,0:T(8,128)(2,1)S(1)}, bf16[4,96,256]{2,1,0:T(8,128)(2,1)S(1)}, u32[]{:S(2)}, u32[]{:S(2)}) collective-permute-start(bf16[4,96,256]{2,1,0:T(8,128)(2,1)S(1)} %constant_dynamic-update-slice_fusion.2.first_ref), channel_id=1, source_target_pairs={{0,2},{1,3},{2,0},{3,1},{4,6},{5,7},{6,4},{7,5},{8,10},{9,11},{10,... | collective-permute-start | bytes 589832 | tf_op jit(solution)/shard_map/ppermute | solution.py:435
  17.5 7.5 %collective-permute-start.5 = (bf16[4,96,256]{2,1,0:T(8,128)(2,1)S(1)}, bf16[4,96,256]{2,1,0:T(8,128)(2,1)S(1)}, u32[]{:S(2)}, u32[]{:S(2)}) collective-permute-start(bf16[4,96,256]{2,1,0:T(8,128)(2,1)S(1)} %constant_dynamic-update-slice_fusion.2.first_ref), channel_id=1, source_target_pairs={{0,4},{1,5},{2,6},{3,7},{4,0},{5,1},{6,2},{7,3},{8,12},{9,13},{10,... | collective-permute-start | bytes 589832 | tf_op jit(solution)/shard_map/ppermute | solution.py:445
  18.0 5.5 %collective-permute-start.7 = (f32[64,64]{1,0:T(8,128)S(1)}, f32[64,64]{1,0:T(8,128)S(1)}, u32[]{:S(2)}, u32[]{:S(2)}) collective-permute-start(f32[64,64]{1,0:T(8,128)S(1)} %add.19), channel_id=1, source_target_pairs={{0,4},{4,0},{8,12},{12,8},{16,20},{20,16},{24,28},{28,24},{1,5},{5... | collective-permute-start | bytes 49160 | tf_op jit(solution)/shard_map/ppermute | solution.py:435
  25.0 6.3 %collective-permute-start.10 = (bf16[5,96,256]{2,1,0:T(8,128)(2,1)S(1)}, bf16[5,96,256]{2,1,0:T(8,128)(2,1)S(1)}, u32[]{:S(2)}, u32[]{:S(2)}) collective-permute-start(bf16[5,96,256]{2,1,0:T(8,128)(2,1)S(1)} %pad_maximum_fusion), channel_id=1, source_target_pairs={{0,2},{1,3},{2,0},{3,1},{4,6},{5,7},{6,4},{7,5},{8,10},{9,11},{10,... | collective-permute-start | bytes 737288 | tf_op jit(solution)/shard_map/ppermute | solution.py:435
  25.6 4.8 %collective-permute-start.11 = (f32[64,64]{1,0:T(8,128)S(1)}, f32[64,64]{1,0:T(8,128)S(1)}, u32[]{:S(2)}, u32[]{:S(2)}) collective-permute-start(f32[64,64]{1,0:T(8,128)S(1)} %add.21), channel_id=1, source_target_pairs={{0,16},{4,20},{8,24},{12,28},{16,0},{20,4},{24,8},{28,12},{1,17},{... | collective-permute-start | bytes 49160 | tf_op jit(solution)/shard_map/ppermute | solution.py:435
  32.9 2.6 %collective-permute-start.12 = (f32[512,256]{1,0:T(8,128)S(1)}, f32[512,256]{1,0:T(8,128)S(1)}, u32[]{:S(2)}, u32[]{:S(2)}) collective-permute-start(f32[512,256]{1,0:T(8,128)S(1)} %get-tuple-element.91.auto_a), channel_id=1, source_target_pairs={{0,1},{1,0},{2,3},{3,2},{4,5},{5,4},{6,7},{7,6},{8,9},{9,8},{10,11... | collective-permute-start | bytes 1572872 | tf_op jit(solution)/shard_map/ppermute | solution.py:435
  35.6 3.6 %collective-permute-start.13 = (f32[544,256]{1,0:T(8,128)S(1)}, f32[544,256]{1,0:T(8,128)S(1)}, u32[]{:S(2)}, u32[]{:S(2)}) collective-permute-start(f32[544,256]{1,0:T(8,128)S(1)} %get-tuple-element.101.refs_0_), channel_id=1, source_target_pairs={{0,1},{1,0},{2,3},{3,2},{4,5},{5,4},{6,7},{7,6},{8,9},{9,8},{10,11... | collective-permute-start | bytes 1671176 | tf_op jit(solution)/shard_map/ppermute | solution.py:435
  36.1 3.1 %collective-permute-start.14 = (f32[8,256]{1,0:T(8,128)S(1)}, f32[8,256]{1,0:T(8,128)S(1)}, u32[]{:S(2)}, u32[]{:S(2)}) collective-permute-start(f32[8,256]{1,0:T(8,128)S(1)} %get-tuple-element.102.refs_2_), channel_id=1, source_target_pairs={{0,1},{1,0},{2,3},{3,2},{4,5},{5,4},{6,7},{7,6},{8,9},{9,8},{10,11... | collective-permute-start | bytes 24584 | tf_op jit(solution)/shard_map/ppermute | solution.py:435
  40.4 4.0 %collective-permute-start.16 = (f32[64,64]{1,0:T(8,128)S(1)}, f32[64,64]{1,0:T(8,128)S(1)}, u32[]{:S(2)}, u32[]{:S(2)}) collective-permute-start(f32[64,64]{1,0:T(8,128)S(1)} %get-tuple-element.112), channel_id=1, source_target_pairs={{0,4},{4,0},{8,12},{12,8},{16,20},{20,16},{24,28},{28,24},{1,5},{5... | collective-permute-start | bytes 49160 | tf_op jit(solution)/shard_map/ppermute | solution.py:435
  44.4 5.7 %collective-permute-start.18 = (f32[64,64]{1,0:T(8,128)S(1)}, f32[64,64]{1,0:T(8,128)S(1)}, u32[]{:S(2)}, u32[]{:S(2)}) collective-permute-start(f32[64,64]{1,0:T(8,128)S(1)} %add.23.refs_3_), channel_id=1, source_target_pairs={{0,24},{4,28},{8,16},{12,20},{16,8},{20,12},{24,0},{28,4},{1,25},{... | collective-permute-start | bytes 49160 | tf_op jit(solution)/shard_map/ppermute | solution.py:435
  45.3 4.8 %collective-permute-start.17 = (f32[64,64]{1,0:T(8,128)S(1)}, f32[64,64]{1,0:T(8,128)S(1)}, u32[]{:S(2)}, u32[]{:S(2)}) collective-permute-start(f32[64,64]{1,0:T(8,128)S(1)} %add.23.refs_3_), channel_id=1, source_target_pairs={{0,8},{1,17},{2,10},{3,19},{4,12},{5,21},{6,14},{7,23},{8,0},{9,25... | collective-permute-start | bytes 49160 | tf_op jit(solution)/shard_map/ppermute | solution.py:445
  45.6 1.3 %collective-permute-start.15 = (f32[8,256]{1,0:T(8,128)S(1)}, f32[8,256]{1,0:T(8,128)S(1)}, u32[]{:S(2)}, u32[]{:S(2)}) collective-permute-start(f32[8,256]{1,0:T(8,128)S(1)} %get-tuple-element.111.refs_1_), channel_id=1, source_target_pairs={{0,1},{1,0},{2,3},{3,2},{4,5},{5,4},{6,7},{7,6},{8,9},{9,8},{10,11... | collective-permute-start | bytes 24584 | tf_op jit(solution)/shard_map/ppermute | solution.py:435
  50.1 1.2 %collective-permute-start.19 = (f32[64,64]{1,0:T(8,128)S(1)}, f32[64,64]{1,0:T(8,128)S(1)}, u32[]{:S(2)}, u32[]{:S(2)}) collective-permute-start(f32[64,64]{1,0:T(8,128)S(1)} %collective-permute-done.17.refs_4_), channel_id=1, source_target_pairs={{0,1},{1,0},{2,3},{3,2},{4,5},{5,4},{6,7},{7,6},{8,9},{9,8},{10,11... | collective-permute-start | bytes 49160 | tf_op jit(solution)/shard_map/ppermute | solution.py:435
  52.6 4.0 %collective-permute-start.21 = (f32[64,64]{1,0:T(8,128)S(1)}, f32[64,64]{1,0:T(8,128)S(1)}, u32[]{:S(2)}, u32[]{:S(2)}) collective-permute-start(f32[64,64]{1,0:T(8,128)S(1)} %get-tuple-element.121), channel_id=1, source_target_pairs={{0,4},{4,0},{8,12},{12,8},{16,20},{20,16},{24,28},{28,24},{1,5},{5... | collective-permute-start | bytes 49160 | tf_op jit(solution)/shard_map/ppermute | solution.py:435
  56.5 5.7 %collective-permute-start.23 = (f32[64,64]{1,0:T(8,128)S(1)}, f32[64,64]{1,0:T(8,128)S(1)}, u32[]{:S(2)}, u32[]{:S(2)}) collective-permute-start(f32[64,64]{1,0:T(8,128)S(1)} %add.24.refs_3_), channel_id=1, source_target_pairs={{0,24},{4,28},{8,16},{12,20},{16,8},{20,12},{24,0},{28,4},{1,25},{... | collective-permute-start | bytes 49160 | tf_op jit(solution)/shard_map/ppermute | solution.py:435
  58.6 4.0 %collective-permute-start.22 = (f32[64,64]{1,0:T(8,128)S(1)}, f32[64,64]{1,0:T(8,128)S(1)}, u32[]{:S(2)}, u32[]{:S(2)}) collective-permute-start(f32[64,64]{1,0:T(8,128)S(1)} %add.24.refs_3_), channel_id=1, source_target_pairs={{0,8},{1,17},{2,10},{3,19},{4,12},{5,21},{6,14},{7,23},{8,0},{9,25... | collective-permute-start | bytes 49160 | tf_op jit(solution)/shard_map/ppermute | solution.py:445
  62.6 1.2 %collective-permute-start.24 = (f32[64,64]{1,0:T(8,128)S(1)}, f32[64,64]{1,0:T(8,128)S(1)}, u32[]{:S(2)}, u32[]{:S(2)}) collective-permute-start(f32[64,64]{1,0:T(8,128)S(1)} %collective-permute-done.22.refs_4_), channel_id=1, source_target_pairs={{0,1},{1,0},{2,3},{3,2},{4,5},{5,4},{6,7},{7,6},{8,9},{9,8},{10,11... | collective-permute-start | bytes 49160 | tf_op jit(solution)/shard_map/ppermute | solution.py:435
  (3 other events, 21.6 us)

commit v4 on v3

--- a/solution.py
+++ b/solution.py
@@ -216,13 +216,14 @@
         rows = slice(s * CHUNKS, s * CHUNKS + plan.rows)
         part = dot(data_ref[rows, :], stk_ref[:, s * deep : (s + 1) * deep], NT)
         if s:
-            numer_ref[...] += part
+            numer_ref[: plan.rows, :] += part
         else:
-            numer_ref[...] = part if before is None else part + before[...]
+            numer_ref[: plan.rows, :] = part if before is None else part + before[...]
 
 
 def numer_tail_body(plan, shards, stk_a, stk_b, data_ref, before, bits_ref, *refs):
-    numer_ref, tail_ref, past, ahead, ahead2 = refs
+    numer_ref, past, ahead, ahead2 = refs
+    tail_ref = numer_ref.at[plan.rows :, :]
     tail_body(plan, shards, bits_ref, (stk_a, stk_b), tail_ref, past, ahead, ahead2)
     numer_body(plan, stk_b, data_ref, numer_ref, before)
 
@@ -372,8 +373,12 @@
 
 
 def update_body(plan, scale, shards, counts, x_ref, bits_ref, low_ref, den_ref, *refs):
-    numers, tails, grams = refs[: counts[0]], refs[counts[0] :][:2], refs[counts[0] + 2 :][: counts[1]]
-    refs = refs[counts[0] + 2 + counts[1] :]
+    numers, refs = refs[: counts[0]], refs[counts[0] :]
+    if counts[0] > 1:
+        tails = [numer[plan.rows :, :] for numer in numers]
+    else:
+        tails, refs = refs[:2], refs[2:]
+    grams, refs = refs[: counts[1]], refs[counts[1] :]
     if counts[0] > 1:
         numer_ref, refs = refs[0], refs[1:]
     out_ref, out_bits, out_low, gram_ref, pen, both = refs
@@ -529,7 +534,7 @@
     bits = doubling("tm")
     tracks = (bits, bits)
 
-    front = slice(0, steps // (2 * LANES) * LANES)
+    front = slice(0, 5 * steps // (8 * LANES) * LANES)
 
     def gather_round(x, i):
         return mixed(x, tracks[0][i], tracks[1][i])
@@ -614,13 +619,13 @@
         (far_front, far_back, far_rims, auto)
     )
     auto_far = swap(auto, "chan", 1)
-    numer, tail = call(
+    numer = call(
         functools.partial(numer_tail_body, plan, shards),
-        (field, rest),
+        sds((rows + REACH, width), F32),
         vmem(5),
         tail_room,
     )(stk, far_stk, lay(far_front, far_back, far_rims), numer, bits_x)
-    numer, tail, auto_far = lax.optimization_barrier((numer, tail, auto_far))
+    numer, auto_far = lax.optimization_barrier((numer, auto_far))
     numer_far = swap(numer, "chan", 1)
     grams = [gram]
 
@@ -655,7 +660,7 @@
             den = conv(every[REACH + 3:], bits_x, part)
             grams = gram_rounds(gram, odd, (part,), (den, tails[1]))
         else:
-            tails = (tail, swap(tail, "chan", 1))
+            tails = ()
         operands = (x, bits_x, low_x, den, *numers_now, *tails, *grams)
         counts = (len(numers_now), len(grams))
         if sweep == ITERS - 1:

time: 65.7 us -> 65.1 us (level)
  waiting for transfers between devices: 18.6 us -> 17.1 us
  starting transfers between devices: 21.9 us -> 22.8 us
    ppermute x19 -> x18, waiting for transfers between devices: 18.3 us -> 16.3 us  [swap(): return lax.ppermute(x, axis, [(i, i ^ bit) for i in range(count)])]
    ppermute x19 -> x18, starting transfers between devices: 15 us -> 16.2 us  [swap(): return lax.ppermute(x, axis, [(i, i ^ bit) for i in range(count)])]
  transfers between devices with their start and end apart: 25 -> 24, of which waited for: 14 -> 16; matrix products, arithmetic and copies ran while one was open for 0% -> 0% of each run, Pallas kernels for 27% -> 28%
where the time goes in v4:
time: 65.1 us; the launch traced here: 64.9 us
  Pallas kernels  23.7 us (36%)
  starting transfers between devices  22.8 us (35%)
  waiting for transfers between devices  17.1 us (26%)
  local copies, waits for them, and re-layouts  0.91 us (1%)
    ppermute x18, waiting for transfers between devices, swap(): return lax.ppermute(x, axis, [(i, i ^ bit) for i in range(count)])  16.3 us
    ppermute x18, starting transfers between devices, swap(): return lax.ppermute(x, axis, [(i, i ^ bit) for i in range(count)])  16.2 us
    ppermute x5, starting transfers between devices, mixed(): return lax.ppermute(x, ('tm', 'chan'), pairs)  6.15 us
    pallas_call x2, Pallas kernels, conv_tail(): call(functools.partial(conv_tail_body, plan, shards, offsets), (field, re...  4.77 us
    pallas_call x2, Pallas kernels, autos(): call(functools.partial(auto_body, plan, moved), (sds((width, plan.tiles *...  3.17 us
    pallas_call x1, Pallas kernels, on_device(): call(functools.partial(first_conv_body, plan, every), (mats, mats, sds((r...  2.97 us
    pallas_call x2, Pallas kernels, on_device(): call(functools.partial(update_body, plan, scale, shards, counts), outs, v...  2.45 us
    pallas_call x1, Pallas kernels, on_device(): call(functools.partial(numer_tail_body, plan, shards), sds((rows + REACH,...  2.12 us
  transfers between devices with their start and end apart: 24, of which 16 were waited for; matrix products, arithmetic and copies ran while one was open for 0% of the time, Pallas kernels for 28%

profile of v4, /device:TPU:0, one launch (start us, length us, event | category | flops | bytes accessed | tf_op | source)
XLA Modules:
  0.0 64.9 jit_solution(5236566757720984618)
XLA Ops:
  0.0 3.0 %collective-permute-start = (bf16[1,96,256]{2,1,0:T(8,128)(2,1)}, bf16[1,96,256]{2,1,0:T(8,128)(2,1)S(1)}, u32[]{:S(2)}, u32[]{:S(2)}) collective-permute-start(bf16[1,96,256]{2,1,0:T(8,128)(2,1)} %bitcast.5), channel_id=1, source_target_pairs={{0,8},{1,9},{2,10},{3,11},{4,12},{5,13},{6,14},{7,15},{8,0},{9,1},... | collective-permute-start | bytes 147464 | tf_op jit(solution)/shard_map/ppermute | solution.py:450
  3.9 1.6 %shard_map.37 = (bf16[96,2048]{1,0:T(8,128)(2,1)S(1)}, bf16[1,96,256]{2,1,0:T(8,128)(2,1)S(1)}, f32[64,64]{1,0:T(8,128)S(1)}, bf16[224,128]{1,0:T(8,128)(2,1)S(1)}, bf16[224,128]{1,0:T(8,128)(2,1)S(1)}) custom-call(f32[64,2048]{1,0:T(8,128)} %load_ref.1, bf16[96,2048]{1,0:T(8,128)(2,1)} %data_any.1, bf16[96,256]{1,0:T(8,128)(2,1)S(1)} %copy-done.1), custom_call_target="tpu_custom_call" | custom-call | tf_op jit(solution)/shard_map/pallas_call | solution.py:516
  5.5 1.9 %collective-permute-start.4 = (bf16[96,1280]{1,0:T(8,128)(2,1)S(1)}, bf16[96,1280]{1,0:T(8,128)(2,1)S(1)}, u32[]{:S(2)}, u32[]{:S(2)}) collective-permute-start(bf16[96,1280]{1,0:T(8,128)(2,1)S(1)} %slice.15), channel_id=1, source_target_pairs={{0,2},{1,3},{2,0},{3,1},{4,6},{5,7},{6,4},{7,5},{8,10},{9,11},{10,... | collective-permute-start | bytes 737288 | tf_op jit(solution)/shard_map/ppermute | solution.py:440
  7.4 2.6 %collective-permute-start.1 = (bf16[2,96,256]{2,1,0:T(8,128)(2,1)S(1)}, bf16[2,96,256]{2,1,0:T(8,128)(2,1)S(1)}, u32[]{:S(2)}, u32[]{:S(2)}) collective-permute-start(bf16[2,96,256]{2,1,0:T(8,128)(2,1)S(1)} %get-tuple-element.123), channel_id=1, source_target_pairs={{0,16},{1,17},{2,18},{3,19},{4,20},{5,21},{6,22},{7,23},{8,24},{9,... | collective-permute-start | bytes 294920 | tf_op jit(solution)/shard_map/ppermute | solution.py:450
  10.0 1.5 %collective-permute-start.3 = (bf16[224,128]{1,0:T(8,128)(2,1)S(1)}, bf16[224,128]{1,0:T(8,128)(2,1)S(1)}, u32[]{:S(2)}, u32[]{:S(2)}) collective-permute-start(bf16[224,128]{1,0:T(8,128)(2,1)S(1)} %get-tuple-element.65), channel_id=1, source_target_pairs={{0,4},{4,0},{8,12},{12,8},{16,20},{20,16},{24,28},{28,24},{1,5},{5... | collective-permute-start | bytes 172040 | tf_op jit(solution)/shard_map/ppermute | solution.py:440
  11.5 1.6 %collective-permute-start.2 = (f32[64,64]{1,0:T(8,128)S(1)}, f32[64,64]{1,0:T(8,128)S(1)}, u32[]{:S(2)}, u32[]{:S(2)}) collective-permute-start(f32[64,64]{1,0:T(8,128)S(1)} %get-tuple-element.63), channel_id=1, source_target_pairs={{0,8},{4,12},{8,0},{12,4},{16,24},{20,28},{24,16},{28,20},{1,9},{5... | collective-permute-start | bytes 49160 | tf_op jit(solution)/shard_map/ppermute | solution.py:440
  13.6 1.8 %collective-permute-done.2 = f32[64,64]{1,0:T(8,128)S(1)} collective-permute-done((f32[64,64]{1,0:T(8,128)S(1)}, f32[64,64]{1,0:T(8,128)S(1)}, u32[]{:S(2)}, u32[]{:S(2)}) %collective-permute-start.2) | collective-permute-done | bytes 16416 | tf_op jit(solution)/shard_map/ppermute | solution.py:440
  15.9 1.6 %collective-permute-start.6 = (bf16[4,96,256]{2,1,0:T(8,128)(2,1)S(1)}, bf16[4,96,256]{2,1,0:T(8,128)(2,1)S(1)}, u32[]{:S(2)}, u32[]{:S(2)}) collective-permute-start(bf16[4,96,256]{2,1,0:T(8,128)(2,1)S(1)} %constant_dynamic-update-slice_fusion.2.first_ref), channel_id=1, source_target_pairs={{0,2},{1,3},{2,0},{3,1},{4,6},{5,7},{6,4},{7,5},{8,10},{9,11},{10,... | collective-permute-start | bytes 589832 | tf_op jit(solution)/shard_map/ppermute | solution.py:440
  18.0 1.5 %collective-permute-start.7 = (f32[64,64]{1,0:T(8,128)S(1)}, f32[64,64]{1,0:T(8,128)S(1)}, u32[]{:S(2)}, u32[]{:S(2)}) collective-permute-start(f32[64,64]{1,0:T(8,128)S(1)} %add.19), channel_id=1, source_target_pairs={{0,4},{4,0},{8,12},{12,8},{16,20},{20,16},{24,28},{28,24},{1,5},{5... | collective-permute-start | bytes 49160 | tf_op jit(solution)/shard_map/ppermute | solution.py:440
  21.8 1.7 %collective-permute-done.7 = f32[64,64]{1,0:T(8,128)S(1)} collective-permute-done((f32[64,64]{1,0:T(8,128)S(1)}, f32[64,64]{1,0:T(8,128)S(1)}, u32[]{:S(2)}, u32[]{:S(2)}) %collective-permute-start.7) | collective-permute-done | bytes 16416 | tf_op jit(solution)/shard_map/ppermute | solution.py:440
  24.7 1.6 %shard_map.40 = (bf16[256,4608]{1,0:T(8,128)(2,1)S(1)}, f32[512,256]{1,0:T(8,128)S(1)}) custom-call(bf16[4,96,256]{2,1,0:T(8,128)(2,1)S(1)} %constant_dynamic-update-slice_fusion.2.first_ref, bf16[4,96,256]{2,1,0:T(8,128)(2,1)S(1)} %collective-permute-done.5.second_ref), custom_call_target="tpu_custom_call" | custom-call | tf_op jit(solution)/shard_map/pallas_call | solution.py:607
  26.3 1.5 %shard_map.41.before = f32[544,256]{1,0:T(8,128)S(1)} custom-call(bf16[256,4608]{1,0:T(8,128)(2,1)S(1)} %get-tuple-element.83.stk_ref.stk_a, bf16[672,512]{1,0:T(8,128)(2,1)S(1)} %shard_map.38.data_ref), custom_call_target="tpu_custom_call" | custom-call | tf_op jit(solution)/shard_map/pallas_call | solution.py:615
  27.8 1.7 %collective-permute-done.11 = f32[64,64]{1,0:T(8,128)S(1)} collective-permute-done((f32[64,64]{1,0:T(8,128)S(1)}, f32[64,64]{1,0:T(8,128)S(1)}, u32[]{:S(2)}, u32[]{:S(2)}) %collective-permute-start.11) | collective-permute-done | bytes 16416 | tf_op jit(solution)/shard_map/ppermute | solution.py:440
  30.2 1.6 %shard_map.42 = (bf16[256,4608]{1,0:T(8,128)(2,1)S(1)}, f32[512,256]{1,0:T(8,128)S(1)}) custom-call(bf16[4,96,256]{2,1,0:T(8,128)(2,1)S(1)} %collective-permute-done.6.first_ref, bf16[5,96,256]{2,1,0:T(8,128)(2,1)S(1)} %collective-permute-done.10.second_ref, f32[512,256]{1,0:T(8,128)S(1)} %get-tuple-element.86.refs_0_), custom_call_target="tpu_custom_call" | custom-call | tf_op jit(solution)/shard_map/pallas_call | solution.py:607
  32.4 2.1 %shard_map.44.refs_0_ = f32[552,256]{1,0:T(8,128)S(1)} custom-call(bf16[256,4608]{1,0:T(8,128)(2,1)S(1)} %get-tuple-element.83.stk_ref.stk_a, bf16[256,4608]{1,0:T(8,128)(2,1)S(1)} %get-tuple-element.89.stk_b, bf16[672,512]{1,0:T(8,128)(2,1)S(1)} %shard_map.43.data_ref, f32[544,256]{1,0:T(8,128)S(1)} %shard_map.41.before, ...), custom_call_target="tpu_custom_call" | custom-call | tf_op jit(solution)/shard_map/pallas_call | solution.py:622
  35.0 3.0 %shard_map.45 = (bf16[2304,256]{1,0:T(8,128)(2,1)S(1)}, bf16[2304,256]{1,0:T(8,128)(2,1)S(1)}, f32[544,256]{1,0:T(8,128)S(1)}) custom-call(f32[512,256]{1,0:T(8,128)S(1)} %get-tuple-element.88.auto_a, f32[512,256]{1,0:T(8,128)S(1)} %collective-permute-done.12.auto_b, bf16[800,256]{1,0:T(8,128)(2,1)S(1)} %get-tuple-element.75.bits_ref), custom_call_target="tpu_custom_call" | custom-call | tf_op jit(solution)/shard_map/pallas_call | solution.py:634
  38.0 1.2 %shard_map.46 = (f32[544,256]{1,0:T(8,128)S(1)}, f32[544,256]{1,0:T(8,128)S(1)}, bf16[800,256]{1,0:T(8,128)(2,1)S(1)}, bf16[544,256]{1,0:T(8,128)(2,1)S(1)}, f32[64,64]{1,0:T(8,128)S(1)}) custom-call(f32[544,256]{1,0:T(8,128)S(1)} %get-tuple-element.74.x_ref, bf16[800,256]{1,0:T(8,128)(2,1)S(1)} %get-tuple-element.75.bits_ref, ...), custom_call_target="tpu_custom_call" | custom-call | tf_op jit(solution)/shard_map/pallas_call | solution.py:676
  40.3 2.4 %shard_map.47 = (f32[544,256]{1,0:T(8,128)S(1)}, f32[8,256]{1,0:T(8,128)S(1)}) custom-call(bf16[800,256]{1,0:T(8,128)(2,1)S(1)} %get-tuple-element.99.bits_ref, bf16[2304,256]{1,0:T(8,128)(2,1)S(1)} %get-tuple-element.101.high_ref, bf16[2304,256]{1,0:T(8,128)(2,1)S(1)} %get-tuple-element.102.low_ref, bf16[256,4608]{1,0:T(8,128)(2,1)S(1)} %get-tuple-element.83.stk_ref.stk_a, ...), custom_call_target="tpu_custom_call" | custom-call | tf_op jit(solution)/shard_map/pallas_call | solution.py:647
  43.3 2.3 %collective-permute-start.17 = (f32[64,64]{1,0:T(8,128)S(1)}, f32[64,64]{1,0:T(8,128)S(1)}, u32[]{:S(2)}, u32[]{:S(2)}) collective-permute-start(f32[64,64]{1,0:T(8,128)S(1)} %add.23.refs_3_), channel_id=1, source_target_pairs={{0,24},{4,28},{8,16},{12,20},{16,8},{20,12},{24,0},{28,4},{1,25},{... | collective-permute-start | bytes 49160 | tf_op jit(solution)/shard_map/ppermute | solution.py:440
  46.7 2.4 %collective-permute-done.17.refs_6_ = f32[64,64]{1,0:T(8,128)S(1)} collective-permute-done((f32[64,64]{1,0:T(8,128)S(1)}, f32[64,64]{1,0:T(8,128)S(1)}, u32[]{:S(2)}, u32[]{:S(2)}) %collective-permute-start.17) | collective-permute-done | bytes 16416 | tf_op jit(solution)/shard_map/ppermute | solution.py:440
  53.2 2.4 %shard_map.50 = (f32[544,256]{1,0:T(8,128)S(1)}, f32[8,256]{1,0:T(8,128)S(1)}) custom-call(bf16[800,256]{1,0:T(8,128)(2,1)S(1)} %get-tuple-element.111.bits_ref, bf16[2304,256]{1,0:T(8,128)(2,1)S(1)} %get-tuple-element.101.high_ref, bf16[2304,256]{1,0:T(8,128)(2,1)S(1)} %get-tuple-element.102.low_ref, bf16[256,4608]{1,0:T(8,128)(2,1)S(1)} %get-tuple-element.83.stk_ref.stk_a, ...), custom_call_target="tpu_custom_call" | custom-call | tf_op jit(solution)/shard_map/pallas_call | solution.py:647
  55.9 1.9 %collective-permute-start.22 = (f32[64,64]{1,0:T(8,128)S(1)}, f32[64,64]{1,0:T(8,128)S(1)}, u32[]{:S(2)}, u32[]{:S(2)}) collective-permute-start(f32[64,64]{1,0:T(8,128)S(1)} %add.24.refs_3_), channel_id=1, source_target_pairs={{0,24},{4,28},{8,16},{12,20},{16,8},{20,12},{24,0},{28,4},{1,25},{... | collective-permute-start | bytes 49160 | tf_op jit(solution)/shard_map/ppermute | solution.py:440
  59.0 2.7 %collective-permute-done.22.refs_6_ = f32[64,64]{1,0:T(8,128)S(1)} collective-permute-done((f32[64,64]{1,0:T(8,128)S(1)}, f32[64,64]{1,0:T(8,128)S(1)}, u32[]{:S(2)}, u32[]{:S(2)}) %collective-permute-start.22) | collective-permute-done | bytes 16416 | tf_op jit(solution)/shard_map/ppermute | solution.py:440
  63.2 1.7 %shard_map.52 = f32[64,2048]{1,0:T(8,128)} custom-call(f32[544,256]{1,0:T(8,128)S(1)} %get-tuple-element.110.x_ref, bf16[800,256]{1,0:T(8,128)(2,1)S(1)} %get-tuple-element.111.bits_ref, bf16[544,256]{1,0:T(8,128)(2,1)S(1)} %get-tuple-element.112.low_ref, f32[544,256]{1,0:T(8,128)S(1)} %shard_map.51.den_ref, f32[544,256]{1,0:T(8,128)S(1)} %get-tuple-element.104.refs_0_, ...), custom_call_target="tpu_custom_call" | custom-call | tf_op jit(solution)/shard_map/pallas_call | solution.py:667
  (60 shorter events, 17.6 us)
Async XLA Ops:
  0.0 5.4 %collective-permute-start = (bf16[1,96,256]{2,1,0:T(8,128)(2,1)}, bf16[1,96,256]{2,1,0:T(8,128)(2,1)S(1)}, u32[]{:S(2)}, u32[]{:S(2)}) collective-permute-start(bf16[1,96,256]{2,1,0:T(8,128)(2,1)} %bitcast.5), channel_id=1, source_target_pairs={{0,8},{1,9},{2,10},{3,11},{4,12},{5,13},{6,14},{7,15},{8,0},{9,1},... | collective-permute-start | bytes 147464 | tf_op jit(solution)/shard_map/ppermute | solution.py:450
  5.5 10.4 %collective-permute-start.4 = (bf16[96,1280]{1,0:T(8,128)(2,1)S(1)}, bf16[96,1280]{1,0:T(8,128)(2,1)S(1)}, u32[]{:S(2)}, u32[]{:S(2)}) collective-permute-start(bf16[96,1280]{1,0:T(8,128)(2,1)S(1)} %slice.15), channel_id=1, source_target_pairs={{0,2},{1,3},{2,0},{3,1},{4,6},{5,7},{6,4},{7,5},{8,10},{9,11},{10,... | collective-permute-start | bytes 737288 | tf_op jit(solution)/shard_map/ppermute | solution.py:440
  7.4 8.5 %collective-permute-start.1 = (bf16[2,96,256]{2,1,0:T(8,128)(2,1)S(1)}, bf16[2,96,256]{2,1,0:T(8,128)(2,1)S(1)}, u32[]{:S(2)}, u32[]{:S(2)}) collective-permute-start(bf16[2,96,256]{2,1,0:T(8,128)(2,1)S(1)} %get-tuple-element.123), channel_id=1, source_target_pairs={{0,16},{1,17},{2,18},{3,19},{4,20},{5,21},{6,22},{7,23},{8,24},{9,... | collective-permute-start | bytes 294920 | tf_op jit(solution)/shard_map/ppermute | solution.py:450
  10.0 5.9 %collective-permute-start.3 = (bf16[224,128]{1,0:T(8,128)(2,1)S(1)}, bf16[224,128]{1,0:T(8,128)(2,1)S(1)}, u32[]{:S(2)}, u32[]{:S(2)}) collective-permute-start(bf16[224,128]{1,0:T(8,128)(2,1)S(1)} %get-tuple-element.65), channel_id=1, source_target_pairs={{0,4},{4,0},{8,12},{12,8},{16,20},{20,16},{24,28},{28,24},{1,5},{5... | collective-permute-start | bytes 172040 | tf_op jit(solution)/shard_map/ppermute | solution.py:440
  11.5 3.9 %collective-permute-start.2 = (f32[64,64]{1,0:T(8,128)S(1)}, f32[64,64]{1,0:T(8,128)S(1)}, u32[]{:S(2)}, u32[]{:S(2)}) collective-permute-start(f32[64,64]{1,0:T(8,128)S(1)} %get-tuple-element.63), channel_id=1, source_target_pairs={{0,8},{4,12},{8,0},{12,4},{16,24},{20,28},{24,16},{28,20},{1,9},{5... | collective-permute-start | bytes 49160 | tf_op jit(solution)/shard_map/ppermute | solution.py:440
  13.0 6.5 %collective-permute-start.9 = (bf16[224,128]{1,0:T(8,128)(2,1)S(1)}, bf16[224,128]{1,0:T(8,128)(2,1)S(1)}, u32[]{:S(2)}, u32[]{:S(2)}) collective-permute-start(bf16[224,128]{1,0:T(8,128)(2,1)S(1)} %get-tuple-element.71), channel_id=1, source_target_pairs={{0,2},{1,3},{2,0},{3,1},{4,8},{5,9},{6,10},{7,11},{8,4},{9,5},{10,... | collective-permute-start | bytes 172040 | tf_op jit(solution)/shard_map/ppermute | solution.py:466
  15.4 6.5 %collective-permute-start.8 = (bf16[96,768]{1,0:T(8,128)(2,1)S(1)}, bf16[96,768]{1,0:T(8,128)(2,1)S(1)}, u32[]{:S(2)}, u32[]{:S(2)}) collective-permute-start(bf16[96,768]{1,0:T(8,128)(2,1)S(1)} %slice.16), channel_id=1, source_target_pairs={{0,2},{1,3},{2,0},{3,1},{4,6},{5,7},{6,4},{7,5},{8,10},{9,11},{10,... | collective-permute-start | bytes 442376 | tf_op jit(solution)/shard_map/ppermute | solution.py:440
  15.9 8.0 %collective-permute-start.6 = (bf16[4,96,256]{2,1,0:T(8,128)(2,1)S(1)}, bf16[4,96,256]{2,1,0:T(8,128)(2,1)S(1)}, u32[]{:S(2)}, u32[]{:S(2)}) collective-permute-start(bf16[4,96,256]{2,1,0:T(8,128)(2,1)S(1)} %constant_dynamic-update-slice_fusion.2.first_ref), channel_id=1, source_target_pairs={{0,2},{1,3},{2,0},{3,1},{4,6},{5,7},{6,4},{7,5},{8,10},{9,11},{10,... | collective-permute-start | bytes 589832 | tf_op jit(solution)/shard_map/ppermute | solution.py:440
  17.5 6.5 %collective-permute-start.5 = (bf16[4,96,256]{2,1,0:T(8,128)(2,1)S(1)}, bf16[4,96,256]{2,1,0:T(8,128)(2,1)S(1)}, u32[]{:S(2)}, u32[]{:S(2)}) collective-permute-start(bf16[4,96,256]{2,1,0:T(8,128)(2,1)S(1)} %constant_dynamic-update-slice_fusion.2.first_ref), channel_id=1, source_target_pairs={{0,4},{1,5},{2,6},{3,7},{4,0},{5,1},{6,2},{7,3},{8,12},{9,13},{10,... | collective-permute-start | bytes 589832 | tf_op jit(solution)/shard_map/ppermute | solution.py:450
  18.0 5.5 %collective-permute-start.7 = (f32[64,64]{1,0:T(8,128)S(1)}, f32[64,64]{1,0:T(8,128)S(1)}, u32[]{:S(2)}, u32[]{:S(2)}) collective-permute-start(f32[64,64]{1,0:T(8,128)S(1)} %add.19), channel_id=1, source_target_pairs={{0,4},{4,0},{8,12},{12,8},{16,20},{20,16},{24,28},{28,24},{1,5},{5... | collective-permute-start | bytes 49160 | tf_op jit(solution)/shard_map/ppermute | solution.py:440
  24.0 6.3 %collective-permute-start.10 = (bf16[5,96,256]{2,1,0:T(8,128)(2,1)S(1)}, bf16[5,96,256]{2,1,0:T(8,128)(2,1)S(1)}, u32[]{:S(2)}, u32[]{:S(2)}) collective-permute-start(bf16[5,96,256]{2,1,0:T(8,128)(2,1)S(1)} %pad_maximum_fusion), channel_id=1, source_target_pairs={{0,2},{1,3},{2,0},{3,1},{4,6},{5,7},{6,4},{7,5},{8,10},{9,11},{10,... | collective-permute-start | bytes 737288 | tf_op jit(solution)/shard_map/ppermute | solution.py:440
  24.7 4.8 %collective-permute-start.11 = (f32[64,64]{1,0:T(8,128)S(1)}, f32[64,64]{1,0:T(8,128)S(1)}, u32[]{:S(2)}, u32[]{:S(2)}) collective-permute-start(f32[64,64]{1,0:T(8,128)S(1)} %add.21), channel_id=1, source_target_pairs={{0,16},{4,20},{8,24},{12,28},{16,0},{20,4},{24,8},{28,12},{1,17},{... | collective-permute-start | bytes 49160 | tf_op jit(solution)/shard_map/ppermute | solution.py:440
  31.8 2.6 %collective-permute-start.12 = (f32[512,256]{1,0:T(8,128)S(1)}, f32[512,256]{1,0:T(8,128)S(1)}, u32[]{:S(2)}, u32[]{:S(2)}) collective-permute-start(f32[512,256]{1,0:T(8,128)S(1)} %get-tuple-element.88.auto_a), channel_id=1, source_target_pairs={{0,1},{1,0},{2,3},{3,2},{4,5},{5,4},{6,7},{7,6},{8,9},{9,8},{10,11... | collective-permute-start | bytes 1572872 | tf_op jit(solution)/shard_map/ppermute | solution.py:440
  34.5 3.5 %collective-permute-start.13 = (f32[552,256]{1,0:T(8,128)S(1)}, f32[552,256]{1,0:T(8,128)S(1)}, u32[]{:S(2)}, u32[]{:S(2)}) collective-permute-start(f32[552,256]{1,0:T(8,128)S(1)} %shard_map.44.refs_0_), channel_id=1, source_target_pairs={{0,1},{1,0},{2,3},{3,2},{4,5},{5,4},{6,7},{7,6},{8,9},{9,8},{10,11... | collective-permute-start | bytes 1695752 | tf_op jit(solution)/shard_map/ppermute | solution.py:440
  39.3 4.0 %collective-permute-start.15 = (f32[64,64]{1,0:T(8,128)S(1)}, f32[64,64]{1,0:T(8,128)S(1)}, u32[]{:S(2)}, u32[]{:S(2)}) collective-permute-start(f32[64,64]{1,0:T(8,128)S(1)} %get-tuple-element.106), channel_id=1, source_target_pairs={{0,4},{4,0},{8,12},{12,8},{16,20},{20,16},{24,28},{28,24},{1,5},{5... | collective-permute-start | bytes 49160 | tf_op jit(solution)/shard_map/ppermute | solution.py:440
  43.3 5.8 %collective-permute-start.17 = (f32[64,64]{1,0:T(8,128)S(1)}, f32[64,64]{1,0:T(8,128)S(1)}, u32[]{:S(2)}, u32[]{:S(2)}) collective-permute-start(f32[64,64]{1,0:T(8,128)S(1)} %add.23.refs_3_), channel_id=1, source_target_pairs={{0,24},{4,28},{8,16},{12,20},{16,8},{20,12},{24,0},{28,4},{1,25},{... | collective-permute-start | bytes 49160 | tf_op jit(solution)/shard_map/ppermute | solution.py:440
  45.5 4.0 %collective-permute-start.16 = (f32[64,64]{1,0:T(8,128)S(1)}, f32[64,64]{1,0:T(8,128)S(1)}, u32[]{:S(2)}, u32[]{:S(2)}) collective-permute-start(f32[64,64]{1,0:T(8,128)S(1)} %add.23.refs_3_), channel_id=1, source_target_pairs={{0,8},{1,17},{2,10},{3,19},{4,12},{5,21},{6,14},{7,23},{8,0},{9,25... | collective-permute-start | bytes 49160 | tf_op jit(solution)/shard_map/ppermute | solution.py:450
  45.5 1.2 %collective-permute-start.14 = (f32[8,256]{1,0:T(8,128)S(1)}, f32[8,256]{1,0:T(8,128)S(1)}, u32[]{:S(2)}, u32[]{:S(2)}) collective-permute-start(f32[8,256]{1,0:T(8,128)S(1)} %get-tuple-element.105.refs_1_), channel_id=1, source_target_pairs={{0,1},{1,0},{2,3},{3,2},{4,5},{5,4},{6,7},{7,6},{8,9},{9,8},{10,11... | collective-permute-start | bytes 24584 | tf_op jit(solution)/shard_map/ppermute | solution.py:440
  49.5 1.2 %collective-permute-start.18 = (f32[64,64]{1,0:T(8,128)S(1)}, f32[64,64]{1,0:T(8,128)S(1)}, u32[]{:S(2)}, u32[]{:S(2)}) collective-permute-start(f32[64,64]{1,0:T(8,128)S(1)} %collective-permute-done.16.refs_4_), channel_id=1, source_target_pairs={{0,1},{1,0},{2,3},{3,2},{4,5},{5,4},{6,7},{7,6},{8,9},{9,8},{10,11... | collective-permute-start | bytes 49160 | tf_op jit(solution)/shard_map/ppermute | solution.py:440
  52.0 4.0 %collective-permute-start.20 = (f32[64,64]{1,0:T(8,128)S(1)}, f32[64,64]{1,0:T(8,128)S(1)}, u32[]{:S(2)}, u32[]{:S(2)}) collective-permute-start(f32[64,64]{1,0:T(8,128)S(1)} %get-tuple-element.115), channel_id=1, source_target_pairs={{0,4},{4,0},{8,12},{12,8},{16,20},{20,16},{24,28},{28,24},{1,5},{5... | collective-permute-start | bytes 49160 | tf_op jit(solution)/shard_map/ppermute | solution.py:440
  55.9 5.7 %collective-permute-start.22 = (f32[64,64]{1,0:T(8,128)S(1)}, f32[64,64]{1,0:T(8,128)S(1)}, u32[]{:S(2)}, u32[]{:S(2)}) collective-permute-start(f32[64,64]{1,0:T(8,128)S(1)} %add.24.refs_3_), channel_id=1, source_target_pairs={{0,24},{4,28},{8,16},{12,20},{16,8},{20,12},{24,0},{28,4},{1,25},{... | collective-permute-start | bytes 49160 | tf_op jit(solution)/shard_map/ppermute | solution.py:440
  57.8 4.2 %collective-permute-start.21 = (f32[64,64]{1,0:T(8,128)S(1)}, f32[64,64]{1,0:T(8,128)S(1)}, u32[]{:S(2)}, u32[]{:S(2)}) collective-permute-start(f32[64,64]{1,0:T(8,128)S(1)} %add.24.refs_3_), channel_id=1, source_target_pairs={{0,8},{1,17},{2,10},{3,19},{4,12},{5,21},{6,14},{7,23},{8,0},{9,25... | collective-permute-start | bytes 49160 | tf_op jit(solution)/shard_map/ppermute | solution.py:450
  57.8 1.2 %collective-permute-start.19 = (f32[8,256]{1,0:T(8,128)S(1)}, f32[8,256]{1,0:T(8,128)S(1)}, u32[]{:S(2)}, u32[]{:S(2)}) collective-permute-start(f32[8,256]{1,0:T(8,128)S(1)} %get-tuple-element.114.refs_1_), channel_id=1, source_target_pairs={{0,1},{1,0},{2,3},{3,2},{4,5},{5,4},{6,7},{7,6},{8,9},{9,8},{10,11... | collective-permute-start | bytes 24584 | tf_op jit(solution)/shard_map/ppermute | solution.py:440
  62.0 1.2 %collective-permute-start.23 = (f32[64,64]{1,0:T(8,128)S(1)}, f32[64,64]{1,0:T(8,128)S(1)}, u32[]{:S(2)}, u32[]{:S(2)}) collective-permute-start(f32[64,64]{1,0:T(8,128)S(1)} %collective-permute-done.21.refs_4_), channel_id=1, source_target_pairs={{0,1},{1,0},{2,3},{3,2},{4,5},{5,4},{6,7},{7,6},{8,9},{9,8},{10,11... | collective-permute-start | bytes 49160 | tf_op jit(solution)/shard_map/ppermute | solution.py:440
  (2 other events, 20.4 us)

commit v5 on v4

--- a/solution.py
+++ b/solution.py
@@ -534,8 +534,6 @@
     bits = doubling("tm")
     tracks = (bits, bits)
 
-    front = slice(0, 5 * steps // (8 * LANES) * LANES)
-
     def gather_round(x, i):
         return mixed(x, tracks[0][i], tracks[1][i])
 
@@ -545,11 +543,10 @@
             gram_near = swap(gram, "tm", bits[i - 1])
             if i == 1:
                 wide_rim = between(wide_rim)
-                ready = after(data_in, even)
-                far_data = [swap(ready[:, at], "chan", 2) for at in (front, slice(front.stop, steps))]
+                far_data = swap(data, "chan", 2)
                 near_rim = swap(after(near_rim, even), "tm", bits[-1])
-                near, gram_near, near_rim, far_front = lax.optimization_barrier(
-                    (near, gram_near, near_rim, far_data[0])
+                near, gram_near, near_rim, far_data = lax.optimization_barrier(
+                    (near, gram_near, near_rim, far_data)
                 )
             else:
                 near, gram_near = lax.optimization_barrier((near, gram_near))
@@ -593,8 +590,8 @@
         vmem(3),
         [pltpu.VMEM((steps + 2 * LANES, LANES), F32)],
     )(loadings, left, right)
-    odds, far_even, gram_near, far_back, own_laid, x, bits_x = lax.optimization_barrier(
-        (odds, far_even, gram_near, far_data[1], own_laid, x, bits_x)
+    odds, far_even, gram_near, own_laid, x, bits_x = lax.optimization_barrier(
+        (odds, far_even, gram_near, own_laid, x, bits_x)
     )
     gram = gram + gram_near
     gram_near = swap(gram, "tm", bits[-2])
@@ -615,16 +612,14 @@
     numer = call(functools.partial(numer_body, plan), field, vmem(2))(stk, own_laid)
     far_odds, numer = lax.optimization_barrier((far_odds, numer))
     far_stk, auto = autos(far_even, far_odds, auto)
-    far_front, far_back, far_rims, auto = lax.optimization_barrier(
-        (far_front, far_back, far_rims, auto)
-    )
+    far_data, far_rims, auto = lax.optimization_barrier((far_data, far_rims, auto))
     auto_far = swap(auto, "chan", 1)
     numer = call(
         functools.partial(numer_tail_body, plan, shards),
         sds((rows + REACH, width), F32),
         vmem(5),
         tail_room,
-    )(stk, far_stk, lay(far_front, far_back, far_rims), numer, bits_x)
+    )(stk, far_stk, lay(far_data, far_rims), numer, bits_x)
     numer, auto_far = lax.optimization_barrier((numer, auto_far))
     numer_far = swap(numer, "chan", 1)
     grams = [gram]

time: 65.1 us -> 63.7 us (0.978)
  waiting for transfers between devices: 17.1 us -> 15.1 us
    ppermute x18 -> x17, waiting for transfers between devices: 16.3 us -> 13.4 us  [swap(): return lax.ppermute(x, axis, [(i, i ^ bit) for i in range(count)])]
    ppermute x18 -> x17, starting transfers between devices: 16.2 us -> 18 us  [swap(): return lax.ppermute(x, axis, [(i, i ^ bit) for i in range(count)])]
    ppermute x5, starting transfers between devices: 6.15 us -> 4.91 us  [mixed(): return lax.ppermute(x, ('tm', 'chan'), pairs)]
    ppermute x5, waiting for transfers between devices: 0.8 us -> 1.6 us  [mixed(): return lax.ppermute(x, ('tm', 'chan'), pairs)]
  transfers between devices with their start and end apart: 24 -> 23, of which waited for: 16 -> 13; matrix products, arithmetic and copies ran while one was open for 0% -> 0% of each run, Pallas kernels for 28% -> 29%
where the time goes in v5:
time: 63.7 us; the launch traced here: 63.5 us
  Pallas kernels  23.9 us (38%)
  starting transfers between devices  23.4 us (37%)
  waiting for transfers between devices  15.1 us (24%)
  local copies, waits for them, and re-layouts  0.87 us (1%)
    ppermute x17, starting transfers between devices, swap(): return lax.ppermute(x, axis, [(i, i ^ bit) for i in range(count)])  18 us
    ppermute x17, waiting for transfers between devices, swap(): return lax.ppermute(x, axis, [(i, i ^ bit) for i in range(count)])  13.4 us
    ppermute x5, starting transfers between devices, mixed(): return lax.ppermute(x, ('tm', 'chan'), pairs)  4.91 us
    pallas_call x2, Pallas kernels, conv_tail(): call(functools.partial(conv_tail_body, plan, shards, offsets), (field, re...  4.77 us
    pallas_call x2, Pallas kernels, autos(): call(functools.partial(auto_body, plan, moved), (sds((width, plan.tiles *...  3.17 us
    pallas_call x1, Pallas kernels, on_device(): call(functools.partial(first_conv_body, plan, every), (mats, mats, sds((r...  2.97 us
    pallas_call x2, Pallas kernels, on_device(): call(functools.partial(update_body, plan, scale, shards, counts), outs, v...  2.45 us
    pallas_call x2, Pallas kernels, conv(): call(functools.partial(conv_body, plan, offsets), field, vmem(4))  2.24 us
  transfers between devices with their start and end apart: 23, of which 13 were waited for; matrix products, arithmetic and copies ran while one was open for 0% of the time, Pallas kernels for 29%

profile of v5, /device:TPU:0, one launch (start us, length us, event | category | flops | bytes accessed | tf_op | source)
XLA Modules:
  0.0 63.5 jit_solution(2371167076714732082)
XLA Ops:
  0.0 3.0 %collective-permute-start.4 = (bf16[96,2048]{1,0:T(8,128)(2,1)}, bf16[96,2048]{1,0:T(8,128)(2,1)S(1)}, u32[]{:S(2)}, u32[]{:S(2)}) collective-permute-start(bf16[96,2048]{1,0:T(8,128)(2,1)} %data_any.1), channel_id=1, source_target_pairs={{0,2},{1,3},{2,0},{3,1},{4,6},{5,7},{6,4},{7,5},{8,10},{9,11},{10,... | collective-permute-start | bytes 1179656 | tf_op jit(solution)/shard_map/ppermute | solution.py:440
  3.0 1.6 %collective-permute-start = (bf16[1,96,256]{2,1,0:T(8,128)(2,1)}, bf16[1,96,256]{2,1,0:T(8,128)(2,1)S(1)}, u32[]{:S(2)}, u32[]{:S(2)}) collective-permute-start(bf16[1,96,256]{2,1,0:T(8,128)(2,1)} %bitcast.5), channel_id=1, source_target_pairs={{0,8},{1,9},{2,10},{3,11},{4,12},{5,13},{6,14},{7,15},{8,0},{9,1},... | collective-permute-start | bytes 147464 | tf_op jit(solution)/shard_map/ppermute | solution.py:450
  5.4 1.6 %shard_map.37 = (bf16[96,2048]{1,0:T(8,128)(2,1)S(1)}, bf16[1,96,256]{2,1,0:T(8,128)(2,1)S(1)}, f32[64,64]{1,0:T(8,128)S(1)}, bf16[224,128]{1,0:T(8,128)(2,1)S(1)}, bf16[224,128]{1,0:T(8,128)(2,1)S(1)}) custom-call(f32[64,2048]{1,0:T(8,128)} %load_ref.1, bf16[96,2048]{1,0:T(8,128)(2,1)} %data_any.1, bf16[96,256]{1,0:T(8,128)(2,1)S(1)} %copy-done.1), custom_call_target="tpu_custom_call" | custom-call | tf_op jit(solution)/shard_map/pallas_call | solution.py:516
  7.3 2.7 %collective-permute-start.1 = (bf16[2,96,256]{2,1,0:T(8,128)(2,1)S(1)}, bf16[2,96,256]{2,1,0:T(8,128)(2,1)S(1)}, u32[]{:S(2)}, u32[]{:S(2)}) collective-permute-start(bf16[2,96,256]{2,1,0:T(8,128)(2,1)S(1)} %get-tuple-element.117), channel_id=1, source_target_pairs={{0,16},{1,17},{2,18},{3,19},{4,20},{5,21},{6,22},{7,23},{8,24},{9,... | collective-permute-start | bytes 294920 | tf_op jit(solution)/shard_map/ppermute | solution.py:450
  9.9 1.5 %collective-permute-start.3 = (bf16[224,128]{1,0:T(8,128)(2,1)S(1)}, bf16[224,128]{1,0:T(8,128)(2,1)S(1)}, u32[]{:S(2)}, u32[]{:S(2)}) collective-permute-start(bf16[224,128]{1,0:T(8,128)(2,1)S(1)} %get-tuple-element.62), channel_id=1, source_target_pairs={{0,4},{4,0},{8,12},{12,8},{16,20},{20,16},{24,28},{28,24},{1,5},{5... | collective-permute-start | bytes 172040 | tf_op jit(solution)/shard_map/ppermute | solution.py:440
  11.4 1.6 %collective-permute-start.2 = (f32[64,64]{1,0:T(8,128)S(1)}, f32[64,64]{1,0:T(8,128)S(1)}, u32[]{:S(2)}, u32[]{:S(2)}) collective-permute-start(f32[64,64]{1,0:T(8,128)S(1)} %get-tuple-element.60), channel_id=1, source_target_pairs={{0,8},{4,12},{8,0},{12,4},{16,24},{20,28},{24,16},{28,20},{1,9},{5... | collective-permute-start | bytes 49160 | tf_op jit(solution)/shard_map/ppermute | solution.py:440
  13.5 1.8 %collective-permute-done.2 = f32[64,64]{1,0:T(8,128)S(1)} collective-permute-done((f32[64,64]{1,0:T(8,128)S(1)}, f32[64,64]{1,0:T(8,128)S(1)}, u32[]{:S(2)}, u32[]{:S(2)}) %collective-permute-start.2) | collective-permute-done | bytes 16416 | tf_op jit(solution)/shard_map/ppermute | solution.py:440
  16.6 1.4 %collective-permute-start.7 = (f32[64,64]{1,0:T(8,128)S(1)}, f32[64,64]{1,0:T(8,128)S(1)}, u32[]{:S(2)}, u32[]{:S(2)}) collective-permute-start(f32[64,64]{1,0:T(8,128)S(1)} %add.19), channel_id=1, source_target_pairs={{0,4},{4,0},{8,12},{12,8},{16,20},{20,16},{24,28},{28,24},{1,5},{5... | collective-permute-start | bytes 49160 | tf_op jit(solution)/shard_map/ppermute | solution.py:440
  19.1 2.9 %collective-permute-done.7 = f32[64,64]{1,0:T(8,128)S(1)} collective-permute-done((f32[64,64]{1,0:T(8,128)S(1)}, f32[64,64]{1,0:T(8,128)S(1)}, u32[]{:S(2)}, u32[]{:S(2)}) %collective-permute-start.7) | collective-permute-done | bytes 16416 | tf_op jit(solution)/shard_map/ppermute | solution.py:440
  22.0 1.6 %collective-permute-start.9 = (bf16[5,96,256]{2,1,0:T(8,128)(2,1)S(1)}, bf16[5,96,256]{2,1,0:T(8,128)(2,1)S(1)}, u32[]{:S(2)}, u32[]{:S(2)}) collective-permute-start(bf16[5,96,256]{2,1,0:T(8,128)(2,1)S(1)} %pad_maximum_fusion), channel_id=1, source_target_pairs={{0,2},{1,3},{2,0},{3,1},{4,6},{5,7},{6,4},{7,5},{8,10},{9,11},{10,... | collective-permute-start | bytes 737288 | tf_op jit(solution)/shard_map/ppermute | solution.py:440
  24.0 1.6 %shard_map.40 = (bf16[256,4608]{1,0:T(8,128)(2,1)S(1)}, f32[512,256]{1,0:T(8,128)S(1)}) custom-call(bf16[4,96,256]{2,1,0:T(8,128)(2,1)S(1)} %constant_dynamic-update-slice_fusion.2.first_ref, bf16[4,96,256]{2,1,0:T(8,128)(2,1)S(1)} %collective-permute-done.5.second_ref), custom_call_target="tpu_custom_call" | custom-call | tf_op jit(solution)/shard_map/pallas_call | solution.py:604
  25.6 1.5 %shard_map.41.before = f32[544,256]{1,0:T(8,128)S(1)} custom-call(bf16[256,4608]{1,0:T(8,128)(2,1)S(1)} %get-tuple-element.78.stk_ref.stk_a, bf16[672,512]{1,0:T(8,128)(2,1)S(1)} %shard_map.38.data_ref), custom_call_target="tpu_custom_call" | custom-call | tf_op jit(solution)/shard_map/pallas_call | solution.py:612
  27.1 1.3 %collective-permute-done.10 = f32[64,64]{1,0:T(8,128)S(1)} collective-permute-done((f32[64,64]{1,0:T(8,128)S(1)}, f32[64,64]{1,0:T(8,128)S(1)}, u32[]{:S(2)}, u32[]{:S(2)}) %collective-permute-start.10) | collective-permute-done | bytes 16416 | tf_op jit(solution)/shard_map/ppermute | solution.py:440
  28.4 1.6 %shard_map.42 = (bf16[256,4608]{1,0:T(8,128)(2,1)S(1)}, f32[512,256]{1,0:T(8,128)S(1)}) custom-call(bf16[4,96,256]{2,1,0:T(8,128)(2,1)S(1)} %collective-permute-done.6.first_ref, bf16[5,96,256]{2,1,0:T(8,128)(2,1)S(1)} %collective-permute-done.9.second_ref, f32[512,256]{1,0:T(8,128)S(1)} %get-tuple-element.81.refs_0_), custom_call_target="tpu_custom_call" | custom-call | tf_op jit(solution)/shard_map/pallas_call | solution.py:604
  30.5 2.1 %shard_map.44.refs_0_ = f32[552,256]{1,0:T(8,128)S(1)} custom-call(bf16[256,4608]{1,0:T(8,128)(2,1)S(1)} %get-tuple-element.78.stk_ref.stk_a, bf16[256,4608]{1,0:T(8,128)(2,1)S(1)} %get-tuple-element.84.stk_b, bf16[672,512]{1,0:T(8,128)(2,1)S(1)} %shard_map.43.data_ref, f32[544,256]{1,0:T(8,128)S(1)} %shard_map.41.before, ...), custom_call_target="tpu_custom_call" | custom-call | tf_op jit(solution)/shard_map/pallas_call | solution.py:617
  33.2 3.0 %shard_map.45 = (bf16[2304,256]{1,0:T(8,128)(2,1)S(1)}, bf16[2304,256]{1,0:T(8,128)(2,1)S(1)}, f32[544,256]{1,0:T(8,128)S(1)}) custom-call(f32[512,256]{1,0:T(8,128)S(1)} %get-tuple-element.83.auto_a, f32[512,256]{1,0:T(8,128)S(1)} %collective-permute-done.11.auto_b, bf16[800,256]{1,0:T(8,128)(2,1)S(1)} %get-tuple-element.71.bits_ref), custom_call_target="tpu_custom_call" | custom-call | tf_op jit(solution)/shard_map/pallas_call | solution.py:629
  38.7 2.4 %shard_map.47 = (f32[544,256]{1,0:T(8,128)S(1)}, f32[8,256]{1,0:T(8,128)S(1)}) custom-call(bf16[800,256]{1,0:T(8,128)(2,1)S(1)} %get-tuple-element.93.bits_ref, bf16[2304,256]{1,0:T(8,128)(2,1)S(1)} %get-tuple-element.95.high_ref, bf16[2304,256]{1,0:T(8,128)(2,1)S(1)} %get-tuple-element.96.low_ref, bf16[256,4608]{1,0:T(8,128)(2,1)S(1)} %get-tuple-element.78.stk_ref.stk_a, ...), custom_call_target="tpu_custom_call" | custom-call | tf_op jit(solution)/shard_map/pallas_call | solution.py:642
  41.4 2.8 %collective-permute-start.16 = (f32[64,64]{1,0:T(8,128)S(1)}, f32[64,64]{1,0:T(8,128)S(1)}, u32[]{:S(2)}, u32[]{:S(2)}) collective-permute-start(f32[64,64]{1,0:T(8,128)S(1)} %add.23.refs_3_), channel_id=1, source_target_pairs={{0,24},{4,28},{8,16},{12,20},{16,8},{20,12},{24,0},{28,4},{1,25},{... | collective-permute-start | bytes 49160 | tf_op jit(solution)/shard_map/ppermute | solution.py:440
  45.4 1.7 %collective-permute-done.16.refs_6_ = f32[64,64]{1,0:T(8,128)S(1)} collective-permute-done((f32[64,64]{1,0:T(8,128)S(1)}, f32[64,64]{1,0:T(8,128)S(1)}, u32[]{:S(2)}, u32[]{:S(2)}) %collective-permute-start.16) | collective-permute-done | bytes 16416 | tf_op jit(solution)/shard_map/ppermute | solution.py:440
  50.5 1.5 %collective-permute-start.19 = (f32[64,64]{1,0:T(8,128)S(1)}, f32[64,64]{1,0:T(8,128)S(1)}, u32[]{:S(2)}, u32[]{:S(2)}) collective-permute-start(f32[64,64]{1,0:T(8,128)S(1)} %get-tuple-element.109), channel_id=1, source_target_pairs={{0,4},{4,0},{8,12},{12,8},{16,20},{20,16},{24,28},{28,24},{1,5},{5... | collective-permute-start | bytes 49160 | tf_op jit(solution)/shard_map/ppermute | solution.py:440
  52.0 2.4 %shard_map.50 = (f32[544,256]{1,0:T(8,128)S(1)}, f32[8,256]{1,0:T(8,128)S(1)}) custom-call(bf16[800,256]{1,0:T(8,128)(2,1)S(1)} %get-tuple-element.105.bits_ref, bf16[2304,256]{1,0:T(8,128)(2,1)S(1)} %get-tuple-element.95.high_ref, bf16[2304,256]{1,0:T(8,128)(2,1)S(1)} %get-tuple-element.96.low_ref, bf16[256,4608]{1,0:T(8,128)(2,1)S(1)} %get-tuple-element.78.stk_ref.stk_a, ...), custom_call_target="tpu_custom_call" | custom-call | tf_op jit(solution)/shard_map/pallas_call | solution.py:642
  54.5 1.8 %collective-permute-start.21 = (f32[64,64]{1,0:T(8,128)S(1)}, f32[64,64]{1,0:T(8,128)S(1)}, u32[]{:S(2)}, u32[]{:S(2)}) collective-permute-start(f32[64,64]{1,0:T(8,128)S(1)} %add.24.refs_3_), channel_id=1, source_target_pairs={{0,24},{4,28},{8,16},{12,20},{16,8},{20,12},{24,0},{28,4},{1,25},{... | collective-permute-start | bytes 49160 | tf_op jit(solution)/shard_map/ppermute | solution.py:440
  57.5 2.8 %collective-permute-done.21.refs_6_ = f32[64,64]{1,0:T(8,128)S(1)} collective-permute-done((f32[64,64]{1,0:T(8,128)S(1)}, f32[64,64]{1,0:T(8,128)S(1)}, u32[]{:S(2)}, u32[]{:S(2)}) %collective-permute-start.21) | collective-permute-done | bytes 16416 | tf_op jit(solution)/shard_map/ppermute | solution.py:440
  61.8 1.7 %shard_map.52 = f32[64,2048]{1,0:T(8,128)} custom-call(f32[544,256]{1,0:T(8,128)S(1)} %get-tuple-element.104.x_ref, bf16[800,256]{1,0:T(8,128)(2,1)S(1)} %get-tuple-element.105.bits_ref, bf16[544,256]{1,0:T(8,128)(2,1)S(1)} %get-tuple-element.106.low_ref, f32[544,256]{1,0:T(8,128)S(1)} %shard_map.51.den_ref, f32[544,256]{1,0:T(8,128)S(1)} %get-tuple-element.98.refs_0_, ...), custom_call_target="tpu_custom_call" | custom-call | tf_op jit(solution)/shard_map/pallas_call | solution.py:662
  (56 shorter events, 15.7 us)
Async XLA Ops:
  0.0 18.0 %copy-start = (f32[64,2048]{1,0:T(8,128)S(1)}, f32[64,2048]{1,0:T(8,128)}, u32[]{:S(2)}) copy-start(f32[64,2048]{1,0:T(8,128)} %load_ref.1) | copy-start | bytes 1572868
  0.0 15.3 %collective-permute-start.4 = (bf16[96,2048]{1,0:T(8,128)(2,1)}, bf16[96,2048]{1,0:T(8,128)(2,1)S(1)}, u32[]{:S(2)}, u32[]{:S(2)}) collective-permute-start(bf16[96,2048]{1,0:T(8,128)(2,1)} %data_any.1), channel_id=1, source_target_pairs={{0,2},{1,3},{2,0},{3,1},{4,6},{5,7},{6,4},{7,5},{8,10},{9,11},{10,... | collective-permute-start | bytes 1179656 | tf_op jit(solution)/shard_map/ppermute | solution.py:440
  3.0 4.3 %collective-permute-start = (bf16[1,96,256]{2,1,0:T(8,128)(2,1)}, bf16[1,96,256]{2,1,0:T(8,128)(2,1)S(1)}, u32[]{:S(2)}, u32[]{:S(2)}) collective-permute-start(bf16[1,96,256]{2,1,0:T(8,128)(2,1)} %bitcast.5), channel_id=1, source_target_pairs={{0,8},{1,9},{2,10},{3,11},{4,12},{5,13},{6,14},{7,15},{8,0},{9,1},... | collective-permute-start | bytes 147464 | tf_op jit(solution)/shard_map/ppermute | solution.py:450
  7.3 8.1 %collective-permute-start.1 = (bf16[2,96,256]{2,1,0:T(8,128)(2,1)S(1)}, bf16[2,96,256]{2,1,0:T(8,128)(2,1)S(1)}, u32[]{:S(2)}, u32[]{:S(2)}) collective-permute-start(bf16[2,96,256]{2,1,0:T(8,128)(2,1)S(1)} %get-tuple-element.117), channel_id=1, source_target_pairs={{0,16},{1,17},{2,18},{3,19},{4,20},{5,21},{6,22},{7,23},{8,24},{9,... | collective-permute-start | bytes 294920 | tf_op jit(solution)/shard_map/ppermute | solution.py:450
  9.9 5.4 %collective-permute-start.3 = (bf16[224,128]{1,0:T(8,128)(2,1)S(1)}, bf16[224,128]{1,0:T(8,128)(2,1)S(1)}, u32[]{:S(2)}, u32[]{:S(2)}) collective-permute-start(bf16[224,128]{1,0:T(8,128)(2,1)S(1)} %get-tuple-element.62), channel_id=1, source_target_pairs={{0,4},{4,0},{8,12},{12,8},{16,20},{20,16},{24,28},{28,24},{1,5},{5... | collective-permute-start | bytes 172040 | tf_op jit(solution)/shard_map/ppermute | solution.py:440
  11.4 3.9 %collective-permute-start.2 = (f32[64,64]{1,0:T(8,128)S(1)}, f32[64,64]{1,0:T(8,128)S(1)}, u32[]{:S(2)}, u32[]{:S(2)}) collective-permute-start(f32[64,64]{1,0:T(8,128)S(1)} %get-tuple-element.60), channel_id=1, source_target_pairs={{0,8},{4,12},{8,0},{12,4},{16,24},{20,28},{24,16},{28,20},{1,9},{5... | collective-permute-start | bytes 49160 | tf_op jit(solution)/shard_map/ppermute | solution.py:440
  13.0 5.0 %collective-permute-start.8 = (bf16[224,128]{1,0:T(8,128)(2,1)S(1)}, bf16[224,128]{1,0:T(8,128)(2,1)S(1)}, u32[]{:S(2)}, u32[]{:S(2)}) collective-permute-start(bf16[224,128]{1,0:T(8,128)(2,1)S(1)} %get-tuple-element.67), channel_id=1, source_target_pairs={{0,2},{1,3},{2,0},{3,1},{4,8},{5,9},{6,10},{7,11},{8,4},{9,5},{10,... | collective-permute-start | bytes 172040 | tf_op jit(solution)/shard_map/ppermute | solution.py:466
  15.4 6.6 %collective-permute-start.6 = (bf16[4,96,256]{2,1,0:T(8,128)(2,1)S(1)}, bf16[4,96,256]{2,1,0:T(8,128)(2,1)S(1)}, u32[]{:S(2)}, u32[]{:S(2)}) collective-permute-start(bf16[4,96,256]{2,1,0:T(8,128)(2,1)S(1)} %constant_dynamic-update-slice_fusion.2.first_ref), channel_id=1, source_target_pairs={{0,2},{1,3},{2,0},{3,1},{4,6},{5,7},{6,4},{7,5},{8,10},{9,11},{10,... | collective-permute-start | bytes 589832 | tf_op jit(solution)/shard_map/ppermute | solution.py:440
  15.9 6.0 %collective-permute-start.5 = (bf16[4,96,256]{2,1,0:T(8,128)(2,1)S(1)}, bf16[4,96,256]{2,1,0:T(8,128)(2,1)S(1)}, u32[]{:S(2)}, u32[]{:S(2)}) collective-permute-start(bf16[4,96,256]{2,1,0:T(8,128)(2,1)S(1)} %constant_dynamic-update-slice_fusion.2.first_ref), channel_id=1, source_target_pairs={{0,4},{1,5},{2,6},{3,7},{4,0},{5,1},{6,2},{7,3},{8,12},{9,13},{10,... | collective-permute-start | bytes 589832 | tf_op jit(solution)/shard_map/ppermute | solution.py:450
  16.6 5.3 %collective-permute-start.7 = (f32[64,64]{1,0:T(8,128)S(1)}, f32[64,64]{1,0:T(8,128)S(1)}, u32[]{:S(2)}, u32[]{:S(2)}) collective-permute-start(f32[64,64]{1,0:T(8,128)S(1)} %add.19), channel_id=1, source_target_pairs={{0,4},{4,0},{8,12},{12,8},{16,20},{20,16},{24,28},{28,24},{1,5},{5... | collective-permute-start | bytes 49160 | tf_op jit(solution)/shard_map/ppermute | solution.py:440
  22.0 6.4 %collective-permute-start.9 = (bf16[5,96,256]{2,1,0:T(8,128)(2,1)S(1)}, bf16[5,96,256]{2,1,0:T(8,128)(2,1)S(1)}, u32[]{:S(2)}, u32[]{:S(2)}) collective-permute-start(bf16[5,96,256]{2,1,0:T(8,128)(2,1)S(1)} %pad_maximum_fusion), channel_id=1, source_target_pairs={{0,2},{1,3},{2,0},{3,1},{4,6},{5,7},{6,4},{7,5},{8,10},{9,11},{10,... | collective-permute-start | bytes 737288 | tf_op jit(solution)/shard_map/ppermute | solution.py:440
  23.6 4.8 %collective-permute-start.10 = (f32[64,64]{1,0:T(8,128)S(1)}, f32[64,64]{1,0:T(8,128)S(1)}, u32[]{:S(2)}, u32[]{:S(2)}) collective-permute-start(f32[64,64]{1,0:T(8,128)S(1)} %add.21), channel_id=1, source_target_pairs={{0,16},{4,20},{8,24},{12,28},{16,0},{20,4},{24,8},{28,12},{1,17},{... | collective-permute-start | bytes 49160 | tf_op jit(solution)/shard_map/ppermute | solution.py:440
  30.0 2.6 %collective-permute-start.11 = (f32[512,256]{1,0:T(8,128)S(1)}, f32[512,256]{1,0:T(8,128)S(1)}, u32[]{:S(2)}, u32[]{:S(2)}) collective-permute-start(f32[512,256]{1,0:T(8,128)S(1)} %get-tuple-element.83.auto_a), channel_id=1, source_target_pairs={{0,1},{1,0},{2,3},{3,2},{4,5},{5,4},{6,7},{7,6},{8,9},{9,8},{10,11... | collective-permute-start | bytes 1572872 | tf_op jit(solution)/shard_map/ppermute | solution.py:440
  32.7 3.5 %collective-permute-start.12 = (f32[552,256]{1,0:T(8,128)S(1)}, f32[552,256]{1,0:T(8,128)S(1)}, u32[]{:S(2)}, u32[]{:S(2)}) collective-permute-start(f32[552,256]{1,0:T(8,128)S(1)} %shard_map.44.refs_0_), channel_id=1, source_target_pairs={{0,1},{1,0},{2,3},{3,2},{4,5},{5,4},{6,7},{7,6},{8,9},{9,8},{10,11... | collective-permute-start | bytes 1695752 | tf_op jit(solution)/shard_map/ppermute | solution.py:440
  37.4 4.0 %collective-permute-start.14 = (f32[64,64]{1,0:T(8,128)S(1)}, f32[64,64]{1,0:T(8,128)S(1)}, u32[]{:S(2)}, u32[]{:S(2)}) collective-permute-start(f32[64,64]{1,0:T(8,128)S(1)} %get-tuple-element.100), channel_id=1, source_target_pairs={{0,4},{4,0},{8,12},{12,8},{16,20},{20,16},{24,28},{28,24},{1,5},{5... | collective-permute-start | bytes 49160 | tf_op jit(solution)/shard_map/ppermute | solution.py:440
  41.4 5.7 %collective-permute-start.16 = (f32[64,64]{1,0:T(8,128)S(1)}, f32[64,64]{1,0:T(8,128)S(1)}, u32[]{:S(2)}, u32[]{:S(2)}) collective-permute-start(f32[64,64]{1,0:T(8,128)S(1)} %add.23.refs_3_), channel_id=1, source_target_pairs={{0,24},{4,28},{8,16},{12,20},{16,8},{20,12},{24,0},{28,4},{1,25},{... | collective-permute-start | bytes 49160 | tf_op jit(solution)/shard_map/ppermute | solution.py:440
  44.2 3.9 %collective-permute-start.15 = (f32[64,64]{1,0:T(8,128)S(1)}, f32[64,64]{1,0:T(8,128)S(1)}, u32[]{:S(2)}, u32[]{:S(2)}) collective-permute-start(f32[64,64]{1,0:T(8,128)S(1)} %add.23.refs_3_), channel_id=1, source_target_pairs={{0,8},{1,17},{2,10},{3,19},{4,12},{5,21},{6,14},{7,23},{8,0},{9,25... | collective-permute-start | bytes 49160 | tf_op jit(solution)/shard_map/ppermute | solution.py:450
  44.2 1.2 %collective-permute-start.13 = (f32[8,256]{1,0:T(8,128)S(1)}, f32[8,256]{1,0:T(8,128)S(1)}, u32[]{:S(2)}, u32[]{:S(2)}) collective-permute-start(f32[8,256]{1,0:T(8,128)S(1)} %get-tuple-element.99.refs_1_), channel_id=1, source_target_pairs={{0,1},{1,0},{2,3},{3,2},{4,5},{5,4},{6,7},{7,6},{8,9},{9,8},{10,11... | collective-permute-start | bytes 24584 | tf_op jit(solution)/shard_map/ppermute | solution.py:440
  48.1 1.2 %collective-permute-start.17 = (f32[64,64]{1,0:T(8,128)S(1)}, f32[64,64]{1,0:T(8,128)S(1)}, u32[]{:S(2)}, u32[]{:S(2)}) collective-permute-start(f32[64,64]{1,0:T(8,128)S(1)} %collective-permute-done.15.refs_4_), channel_id=1, source_target_pairs={{0,1},{1,0},{2,3},{3,2},{4,5},{5,4},{6,7},{7,6},{8,9},{9,8},{10,11... | collective-permute-start | bytes 49160 | tf_op jit(solution)/shard_map/ppermute | solution.py:440
  50.5 4.0 %collective-permute-start.19 = (f32[64,64]{1,0:T(8,128)S(1)}, f32[64,64]{1,0:T(8,128)S(1)}, u32[]{:S(2)}, u32[]{:S(2)}) collective-permute-start(f32[64,64]{1,0:T(8,128)S(1)} %get-tuple-element.109), channel_id=1, source_target_pairs={{0,4},{4,0},{8,12},{12,8},{16,20},{20,16},{24,28},{28,24},{1,5},{5... | collective-permute-start | bytes 49160 | tf_op jit(solution)/shard_map/ppermute | solution.py:440
  54.5 5.8 %collective-permute-start.21 = (f32[64,64]{1,0:T(8,128)S(1)}, f32[64,64]{1,0:T(8,128)S(1)}, u32[]{:S(2)}, u32[]{:S(2)}) collective-permute-start(f32[64,64]{1,0:T(8,128)S(1)} %add.24.refs_3_), channel_id=1, source_target_pairs={{0,24},{4,28},{8,16},{12,20},{16,8},{20,12},{24,0},{28,4},{1,25},{... | collective-permute-start | bytes 49160 | tf_op jit(solution)/shard_map/ppermute | solution.py:440
  56.3 4.3 %collective-permute-start.20 = (f32[64,64]{1,0:T(8,128)S(1)}, f32[64,64]{1,0:T(8,128)S(1)}, u32[]{:S(2)}, u32[]{:S(2)}) collective-permute-start(f32[64,64]{1,0:T(8,128)S(1)} %add.24.refs_3_), channel_id=1, source_target_pairs={{0,8},{1,17},{2,10},{3,19},{4,12},{5,21},{6,14},{7,23},{8,0},{9,25... | collective-permute-start | bytes 49160 | tf_op jit(solution)/shard_map/ppermute | solution.py:450
  56.3 1.2 %collective-permute-start.18 = (f32[8,256]{1,0:T(8,128)S(1)}, f32[8,256]{1,0:T(8,128)S(1)}, u32[]{:S(2)}, u32[]{:S(2)}) collective-permute-start(f32[8,256]{1,0:T(8,128)S(1)} %get-tuple-element.108.refs_1_), channel_id=1, source_target_pairs={{0,1},{1,0},{2,3},{3,2},{4,5},{5,4},{6,7},{7,6},{8,9},{9,8},{10,11... | collective-permute-start | bytes 24584 | tf_op jit(solution)/shard_map/ppermute | solution.py:440
  60.6 1.2 %collective-permute-start.22 = (f32[64,64]{1,0:T(8,128)S(1)}, f32[64,64]{1,0:T(8,128)S(1)}, u32[]{:S(2)}, u32[]{:S(2)}) collective-permute-start(f32[64,64]{1,0:T(8,128)S(1)} %collective-permute-done.20.refs_4_), channel_id=1, source_target_pairs={{0,1},{1,0},{2,3},{3,2},{4,5},{5,4},{6,7},{7,6},{8,9},{9,8},{10,11... | collective-permute-start | bytes 49160 | tf_op jit(solution)/shard_map/ppermute | solution.py:440
  (1 other events, 0.8 us)

commit v6 on v5

--- a/solution.py
+++ b/solution.py
@@ -650,9 +650,9 @@
     numers_now = (numer, numer_far)
     for sweep in range(ITERS):
         if sweep:
-            part, tail = conv_tail(every[:REACH + 3], bits_x)
+            part, tail = conv_tail(every[:REACH], bits_x)
             tails = (tail, swap(tail, "chan", 1))
-            den = conv(every[REACH + 3:], bits_x, part)
+            den = conv(every[REACH:], bits_x, part)
             grams = gram_rounds(gram, odd, (part,), (den, tails[1]))
         else:
             tails = ()

time: 63.7 us -> 63.3 us (level)
    pallas_call x2, Pallas kernels: 4.77 us -> 3.88 us  [conv_tail(): call(functools.partial(conv_tail_body, plan, shards, offsets), (field, re...]
    pallas_call x2, Pallas kernels: 2.24 us -> 3.13 us  [conv(): call(functools.partial(conv_body, plan, offsets), field, vmem(4))]
  transfers between devices with their start and end apart: 23 -> 23, of which waited for: 13 -> 12; matrix products, arithmetic and copies ran while one was open for 0% -> 0% of each run, Pallas kernels for 29% -> 29%
where the time goes in v6:
time: 63.3 us; the launch traced here: 63.1 us
  Pallas kernels  23.9 us (38%)
  starting transfers between devices  23.1 us (36%)
  waiting for transfers between devices  14.9 us (24%)
  local copies, waits for them, and re-layouts  0.87 us (1%)
    ppermute x17, starting transfers between devices, swap(): return lax.ppermute(x, axis, [(i, i ^ bit) for i in range(count)])  17.7 us
    ppermute x17, waiting for transfers between devices, swap(): return lax.ppermute(x, axis, [(i, i ^ bit) for i in range(count)])  13.8 us
    ppermute x5, starting transfers between devices, mixed(): return lax.ppermute(x, ('tm', 'chan'), pairs)  4.91 us
    pallas_call x2, Pallas kernels, conv_tail(): call(functools.partial(conv_tail_body, plan, shards, offsets), (field, re...  3.88 us
    pallas_call x2, Pallas kernels, autos(): call(functools.partial(auto_body, plan, moved), (sds((width, plan.tiles *...  3.17 us
    pallas_call x2, Pallas kernels, conv(): call(functools.partial(conv_body, plan, offsets), field, vmem(4))  3.13 us
    pallas_call x1, Pallas kernels, on_device(): call(functools.partial(first_conv_body, plan, every), (mats, mats, sds((r...  2.97 us
    pallas_call x2, Pallas kernels, on_device(): call(functools.partial(update_body, plan, scale, shards, counts), outs, v...  2.45 us
  transfers between devices with their start and end apart: 23, of which 12 were waited for; matrix products, arithmetic and copies ran while one was open for 0% of the time, Pallas kernels for 29%

profile of v6, /device:TPU:0, one launch (start us, length us, event | category | flops | bytes accessed | tf_op | source)
XLA Modules:
  0.0 63.1 jit_solution(2437227563435596092)
XLA Ops:
  0.0 3.0 %collective-permute-start.4 = (bf16[96,2048]{1,0:T(8,128)(2,1)}, bf16[96,2048]{1,0:T(8,128)(2,1)S(1)}, u32[]{:S(2)}, u32[]{:S(2)}) collective-permute-start(bf16[96,2048]{1,0:T(8,128)(2,1)} %data_any.1), channel_id=1, source_target_pairs={{0,2},{1,3},{2,0},{3,1},{4,6},{5,7},{6,4},{7,5},{8,10},{9,11},{10,... | collective-permute-start | bytes 1179656 | tf_op jit(solution)/shard_map/ppermute | solution.py:440
  3.0 1.6 %collective-permute-start = (bf16[1,96,256]{2,1,0:T(8,128)(2,1)}, bf16[1,96,256]{2,1,0:T(8,128)(2,1)S(1)}, u32[]{:S(2)}, u32[]{:S(2)}) collective-permute-start(bf16[1,96,256]{2,1,0:T(8,128)(2,1)} %bitcast.5), channel_id=1, source_target_pairs={{0,8},{1,9},{2,10},{3,11},{4,12},{5,13},{6,14},{7,15},{8,0},{9,1},... | collective-permute-start | bytes 147464 | tf_op jit(solution)/shard_map/ppermute | solution.py:450
  5.4 1.6 %shard_map.37 = (bf16[96,2048]{1,0:T(8,128)(2,1)S(1)}, bf16[1,96,256]{2,1,0:T(8,128)(2,1)S(1)}, f32[64,64]{1,0:T(8,128)S(1)}, bf16[224,128]{1,0:T(8,128)(2,1)S(1)}, bf16[224,128]{1,0:T(8,128)(2,1)S(1)}) custom-call(f32[64,2048]{1,0:T(8,128)} %load_ref.1, bf16[96,2048]{1,0:T(8,128)(2,1)} %data_any.1, bf16[96,256]{1,0:T(8,128)(2,1)S(1)} %copy-done.1), custom_call_target="tpu_custom_call" | custom-call | tf_op jit(solution)/shard_map/pallas_call | solution.py:516
  7.3 2.7 %collective-permute-start.1 = (bf16[2,96,256]{2,1,0:T(8,128)(2,1)S(1)}, bf16[2,96,256]{2,1,0:T(8,128)(2,1)S(1)}, u32[]{:S(2)}, u32[]{:S(2)}) collective-permute-start(bf16[2,96,256]{2,1,0:T(8,128)(2,1)S(1)} %get-tuple-element.117), channel_id=1, source_target_pairs={{0,16},{1,17},{2,18},{3,19},{4,20},{5,21},{6,22},{7,23},{8,24},{9,... | collective-permute-start | bytes 294920 | tf_op jit(solution)/shard_map/ppermute | solution.py:450
  9.9 1.5 %collective-permute-start.3 = (bf16[224,128]{1,0:T(8,128)(2,1)S(1)}, bf16[224,128]{1,0:T(8,128)(2,1)S(1)}, u32[]{:S(2)}, u32[]{:S(2)}) collective-permute-start(bf16[224,128]{1,0:T(8,128)(2,1)S(1)} %get-tuple-element.62), channel_id=1, source_target_pairs={{0,4},{4,0},{8,12},{12,8},{16,20},{20,16},{24,28},{28,24},{1,5},{5... | collective-permute-start | bytes 172040 | tf_op jit(solution)/shard_map/ppermute | solution.py:440
  11.4 1.6 %collective-permute-start.2 = (f32[64,64]{1,0:T(8,128)S(1)}, f32[64,64]{1,0:T(8,128)S(1)}, u32[]{:S(2)}, u32[]{:S(2)}) collective-permute-start(f32[64,64]{1,0:T(8,128)S(1)} %get-tuple-element.60), channel_id=1, source_target_pairs={{0,8},{4,12},{8,0},{12,4},{16,24},{20,28},{24,16},{28,20},{1,9},{5... | collective-permute-start | bytes 49160 | tf_op jit(solution)/shard_map/ppermute | solution.py:440
  13.5 1.8 %collective-permute-done.2 = f32[64,64]{1,0:T(8,128)S(1)} collective-permute-done((f32[64,64]{1,0:T(8,128)S(1)}, f32[64,64]{1,0:T(8,128)S(1)}, u32[]{:S(2)}, u32[]{:S(2)}) %collective-permute-start.2) | collective-permute-done | bytes 16416 | tf_op jit(solution)/shard_map/ppermute | solution.py:440
  19.1 2.9 %collective-permute-done.7 = f32[64,64]{1,0:T(8,128)S(1)} collective-permute-done((f32[64,64]{1,0:T(8,128)S(1)}, f32[64,64]{1,0:T(8,128)S(1)}, u32[]{:S(2)}, u32[]{:S(2)}) %collective-permute-start.7) | collective-permute-done | bytes 16416 | tf_op jit(solution)/shard_map/ppermute | solution.py:440
  22.0 1.6 %collective-permute-start.9 = (bf16[5,96,256]{2,1,0:T(8,128)(2,1)S(1)}, bf16[5,96,256]{2,1,0:T(8,128)(2,1)S(1)}, u32[]{:S(2)}, u32[]{:S(2)}) collective-permute-start(bf16[5,96,256]{2,1,0:T(8,128)(2,1)S(1)} %pad_maximum_fusion), channel_id=1, source_target_pairs={{0,2},{1,3},{2,0},{3,1},{4,6},{5,7},{6,4},{7,5},{8,10},{9,11},{10,... | collective-permute-start | bytes 737288 | tf_op jit(solution)/shard_map/ppermute | solution.py:440
  24.0 1.6 %shard_map.40 = (bf16[256,4608]{1,0:T(8,128)(2,1)S(1)}, f32[512,256]{1,0:T(8,128)S(1)}) custom-call(bf16[4,96,256]{2,1,0:T(8,128)(2,1)S(1)} %constant_dynamic-update-slice_fusion.2.first_ref, bf16[4,96,256]{2,1,0:T(8,128)(2,1)S(1)} %collective-permute-done.5.second_ref), custom_call_target="tpu_custom_call" | custom-call | tf_op jit(solution)/shard_map/pallas_call | solution.py:604
  25.6 1.5 %shard_map.41.before = f32[544,256]{1,0:T(8,128)S(1)} custom-call(bf16[256,4608]{1,0:T(8,128)(2,1)S(1)} %get-tuple-element.78.stk_ref.stk_a, bf16[672,512]{1,0:T(8,128)(2,1)S(1)} %shard_map.38.data_ref), custom_call_target="tpu_custom_call" | custom-call | tf_op jit(solution)/shard_map/pallas_call | solution.py:612
  28.4 1.6 %shard_map.42 = (bf16[256,4608]{1,0:T(8,128)(2,1)S(1)}, f32[512,256]{1,0:T(8,128)S(1)}) custom-call(bf16[4,96,256]{2,1,0:T(8,128)(2,1)S(1)} %collective-permute-done.6.first_ref, bf16[5,96,256]{2,1,0:T(8,128)(2,1)S(1)} %collective-permute-done.9.second_ref, f32[512,256]{1,0:T(8,128)S(1)} %get-tuple-element.81.refs_0_), custom_call_target="tpu_custom_call" | custom-call | tf_op jit(solution)/shard_map/pallas_call | solution.py:604
  30.5 2.1 %shard_map.44.refs_0_ = f32[552,256]{1,0:T(8,128)S(1)} custom-call(bf16[256,4608]{1,0:T(8,128)(2,1)S(1)} %get-tuple-element.78.stk_ref.stk_a, bf16[256,4608]{1,0:T(8,128)(2,1)S(1)} %get-tuple-element.84.stk_b, bf16[672,512]{1,0:T(8,128)(2,1)S(1)} %shard_map.43.data_ref, f32[544,256]{1,0:T(8,128)S(1)} %shard_map.41.before, ...), custom_call_target="tpu_custom_call" | custom-call | tf_op jit(solution)/shard_map/pallas_call | solution.py:617
  33.2 3.0 %shard_map.45 = (bf16[2304,256]{1,0:T(8,128)(2,1)S(1)}, bf16[2304,256]{1,0:T(8,128)(2,1)S(1)}, f32[544,256]{1,0:T(8,128)S(1)}) custom-call(f32[512,256]{1,0:T(8,128)S(1)} %get-tuple-element.83.auto_a, f32[512,256]{1,0:T(8,128)S(1)} %collective-permute-done.11.auto_b, bf16[800,256]{1,0:T(8,128)(2,1)S(1)} %get-tuple-element.71.bits_ref), custom_call_target="tpu_custom_call" | custom-call | tf_op jit(solution)/shard_map/pallas_call | solution.py:629
  38.7 1.9 %shard_map.47 = (f32[544,256]{1,0:T(8,128)S(1)}, f32[8,256]{1,0:T(8,128)S(1)}) custom-call(bf16[800,256]{1,0:T(8,128)(2,1)S(1)} %get-tuple-element.93.bits_ref, bf16[2304,256]{1,0:T(8,128)(2,1)S(1)} %get-tuple-element.95.high_ref, bf16[2304,256]{1,0:T(8,128)(2,1)S(1)} %get-tuple-element.96.low_ref, bf16[256,4608]{1,0:T(8,128)(2,1)S(1)} %get-tuple-element.78.stk_ref.stk_a, ...), custom_call_target="tpu_custom_call" | custom-call | tf_op jit(solution)/shard_map/pallas_call | solution.py:642
  41.4 2.3 %collective-permute-start.16 = (f32[64,64]{1,0:T(8,128)S(1)}, f32[64,64]{1,0:T(8,128)S(1)}, u32[]{:S(2)}, u32[]{:S(2)}) collective-permute-start(f32[64,64]{1,0:T(8,128)S(1)} %add.23.refs_3_), channel_id=1, source_target_pairs={{0,24},{4,28},{8,16},{12,20},{16,8},{20,12},{24,0},{28,4},{1,25},{... | collective-permute-start | bytes 49160 | tf_op jit(solution)/shard_map/ppermute | solution.py:440
  43.8 1.7 %shard_map.48.den_ref = f32[544,256]{1,0:T(8,128)S(1)} custom-call(bf16[800,256]{1,0:T(8,128)(2,1)S(1)} %get-tuple-element.93.bits_ref, bf16[2304,256]{1,0:T(8,128)(2,1)S(1)} %get-tuple-element.95.high_ref, bf16[2304,256]{1,0:T(8,128)(2,1)S(1)} %get-tuple-element.96.low_ref, f32[544,256]{1,0:T(8,128)S(1)} %get-tuple-element.97.refs_0_), custom_call_target="tpu_custom_call" | custom-call | tf_op jit(solution)/shard_map/pallas_call | solution.py:637
  45.4 1.8 %collective-permute-done.16.refs_6_ = f32[64,64]{1,0:T(8,128)S(1)} collective-permute-done((f32[64,64]{1,0:T(8,128)S(1)}, f32[64,64]{1,0:T(8,128)S(1)}, u32[]{:S(2)}, u32[]{:S(2)}) %collective-permute-start.16) | collective-permute-done | bytes 16416 | tf_op jit(solution)/shard_map/ppermute | solution.py:440
  50.2 1.8 %collective-permute-start.19 = (f32[64,64]{1,0:T(8,128)S(1)}, f32[64,64]{1,0:T(8,128)S(1)}, u32[]{:S(2)}, u32[]{:S(2)}) collective-permute-start(f32[64,64]{1,0:T(8,128)S(1)} %get-tuple-element.109), channel_id=1, source_target_pairs={{0,4},{4,0},{8,12},{12,8},{16,20},{20,16},{24,28},{28,24},{1,5},{5... | collective-permute-start | bytes 49160 | tf_op jit(solution)/shard_map/ppermute | solution.py:440
  52.0 1.9 %shard_map.50 = (f32[544,256]{1,0:T(8,128)S(1)}, f32[8,256]{1,0:T(8,128)S(1)}) custom-call(bf16[800,256]{1,0:T(8,128)(2,1)S(1)} %get-tuple-element.105.bits_ref, bf16[2304,256]{1,0:T(8,128)(2,1)S(1)} %get-tuple-element.95.high_ref, bf16[2304,256]{1,0:T(8,128)(2,1)S(1)} %get-tuple-element.96.low_ref, bf16[256,4608]{1,0:T(8,128)(2,1)S(1)} %get-tuple-element.78.stk_ref.stk_a, ...), custom_call_target="tpu_custom_call" | custom-call | tf_op jit(solution)/shard_map/pallas_call | solution.py:642
  54.2 1.7 %collective-permute-start.21 = (f32[64,64]{1,0:T(8,128)S(1)}, f32[64,64]{1,0:T(8,128)S(1)}, u32[]{:S(2)}, u32[]{:S(2)}) collective-permute-start(f32[64,64]{1,0:T(8,128)S(1)} %add.24.refs_3_), channel_id=1, source_target_pairs={{0,24},{4,28},{8,16},{12,20},{16,8},{20,12},{24,0},{28,4},{1,25},{... | collective-permute-start | bytes 49160 | tf_op jit(solution)/shard_map/ppermute | solution.py:440
  55.9 1.5 %shard_map.51.den_ref = f32[544,256]{1,0:T(8,128)S(1)} custom-call(bf16[800,256]{1,0:T(8,128)(2,1)S(1)} %get-tuple-element.105.bits_ref, bf16[2304,256]{1,0:T(8,128)(2,1)S(1)} %get-tuple-element.95.high_ref, bf16[2304,256]{1,0:T(8,128)(2,1)S(1)} %get-tuple-element.96.low_ref, f32[544,256]{1,0:T(8,128)S(1)} %get-tuple-element.107.refs_0_), custom_call_target="tpu_custom_call" | custom-call | tf_op jit(solution)/shard_map/pallas_call | solution.py:637
  57.4 2.6 %collective-permute-done.21.refs_6_ = f32[64,64]{1,0:T(8,128)S(1)} collective-permute-done((f32[64,64]{1,0:T(8,128)S(1)}, f32[64,64]{1,0:T(8,128)S(1)}, u32[]{:S(2)}, u32[]{:S(2)}) %collective-permute-start.21) | collective-permute-done | bytes 16416 | tf_op jit(solution)/shard_map/ppermute | solution.py:440
  61.4 1.7 %shard_map.52 = f32[64,2048]{1,0:T(8,128)} custom-call(f32[544,256]{1,0:T(8,128)S(1)} %get-tuple-element.104.x_ref, bf16[800,256]{1,0:T(8,128)(2,1)S(1)} %get-tuple-element.105.bits_ref, bf16[544,256]{1,0:T(8,128)(2,1)S(1)} %get-tuple-element.106.low_ref, f32[544,256]{1,0:T(8,128)S(1)} %shard_map.51.den_ref, f32[544,256]{1,0:T(8,128)S(1)} %get-tuple-element.98.refs_0_, ...), custom_call_target="tpu_custom_call" | custom-call | tf_op jit(solution)/shard_map/pallas_call | solution.py:662
  (56 shorter events, 16.0 us)
Async XLA Ops:
  0.0 18.0 %copy-start = (f32[64,2048]{1,0:T(8,128)S(1)}, f32[64,2048]{1,0:T(8,128)}, u32[]{:S(2)}) copy-start(f32[64,2048]{1,0:T(8,128)} %load_ref.1) | copy-start | bytes 1572868
  0.0 15.3 %collective-permute-start.4 = (bf16[96,2048]{1,0:T(8,128)(2,1)}, bf16[96,2048]{1,0:T(8,128)(2,1)S(1)}, u32[]{:S(2)}, u32[]{:S(2)}) collective-permute-start(bf16[96,2048]{1,0:T(8,128)(2,1)} %data_any.1), channel_id=1, source_target_pairs={{0,2},{1,3},{2,0},{3,1},{4,6},{5,7},{6,4},{7,5},{8,10},{9,11},{10,... | collective-permute-start | bytes 1179656 | tf_op jit(solution)/shard_map/ppermute | solution.py:440
  3.0 4.3 %collective-permute-start = (bf16[1,96,256]{2,1,0:T(8,128)(2,1)}, bf16[1,96,256]{2,1,0:T(8,128)(2,1)S(1)}, u32[]{:S(2)}, u32[]{:S(2)}) collective-permute-start(bf16[1,96,256]{2,1,0:T(8,128)(2,1)} %bitcast.5), channel_id=1, source_target_pairs={{0,8},{1,9},{2,10},{3,11},{4,12},{5,13},{6,14},{7,15},{8,0},{9,1},... | collective-permute-start | bytes 147464 | tf_op jit(solution)/shard_map/ppermute | solution.py:450
  7.3 8.1 %collective-permute-start.1 = (bf16[2,96,256]{2,1,0:T(8,128)(2,1)S(1)}, bf16[2,96,256]{2,1,0:T(8,128)(2,1)S(1)}, u32[]{:S(2)}, u32[]{:S(2)}) collective-permute-start(bf16[2,96,256]{2,1,0:T(8,128)(2,1)S(1)} %get-tuple-element.117), channel_id=1, source_target_pairs={{0,16},{1,17},{2,18},{3,19},{4,20},{5,21},{6,22},{7,23},{8,24},{9,... | collective-permute-start | bytes 294920 | tf_op jit(solution)/shard_map/ppermute | solution.py:450
  9.9 5.4 %collective-permute-start.3 = (bf16[224,128]{1,0:T(8,128)(2,1)S(1)}, bf16[224,128]{1,0:T(8,128)(2,1)S(1)}, u32[]{:S(2)}, u32[]{:S(2)}) collective-permute-start(bf16[224,128]{1,0:T(8,128)(2,1)S(1)} %get-tuple-element.62), channel_id=1, source_target_pairs={{0,4},{4,0},{8,12},{12,8},{16,20},{20,16},{24,28},{28,24},{1,5},{5... | collective-permute-start | bytes 172040 | tf_op jit(solution)/shard_map/ppermute | solution.py:440
  11.4 3.9 %collective-permute-start.2 = (f32[64,64]{1,0:T(8,128)S(1)}, f32[64,64]{1,0:T(8,128)S(1)}, u32[]{:S(2)}, u32[]{:S(2)}) collective-permute-start(f32[64,64]{1,0:T(8,128)S(1)} %get-tuple-element.60), channel_id=1, source_target_pairs={{0,8},{4,12},{8,0},{12,4},{16,24},{20,28},{24,16},{28,20},{1,9},{5... | collective-permute-start | bytes 49160 | tf_op jit(solution)/shard_map/ppermute | solution.py:440
  13.0 5.0 %collective-permute-start.8 = (bf16[224,128]{1,0:T(8,128)(2,1)S(1)}, bf16[224,128]{1,0:T(8,128)(2,1)S(1)}, u32[]{:S(2)}, u32[]{:S(2)}) collective-permute-start(bf16[224,128]{1,0:T(8,128)(2,1)S(1)} %get-tuple-element.67), channel_id=1, source_target_pairs={{0,2},{1,3},{2,0},{3,1},{4,8},{5,9},{6,10},{7,11},{8,4},{9,5},{10,... | collective-permute-start | bytes 172040 | tf_op jit(solution)/shard_map/ppermute | solution.py:466
  15.4 6.6 %collective-permute-start.6 = (bf16[4,96,256]{2,1,0:T(8,128)(2,1)S(1)}, bf16[4,96,256]{2,1,0:T(8,128)(2,1)S(1)}, u32[]{:S(2)}, u32[]{:S(2)}) collective-permute-start(bf16[4,96,256]{2,1,0:T(8,128)(2,1)S(1)} %constant_dynamic-update-slice_fusion.2.first_ref), channel_id=1, source_target_pairs={{0,2},{1,3},{2,0},{3,1},{4,6},{5,7},{6,4},{7,5},{8,10},{9,11},{10,... | collective-permute-start | bytes 589832 | tf_op jit(solution)/shard_map/ppermute | solution.py:440
  15.9 6.0 %collective-permute-start.5 = (bf16[4,96,256]{2,1,0:T(8,128)(2,1)S(1)}, bf16[4,96,256]{2,1,0:T(8,128)(2,1)S(1)}, u32[]{:S(2)}, u32[]{:S(2)}) collective-permute-start(bf16[4,96,256]{2,1,0:T(8,128)(2,1)S(1)} %constant_dynamic-update-slice_fusion.2.first_ref), channel_id=1, source_target_pairs={{0,4},{1,5},{2,6},{3,7},{4,0},{5,1},{6,2},{7,3},{8,12},{9,13},{10,... | collective-permute-start | bytes 589832 | tf_op jit(solution)/shard_map/ppermute | solution.py:450
  16.6 5.3 %collective-permute-start.7 = (f32[64,64]{1,0:T(8,128)S(1)}, f32[64,64]{1,0:T(8,128)S(1)}, u32[]{:S(2)}, u32[]{:S(2)}) collective-permute-start(f32[64,64]{1,0:T(8,128)S(1)} %add.19), channel_id=1, source_target_pairs={{0,4},{4,0},{8,12},{12,8},{16,20},{20,16},{24,28},{28,24},{1,5},{5... | collective-permute-start | bytes 49160 | tf_op jit(solution)/shard_map/ppermute | solution.py:440
  22.0 6.4 %collective-permute-start.9 = (bf16[5,96,256]{2,1,0:T(8,128)(2,1)S(1)}, bf16[5,96,256]{2,1,0:T(8,128)(2,1)S(1)}, u32[]{:S(2)}, u32[]{:S(2)}) collective-permute-start(bf16[5,96,256]{2,1,0:T(8,128)(2,1)S(1)} %pad_maximum_fusion), channel_id=1, source_target_pairs={{0,2},{1,3},{2,0},{3,1},{4,6},{5,7},{6,4},{7,5},{8,10},{9,11},{10,... | collective-permute-start | bytes 737288 | tf_op jit(solution)/shard_map/ppermute | solution.py:440
  23.6 4.8 %collective-permute-start.10 = (f32[64,64]{1,0:T(8,128)S(1)}, f32[64,64]{1,0:T(8,128)S(1)}, u32[]{:S(2)}, u32[]{:S(2)}) collective-permute-start(f32[64,64]{1,0:T(8,128)S(1)} %add.21), channel_id=1, source_target_pairs={{0,16},{4,20},{8,24},{12,28},{16,0},{20,4},{24,8},{28,12},{1,17},{... | collective-permute-start | bytes 49160 | tf_op jit(solution)/shard_map/ppermute | solution.py:440
  30.0 2.6 %collective-permute-start.11 = (f32[512,256]{1,0:T(8,128)S(1)}, f32[512,256]{1,0:T(8,128)S(1)}, u32[]{:S(2)}, u32[]{:S(2)}) collective-permute-start(f32[512,256]{1,0:T(8,128)S(1)} %get-tuple-element.83.auto_a), channel_id=1, source_target_pairs={{0,1},{1,0},{2,3},{3,2},{4,5},{5,4},{6,7},{7,6},{8,9},{9,8},{10,11... | collective-permute-start | bytes 1572872 | tf_op jit(solution)/shard_map/ppermute | solution.py:440
  32.7 3.5 %collective-permute-start.12 = (f32[552,256]{1,0:T(8,128)S(1)}, f32[552,256]{1,0:T(8,128)S(1)}, u32[]{:S(2)}, u32[]{:S(2)}) collective-permute-start(f32[552,256]{1,0:T(8,128)S(1)} %shard_map.44.refs_0_), channel_id=1, source_target_pairs={{0,1},{1,0},{2,3},{3,2},{4,5},{5,4},{6,7},{7,6},{8,9},{9,8},{10,11... | collective-permute-start | bytes 1695752 | tf_op jit(solution)/shard_map/ppermute | solution.py:440
  37.4 4.0 %collective-permute-start.14 = (f32[64,64]{1,0:T(8,128)S(1)}, f32[64,64]{1,0:T(8,128)S(1)}, u32[]{:S(2)}, u32[]{:S(2)}) collective-permute-start(f32[64,64]{1,0:T(8,128)S(1)} %get-tuple-element.100), channel_id=1, source_target_pairs={{0,4},{4,0},{8,12},{12,8},{16,20},{20,16},{24,28},{28,24},{1,5},{5... | collective-permute-start | bytes 49160 | tf_op jit(solution)/shard_map/ppermute | solution.py:440
  41.4 5.8 %collective-permute-start.16 = (f32[64,64]{1,0:T(8,128)S(1)}, f32[64,64]{1,0:T(8,128)S(1)}, u32[]{:S(2)}, u32[]{:S(2)}) collective-permute-start(f32[64,64]{1,0:T(8,128)S(1)} %add.23.refs_3_), channel_id=1, source_target_pairs={{0,24},{4,28},{8,16},{12,20},{16,8},{20,12},{24,0},{28,4},{1,25},{... | collective-permute-start | bytes 49160 | tf_op jit(solution)/shard_map/ppermute | solution.py:440
  43.8 4.1 %collective-permute-start.15 = (f32[64,64]{1,0:T(8,128)S(1)}, f32[64,64]{1,0:T(8,128)S(1)}, u32[]{:S(2)}, u32[]{:S(2)}) collective-permute-start(f32[64,64]{1,0:T(8,128)S(1)} %add.23.refs_3_), channel_id=1, source_target_pairs={{0,8},{1,17},{2,10},{3,19},{4,12},{5,21},{6,14},{7,23},{8,0},{9,25... | collective-permute-start | bytes 49160 | tf_op jit(solution)/shard_map/ppermute | solution.py:450
  43.8 1.7 %collective-permute-start.13 = (f32[8,256]{1,0:T(8,128)S(1)}, f32[8,256]{1,0:T(8,128)S(1)}, u32[]{:S(2)}, u32[]{:S(2)}) collective-permute-start(f32[8,256]{1,0:T(8,128)S(1)} %get-tuple-element.99.refs_1_), channel_id=1, source_target_pairs={{0,1},{1,0},{2,3},{3,2},{4,5},{5,4},{6,7},{7,6},{8,9},{9,8},{10,11... | collective-permute-start | bytes 24584 | tf_op jit(solution)/shard_map/ppermute | solution.py:440
  47.8 1.2 %collective-permute-start.17 = (f32[64,64]{1,0:T(8,128)S(1)}, f32[64,64]{1,0:T(8,128)S(1)}, u32[]{:S(2)}, u32[]{:S(2)}) collective-permute-start(f32[64,64]{1,0:T(8,128)S(1)} %collective-permute-done.15.refs_4_), channel_id=1, source_target_pairs={{0,1},{1,0},{2,3},{3,2},{4,5},{5,4},{6,7},{7,6},{8,9},{9,8},{10,11... | collective-permute-start | bytes 49160 | tf_op jit(solution)/shard_map/ppermute | solution.py:440
  50.2 4.0 %collective-permute-start.19 = (f32[64,64]{1,0:T(8,128)S(1)}, f32[64,64]{1,0:T(8,128)S(1)}, u32[]{:S(2)}, u32[]{:S(2)}) collective-permute-start(f32[64,64]{1,0:T(8,128)S(1)} %get-tuple-element.109), channel_id=1, source_target_pairs={{0,4},{4,0},{8,12},{12,8},{16,20},{20,16},{24,28},{28,24},{1,5},{5... | collective-permute-start | bytes 49160 | tf_op jit(solution)/shard_map/ppermute | solution.py:440
  54.2 5.8 %collective-permute-start.21 = (f32[64,64]{1,0:T(8,128)S(1)}, f32[64,64]{1,0:T(8,128)S(1)}, u32[]{:S(2)}, u32[]{:S(2)}) collective-permute-start(f32[64,64]{1,0:T(8,128)S(1)} %add.24.refs_3_), channel_id=1, source_target_pairs={{0,24},{4,28},{8,16},{12,20},{16,8},{20,12},{24,0},{28,4},{1,25},{... | collective-permute-start | bytes 49160 | tf_op jit(solution)/shard_map/ppermute | solution.py:440
  55.9 4.3 %collective-permute-start.20 = (f32[64,64]{1,0:T(8,128)S(1)}, f32[64,64]{1,0:T(8,128)S(1)}, u32[]{:S(2)}, u32[]{:S(2)}) collective-permute-start(f32[64,64]{1,0:T(8,128)S(1)} %add.24.refs_3_), channel_id=1, source_target_pairs={{0,8},{1,17},{2,10},{3,19},{4,12},{5,21},{6,14},{7,23},{8,0},{9,25... | collective-permute-start | bytes 49160 | tf_op jit(solution)/shard_map/ppermute | solution.py:450
  55.9 1.5 %collective-permute-start.18 = (f32[8,256]{1,0:T(8,128)S(1)}, f32[8,256]{1,0:T(8,128)S(1)}, u32[]{:S(2)}, u32[]{:S(2)}) collective-permute-start(f32[8,256]{1,0:T(8,128)S(1)} %get-tuple-element.108.refs_1_), channel_id=1, source_target_pairs={{0,1},{1,0},{2,3},{3,2},{4,5},{5,4},{6,7},{7,6},{8,9},{9,8},{10,11... | collective-permute-start | bytes 24584 | tf_op jit(solution)/shard_map/ppermute | solution.py:440
  60.2 1.2 %collective-permute-start.22 = (f32[64,64]{1,0:T(8,128)S(1)}, f32[64,64]{1,0:T(8,128)S(1)}, u32[]{:S(2)}, u32[]{:S(2)}) collective-permute-start(f32[64,64]{1,0:T(8,128)S(1)} %collective-permute-done.20.refs_4_), channel_id=1, source_target_pairs={{0,1},{1,0},{2,3},{3,2},{4,5},{5,4},{6,7},{7,6},{8,9},{9,8},{10,11... | collective-permute-start | bytes 49160 | tf_op jit(solution)/shard_map/ppermute | solution.py:440
  (1 other events, 0.8 us)

commit v7 on v6

--- a/solution.py
+++ b/solution.py
@@ -650,9 +650,9 @@
     numers_now = (numer, numer_far)
     for sweep in range(ITERS):
         if sweep:
-            part, tail = conv_tail(every[:REACH], bits_x)
+            part, tail = conv_tail(every[: REACH - 2], bits_x)
             tails = (tail, swap(tail, "chan", 1))
-            den = conv(every[REACH:], bits_x, part)
+            den = conv(every[REACH - 2 :], bits_x, part)
             grams = gram_rounds(gram, odd, (part,), (den, tails[1]))
         else:
             tails = ()

time: 63.3 us -> 63.2 us (level)
  no operation moved by 1% of the time
where the time goes in v7:
time: 63.2 us; the launch traced here: 63 us
  Pallas kernels  23.9 us (38%)
  starting transfers between devices  23.5 us (37%)
  waiting for transfers between devices  14.4 us (23%)
  local copies, waits for them, and re-layouts  0.87 us (1%)
    ppermute x17, starting transfers between devices, swap(): return lax.ppermute(x, axis, [(i, i ^ bit) for i in range(count)])  18.1 us
    ppermute x17, waiting for transfers between devices, swap(): return lax.ppermute(x, axis, [(i, i ^ bit) for i in range(count)])  13.4 us
    ppermute x5, starting transfers between devices, mixed(): return lax.ppermute(x, ('tm', 'chan'), pairs)  4.91 us
    pallas_call x2, Pallas kernels, conv(): call(functools.partial(conv_body, plan, offsets), field, vmem(4))  3.69 us
    pallas_call x2, Pallas kernels, conv_tail(): call(functools.partial(conv_tail_body, plan, shards, offsets), (field, re...  3.31 us
    pallas_call x2, Pallas kernels, autos(): call(functools.partial(auto_body, plan, moved), (sds((width, plan.tiles *...  3.17 us
    pallas_call x1, Pallas kernels, on_device(): call(functools.partial(first_conv_body, plan, every), (mats, mats, sds((r...  2.97 us
    pallas_call x2, Pallas kernels, on_device(): call(functools.partial(update_body, plan, scale, shards, counts), outs, v...  2.45 us
  transfers between devices with their start and end apart: 23, of which 12 were waited for; matrix products, arithmetic and copies ran while one was open for 0% of the time, Pallas kernels for 29%

profile of v7, /device:TPU:0, one launch (start us, length us, event | category | flops | bytes accessed | tf_op | source)
XLA Modules:
  0.0 63.0 jit_solution(8005729331825003790)
XLA Ops:
  0.0 3.0 %collective-permute-start.4 = (bf16[96,2048]{1,0:T(8,128)(2,1)}, bf16[96,2048]{1,0:T(8,128)(2,1)S(1)}, u32[]{:S(2)}, u32[]{:S(2)}) collective-permute-start(bf16[96,2048]{1,0:T(8,128)(2,1)} %data_any.1), channel_id=1, source_target_pairs={{0,2},{1,3},{2,0},{3,1},{4,6},{5,7},{6,4},{7,5},{8,10},{9,11},{10,... | collective-permute-start | bytes 1179656 | tf_op jit(solution)/shard_map/ppermute | solution.py:440
  3.0 1.6 %collective-permute-start = (bf16[1,96,256]{2,1,0:T(8,128)(2,1)}, bf16[1,96,256]{2,1,0:T(8,128)(2,1)S(1)}, u32[]{:S(2)}, u32[]{:S(2)}) collective-permute-start(bf16[1,96,256]{2,1,0:T(8,128)(2,1)} %bitcast.5), channel_id=1, source_target_pairs={{0,8},{1,9},{2,10},{3,11},{4,12},{5,13},{6,14},{7,15},{8,0},{9,1},... | collective-permute-start | bytes 147464 | tf_op jit(solution)/shard_map/ppermute | solution.py:450
  5.4 1.6 %shard_map.37 = (bf16[96,2048]{1,0:T(8,128)(2,1)S(1)}, bf16[1,96,256]{2,1,0:T(8,128)(2,1)S(1)}, f32[64,64]{1,0:T(8,128)S(1)}, bf16[224,128]{1,0:T(8,128)(2,1)S(1)}, bf16[224,128]{1,0:T(8,128)(2,1)S(1)}) custom-call(f32[64,2048]{1,0:T(8,128)} %load_ref.1, bf16[96,2048]{1,0:T(8,128)(2,1)} %data_any.1, bf16[96,256]{1,0:T(8,128)(2,1)S(1)} %copy-done.1), custom_call_target="tpu_custom_call" | custom-call | tf_op jit(solution)/shard_map/pallas_call | solution.py:516
  7.3 2.7 %collective-permute-start.1 = (bf16[2,96,256]{2,1,0:T(8,128)(2,1)S(1)}, bf16[2,96,256]{2,1,0:T(8,128)(2,1)S(1)}, u32[]{:S(2)}, u32[]{:S(2)}) collective-permute-start(bf16[2,96,256]{2,1,0:T(8,128)(2,1)S(1)} %get-tuple-element.117), channel_id=1, source_target_pairs={{0,16},{1,17},{2,18},{3,19},{4,20},{5,21},{6,22},{7,23},{8,24},{9,... | collective-permute-start | bytes 294920 | tf_op jit(solution)/shard_map/ppermute | solution.py:450
  9.9 1.5 %collective-permute-start.3 = (bf16[224,128]{1,0:T(8,128)(2,1)S(1)}, bf16[224,128]{1,0:T(8,128)(2,1)S(1)}, u32[]{:S(2)}, u32[]{:S(2)}) collective-permute-start(bf16[224,128]{1,0:T(8,128)(2,1)S(1)} %get-tuple-element.62), channel_id=1, source_target_pairs={{0,4},{4,0},{8,12},{12,8},{16,20},{20,16},{24,28},{28,24},{1,5},{5... | collective-permute-start | bytes 172040 | tf_op jit(solution)/shard_map/ppermute | solution.py:440
  11.4 1.6 %collective-permute-start.2 = (f32[64,64]{1,0:T(8,128)S(1)}, f32[64,64]{1,0:T(8,128)S(1)}, u32[]{:S(2)}, u32[]{:S(2)}) collective-permute-start(f32[64,64]{1,0:T(8,128)S(1)} %get-tuple-element.60), channel_id=1, source_target_pairs={{0,8},{4,12},{8,0},{12,4},{16,24},{20,28},{24,16},{28,20},{1,9},{5... | collective-permute-start | bytes 49160 | tf_op jit(solution)/shard_map/ppermute | solution.py:440
  13.5 1.8 %collective-permute-done.2 = f32[64,64]{1,0:T(8,128)S(1)} collective-permute-done((f32[64,64]{1,0:T(8,128)S(1)}, f32[64,64]{1,0:T(8,128)S(1)}, u32[]{:S(2)}, u32[]{:S(2)}) %collective-permute-start.2) | collective-permute-done | bytes 16416 | tf_op jit(solution)/shard_map/ppermute | solution.py:440
  19.1 2.9 %collective-permute-done.7 = f32[64,64]{1,0:T(8,128)S(1)} collective-permute-done((f32[64,64]{1,0:T(8,128)S(1)}, f32[64,64]{1,0:T(8,128)S(1)}, u32[]{:S(2)}, u32[]{:S(2)}) %collective-permute-start.7) | collective-permute-done | bytes 16416 | tf_op jit(solution)/shard_map/ppermute | solution.py:440
  22.0 1.6 %collective-permute-start.9 = (bf16[5,96,256]{2,1,0:T(8,128)(2,1)S(1)}, bf16[5,96,256]{2,1,0:T(8,128)(2,1)S(1)}, u32[]{:S(2)}, u32[]{:S(2)}) collective-permute-start(bf16[5,96,256]{2,1,0:T(8,128)(2,1)S(1)} %pad_maximum_fusion), channel_id=1, source_target_pairs={{0,2},{1,3},{2,0},{3,1},{4,6},{5,7},{6,4},{7,5},{8,10},{9,11},{10,... | collective-permute-start | bytes 737288 | tf_op jit(solution)/shard_map/ppermute | solution.py:440
  24.0 1.6 %shard_map.40 = (bf16[256,4608]{1,0:T(8,128)(2,1)S(1)}, f32[512,256]{1,0:T(8,128)S(1)}) custom-call(bf16[4,96,256]{2,1,0:T(8,128)(2,1)S(1)} %constant_dynamic-update-slice_fusion.2.first_ref, bf16[4,96,256]{2,1,0:T(8,128)(2,1)S(1)} %collective-permute-done.5.second_ref), custom_call_target="tpu_custom_call" | custom-call | tf_op jit(solution)/shard_map/pallas_call | solution.py:604
  25.6 1.5 %shard_map.41.before = f32[544,256]{1,0:T(8,128)S(1)} custom-call(bf16[256,4608]{1,0:T(8,128)(2,1)S(1)} %get-tuple-element.78.stk_ref.stk_a, bf16[672,512]{1,0:T(8,128)(2,1)S(1)} %shard_map.38.data_ref), custom_call_target="tpu_custom_call" | custom-call | tf_op jit(solution)/shard_map/pallas_call | solution.py:612
  28.4 1.6 %shard_map.42 = (bf16[256,4608]{1,0:T(8,128)(2,1)S(1)}, f32[512,256]{1,0:T(8,128)S(1)}) custom-call(bf16[4,96,256]{2,1,0:T(8,128)(2,1)S(1)} %collective-permute-done.6.first_ref, bf16[5,96,256]{2,1,0:T(8,128)(2,1)S(1)} %collective-permute-done.9.second_ref, f32[512,256]{1,0:T(8,128)S(1)} %get-tuple-element.81.refs_0_), custom_call_target="tpu_custom_call" | custom-call | tf_op jit(solution)/shard_map/pallas_call | solution.py:604
  30.5 2.1 %shard_map.44.refs_0_ = f32[552,256]{1,0:T(8,128)S(1)} custom-call(bf16[256,4608]{1,0:T(8,128)(2,1)S(1)} %get-tuple-element.78.stk_ref.stk_a, bf16[256,4608]{1,0:T(8,128)(2,1)S(1)} %get-tuple-element.84.stk_b, bf16[672,512]{1,0:T(8,128)(2,1)S(1)} %shard_map.43.data_ref, f32[544,256]{1,0:T(8,128)S(1)} %shard_map.41.before, ...), custom_call_target="tpu_custom_call" | custom-call | tf_op jit(solution)/shard_map/pallas_call | solution.py:617
  33.2 3.0 %shard_map.45 = (bf16[2304,256]{1,0:T(8,128)(2,1)S(1)}, bf16[2304,256]{1,0:T(8,128)(2,1)S(1)}, f32[544,256]{1,0:T(8,128)S(1)}) custom-call(f32[512,256]{1,0:T(8,128)S(1)} %get-tuple-element.83.auto_a, f32[512,256]{1,0:T(8,128)S(1)} %collective-permute-done.11.auto_b, bf16[800,256]{1,0:T(8,128)(2,1)S(1)} %get-tuple-element.71.bits_ref), custom_call_target="tpu_custom_call" | custom-call | tf_op jit(solution)/shard_map/pallas_call | solution.py:629
  38.7 1.6 %shard_map.47 = (f32[544,256]{1,0:T(8,128)S(1)}, f32[8,256]{1,0:T(8,128)S(1)}) custom-call(bf16[800,256]{1,0:T(8,128)(2,1)S(1)} %get-tuple-element.93.bits_ref, bf16[2304,256]{1,0:T(8,128)(2,1)S(1)} %get-tuple-element.95.high_ref, bf16[2304,256]{1,0:T(8,128)(2,1)S(1)} %get-tuple-element.96.low_ref, bf16[256,4608]{1,0:T(8,128)(2,1)S(1)} %get-tuple-element.78.stk_ref.stk_a, ...), custom_call_target="tpu_custom_call" | custom-call | tf_op jit(solution)/shard_map/pallas_call | solution.py:642
  41.4 2.3 %collective-permute-start.16 = (f32[64,64]{1,0:T(8,128)S(1)}, f32[64,64]{1,0:T(8,128)S(1)}, u32[]{:S(2)}, u32[]{:S(2)}) collective-permute-start(f32[64,64]{1,0:T(8,128)S(1)} %add.23.refs_3_), channel_id=1, source_target_pairs={{0,24},{4,28},{8,16},{12,20},{16,8},{20,12},{24,0},{28,4},{1,25},{... | collective-permute-start | bytes 49160 | tf_op jit(solution)/shard_map/ppermute | solution.py:440
  43.7 1.9 %shard_map.48.den_ref = f32[544,256]{1,0:T(8,128)S(1)} custom-call(bf16[800,256]{1,0:T(8,128)(2,1)S(1)} %get-tuple-element.93.bits_ref, bf16[2304,256]{1,0:T(8,128)(2,1)S(1)} %get-tuple-element.95.high_ref, bf16[2304,256]{1,0:T(8,128)(2,1)S(1)} %get-tuple-element.96.low_ref, f32[544,256]{1,0:T(8,128)S(1)} %get-tuple-element.97.refs_0_), custom_call_target="tpu_custom_call" | custom-call | tf_op jit(solution)/shard_map/pallas_call | solution.py:637
  45.7 1.5 %collective-permute-done.16.refs_6_ = f32[64,64]{1,0:T(8,128)S(1)} collective-permute-done((f32[64,64]{1,0:T(8,128)S(1)}, f32[64,64]{1,0:T(8,128)S(1)}, u32[]{:S(2)}, u32[]{:S(2)}) %collective-permute-start.16) | collective-permute-done | bytes 16416 | tf_op jit(solution)/shard_map/ppermute | solution.py:440
  50.0 2.0 %collective-permute-start.19 = (f32[64,64]{1,0:T(8,128)S(1)}, f32[64,64]{1,0:T(8,128)S(1)}, u32[]{:S(2)}, u32[]{:S(2)}) collective-permute-start(f32[64,64]{1,0:T(8,128)S(1)} %get-tuple-element.109), channel_id=1, source_target_pairs={{0,4},{4,0},{8,12},{12,8},{16,20},{20,16},{24,28},{28,24},{1,5},{5... | collective-permute-start | bytes 49160 | tf_op jit(solution)/shard_map/ppermute | solution.py:440
  52.0 1.7 %shard_map.50 = (f32[544,256]{1,0:T(8,128)S(1)}, f32[8,256]{1,0:T(8,128)S(1)}) custom-call(bf16[800,256]{1,0:T(8,128)(2,1)S(1)} %get-tuple-element.105.bits_ref, bf16[2304,256]{1,0:T(8,128)(2,1)S(1)} %get-tuple-element.95.high_ref, bf16[2304,256]{1,0:T(8,128)(2,1)S(1)} %get-tuple-element.96.low_ref, bf16[256,4608]{1,0:T(8,128)(2,1)S(1)} %get-tuple-element.78.stk_ref.stk_a, ...), custom_call_target="tpu_custom_call" | custom-call | tf_op jit(solution)/shard_map/pallas_call | solution.py:642
  54.0 1.9 %collective-permute-start.21 = (f32[64,64]{1,0:T(8,128)S(1)}, f32[64,64]{1,0:T(8,128)S(1)}, u32[]{:S(2)}, u32[]{:S(2)}) collective-permute-start(f32[64,64]{1,0:T(8,128)S(1)} %add.24.refs_3_), channel_id=1, source_target_pairs={{0,24},{4,28},{8,16},{12,20},{16,8},{20,12},{24,0},{28,4},{1,25},{... | collective-permute-start | bytes 49160 | tf_op jit(solution)/shard_map/ppermute | solution.py:440
  55.9 1.8 %shard_map.51.den_ref = f32[544,256]{1,0:T(8,128)S(1)} custom-call(bf16[800,256]{1,0:T(8,128)(2,1)S(1)} %get-tuple-element.105.bits_ref, bf16[2304,256]{1,0:T(8,128)(2,1)S(1)} %get-tuple-element.95.high_ref, bf16[2304,256]{1,0:T(8,128)(2,1)S(1)} %get-tuple-element.96.low_ref, f32[544,256]{1,0:T(8,128)S(1)} %get-tuple-element.107.refs_0_), custom_call_target="tpu_custom_call" | custom-call | tf_op jit(solution)/shard_map/pallas_call | solution.py:637
  57.7 2.0 %collective-permute-done.21.refs_6_ = f32[64,64]{1,0:T(8,128)S(1)} collective-permute-done((f32[64,64]{1,0:T(8,128)S(1)}, f32[64,64]{1,0:T(8,128)S(1)}, u32[]{:S(2)}, u32[]{:S(2)}) %collective-permute-start.21) | collective-permute-done | bytes 16416 | tf_op jit(solution)/shard_map/ppermute | solution.py:440
  61.3 1.7 %shard_map.52 = f32[64,2048]{1,0:T(8,128)} custom-call(f32[544,256]{1,0:T(8,128)S(1)} %get-tuple-element.104.x_ref, bf16[800,256]{1,0:T(8,128)(2,1)S(1)} %get-tuple-element.105.bits_ref, bf16[544,256]{1,0:T(8,128)(2,1)S(1)} %get-tuple-element.106.low_ref, f32[544,256]{1,0:T(8,128)S(1)} %shard_map.51.den_ref, f32[544,256]{1,0:T(8,128)S(1)} %get-tuple-element.98.refs_0_, ...), custom_call_target="tpu_custom_call" | custom-call | tf_op jit(solution)/shard_map/pallas_call | solution.py:662
  (56 shorter events, 16.4 us)
Async XLA Ops:
  0.0 18.0 %copy-start = (f32[64,2048]{1,0:T(8,128)S(1)}, f32[64,2048]{1,0:T(8,128)}, u32[]{:S(2)}) copy-start(f32[64,2048]{1,0:T(8,128)} %load_ref.1) | copy-start | bytes 1572868
  0.0 15.3 %collective-permute-start.4 = (bf16[96,2048]{1,0:T(8,128)(2,1)}, bf16[96,2048]{1,0:T(8,128)(2,1)S(1)}, u32[]{:S(2)}, u32[]{:S(2)}) collective-permute-start(bf16[96,2048]{1,0:T(8,128)(2,1)} %data_any.1), channel_id=1, source_target_pairs={{0,2},{1,3},{2,0},{3,1},{4,6},{5,7},{6,4},{7,5},{8,10},{9,11},{10,... | collective-permute-start | bytes 1179656 | tf_op jit(solution)/shard_map/ppermute | solution.py:440
  3.0 4.3 %collective-permute-start = (bf16[1,96,256]{2,1,0:T(8,128)(2,1)}, bf16[1,96,256]{2,1,0:T(8,128)(2,1)S(1)}, u32[]{:S(2)}, u32[]{:S(2)}) collective-permute-start(bf16[1,96,256]{2,1,0:T(8,128)(2,1)} %bitcast.5), channel_id=1, source_target_pairs={{0,8},{1,9},{2,10},{3,11},{4,12},{5,13},{6,14},{7,15},{8,0},{9,1},... | collective-permute-start | bytes 147464 | tf_op jit(solution)/shard_map/ppermute | solution.py:450
  7.3 8.1 %collective-permute-start.1 = (bf16[2,96,256]{2,1,0:T(8,128)(2,1)S(1)}, bf16[2,96,256]{2,1,0:T(8,128)(2,1)S(1)}, u32[]{:S(2)}, u32[]{:S(2)}) collective-permute-start(bf16[2,96,256]{2,1,0:T(8,128)(2,1)S(1)} %get-tuple-element.117), channel_id=1, source_target_pairs={{0,16},{1,17},{2,18},{3,19},{4,20},{5,21},{6,22},{7,23},{8,24},{9,... | collective-permute-start | bytes 294920 | tf_op jit(solution)/shard_map/ppermute | solution.py:450
  9.9 5.4 %collective-permute-start.3 = (bf16[224,128]{1,0:T(8,128)(2,1)S(1)}, bf16[224,128]{1,0:T(8,128)(2,1)S(1)}, u32[]{:S(2)}, u32[]{:S(2)}) collective-permute-start(bf16[224,128]{1,0:T(8,128)(2,1)S(1)} %get-tuple-element.62), channel_id=1, source_target_pairs={{0,4},{4,0},{8,12},{12,8},{16,20},{20,16},{24,28},{28,24},{1,5},{5... | collective-permute-start | bytes 172040 | tf_op jit(solution)/shard_map/ppermute | solution.py:440
  11.4 3.9 %collective-permute-start.2 = (f32[64,64]{1,0:T(8,128)S(1)}, f32[64,64]{1,0:T(8,128)S(1)}, u32[]{:S(2)}, u32[]{:S(2)}) collective-permute-start(f32[64,64]{1,0:T(8,128)S(1)} %get-tuple-element.60), channel_id=1, source_target_pairs={{0,8},{4,12},{8,0},{12,4},{16,24},{20,28},{24,16},{28,20},{1,9},{5... | collective-permute-start | bytes 49160 | tf_op jit(solution)/shard_map/ppermute | solution.py:440
  13.0 5.0 %collective-permute-start.8 = (bf16[224,128]{1,0:T(8,128)(2,1)S(1)}, bf16[224,128]{1,0:T(8,128)(2,1)S(1)}, u32[]{:S(2)}, u32[]{:S(2)}) collective-permute-start(bf16[224,128]{1,0:T(8,128)(2,1)S(1)} %get-tuple-element.67), channel_id=1, source_target_pairs={{0,2},{1,3},{2,0},{3,1},{4,8},{5,9},{6,10},{7,11},{8,4},{9,5},{10,... | collective-permute-start | bytes 172040 | tf_op jit(solution)/shard_map/ppermute | solution.py:466
  15.4 6.6 %collective-permute-start.6 = (bf16[4,96,256]{2,1,0:T(8,128)(2,1)S(1)}, bf16[4,96,256]{2,1,0:T(8,128)(2,1)S(1)}, u32[]{:S(2)}, u32[]{:S(2)}) collective-permute-start(bf16[4,96,256]{2,1,0:T(8,128)(2,1)S(1)} %constant_dynamic-update-slice_fusion.2.first_ref), channel_id=1, source_target_pairs={{0,2},{1,3},{2,0},{3,1},{4,6},{5,7},{6,4},{7,5},{8,10},{9,11},{10,... | collective-permute-start | bytes 589832 | tf_op jit(solution)/shard_map/ppermute | solution.py:440
  15.9 6.0 %collective-permute-start.5 = (bf16[4,96,256]{2,1,0:T(8,128)(2,1)S(1)}, bf16[4,96,256]{2,1,0:T(8,128)(2,1)S(1)}, u32[]{:S(2)}, u32[]{:S(2)}) collective-permute-start(bf16[4,96,256]{2,1,0:T(8,128)(2,1)S(1)} %constant_dynamic-update-slice_fusion.2.first_ref), channel_id=1, source_target_pairs={{0,4},{1,5},{2,6},{3,7},{4,0},{5,1},{6,2},{7,3},{8,12},{9,13},{10,... | collective-permute-start | bytes 589832 | tf_op jit(solution)/shard_map/ppermute | solution.py:450
  16.6 5.3 %collective-permute-start.7 = (f32[64,64]{1,0:T(8,128)S(1)}, f32[64,64]{1,0:T(8,128)S(1)}, u32[]{:S(2)}, u32[]{:S(2)}) collective-permute-start(f32[64,64]{1,0:T(8,128)S(1)} %add.19), channel_id=1, source_target_pairs={{0,4},{4,0},{8,12},{12,8},{16,20},{20,16},{24,28},{28,24},{1,5},{5... | collective-permute-start | bytes 49160 | tf_op jit(solution)/shard_map/ppermute | solution.py:440
  22.0 6.4 %collective-permute-start.9 = (bf16[5,96,256]{2,1,0:T(8,128)(2,1)S(1)}, bf16[5,96,256]{2,1,0:T(8,128)(2,1)S(1)}, u32[]{:S(2)}, u32[]{:S(2)}) collective-permute-start(bf16[5,96,256]{2,1,0:T(8,128)(2,1)S(1)} %pad_maximum_fusion), channel_id=1, source_target_pairs={{0,2},{1,3},{2,0},{3,1},{4,6},{5,7},{6,4},{7,5},{8,10},{9,11},{10,... | collective-permute-start | bytes 737288 | tf_op jit(solution)/shard_map/ppermute | solution.py:440
  23.6 4.8 %collective-permute-start.10 = (f32[64,64]{1,0:T(8,128)S(1)}, f32[64,64]{1,0:T(8,128)S(1)}, u32[]{:S(2)}, u32[]{:S(2)}) collective-permute-start(f32[64,64]{1,0:T(8,128)S(1)} %add.21), channel_id=1, source_target_pairs={{0,16},{4,20},{8,24},{12,28},{16,0},{20,4},{24,8},{28,12},{1,17},{... | collective-permute-start | bytes 49160 | tf_op jit(solution)/shard_map/ppermute | solution.py:440
  30.0 2.6 %collective-permute-start.11 = (f32[512,256]{1,0:T(8,128)S(1)}, f32[512,256]{1,0:T(8,128)S(1)}, u32[]{:S(2)}, u32[]{:S(2)}) collective-permute-start(f32[512,256]{1,0:T(8,128)S(1)} %get-tuple-element.83.auto_a), channel_id=1, source_target_pairs={{0,1},{1,0},{2,3},{3,2},{4,5},{5,4},{6,7},{7,6},{8,9},{9,8},{10,11... | collective-permute-start | bytes 1572872 | tf_op jit(solution)/shard_map/ppermute | solution.py:440
  32.7 3.5 %collective-permute-start.12 = (f32[552,256]{1,0:T(8,128)S(1)}, f32[552,256]{1,0:T(8,128)S(1)}, u32[]{:S(2)}, u32[]{:S(2)}) collective-permute-start(f32[552,256]{1,0:T(8,128)S(1)} %shard_map.44.refs_0_), channel_id=1, source_target_pairs={{0,1},{1,0},{2,3},{3,2},{4,5},{5,4},{6,7},{7,6},{8,9},{9,8},{10,11... | collective-permute-start | bytes 1695752 | tf_op jit(solution)/shard_map/ppermute | solution.py:440
  37.4 4.0 %collective-permute-start.14 = (f32[64,64]{1,0:T(8,128)S(1)}, f32[64,64]{1,0:T(8,128)S(1)}, u32[]{:S(2)}, u32[]{:S(2)}) collective-permute-start(f32[64,64]{1,0:T(8,128)S(1)} %get-tuple-element.100), channel_id=1, source_target_pairs={{0,4},{4,0},{8,12},{12,8},{16,20},{20,16},{24,28},{28,24},{1,5},{5... | collective-permute-start | bytes 49160 | tf_op jit(solution)/shard_map/ppermute | solution.py:440
  41.4 5.7 %collective-permute-start.16 = (f32[64,64]{1,0:T(8,128)S(1)}, f32[64,64]{1,0:T(8,128)S(1)}, u32[]{:S(2)}, u32[]{:S(2)}) collective-permute-start(f32[64,64]{1,0:T(8,128)S(1)} %add.23.refs_3_), channel_id=1, source_target_pairs={{0,24},{4,28},{8,16},{12,20},{16,8},{20,12},{24,0},{28,4},{1,25},{... | collective-permute-start | bytes 49160 | tf_op jit(solution)/shard_map/ppermute | solution.py:440
  43.7 3.9 %collective-permute-start.15 = (f32[64,64]{1,0:T(8,128)S(1)}, f32[64,64]{1,0:T(8,128)S(1)}, u32[]{:S(2)}, u32[]{:S(2)}) collective-permute-start(f32[64,64]{1,0:T(8,128)S(1)} %add.23.refs_3_), channel_id=1, source_target_pairs={{0,8},{1,17},{2,10},{3,19},{4,12},{5,21},{6,14},{7,23},{8,0},{9,25... | collective-permute-start | bytes 49160 | tf_op jit(solution)/shard_map/ppermute | solution.py:450
  43.7 2.0 %collective-permute-start.13 = (f32[8,256]{1,0:T(8,128)S(1)}, f32[8,256]{1,0:T(8,128)S(1)}, u32[]{:S(2)}, u32[]{:S(2)}) collective-permute-start(f32[8,256]{1,0:T(8,128)S(1)} %get-tuple-element.99.refs_1_), channel_id=1, source_target_pairs={{0,1},{1,0},{2,3},{3,2},{4,5},{5,4},{6,7},{7,6},{8,9},{9,8},{10,11... | collective-permute-start | bytes 24584 | tf_op jit(solution)/shard_map/ppermute | solution.py:440
  47.6 1.2 %collective-permute-start.17 = (f32[64,64]{1,0:T(8,128)S(1)}, f32[64,64]{1,0:T(8,128)S(1)}, u32[]{:S(2)}, u32[]{:S(2)}) collective-permute-start(f32[64,64]{1,0:T(8,128)S(1)} %collective-permute-done.15.refs_4_), channel_id=1, source_target_pairs={{0,1},{1,0},{2,3},{3,2},{4,5},{5,4},{6,7},{7,6},{8,9},{9,8},{10,11... | collective-permute-start | bytes 49160 | tf_op jit(solution)/shard_map/ppermute | solution.py:440
  50.0 4.0 %collective-permute-start.19 = (f32[64,64]{1,0:T(8,128)S(1)}, f32[64,64]{1,0:T(8,128)S(1)}, u32[]{:S(2)}, u32[]{:S(2)}) collective-permute-start(f32[64,64]{1,0:T(8,128)S(1)} %get-tuple-element.109), channel_id=1, source_target_pairs={{0,4},{4,0},{8,12},{12,8},{16,20},{20,16},{24,28},{28,24},{1,5},{5... | collective-permute-start | bytes 49160 | tf_op jit(solution)/shard_map/ppermute | solution.py:440
  54.0 5.7 %collective-permute-start.21 = (f32[64,64]{1,0:T(8,128)S(1)}, f32[64,64]{1,0:T(8,128)S(1)}, u32[]{:S(2)}, u32[]{:S(2)}) collective-permute-start(f32[64,64]{1,0:T(8,128)S(1)} %add.24.refs_3_), channel_id=1, source_target_pairs={{0,24},{4,28},{8,16},{12,20},{16,8},{20,12},{24,0},{28,4},{1,25},{... | collective-permute-start | bytes 49160 | tf_op jit(solution)/shard_map/ppermute | solution.py:440
  55.9 4.2 %collective-permute-start.20 = (f32[64,64]{1,0:T(8,128)S(1)}, f32[64,64]{1,0:T(8,128)S(1)}, u32[]{:S(2)}, u32[]{:S(2)}) collective-permute-start(f32[64,64]{1,0:T(8,128)S(1)} %add.24.refs_3_), channel_id=1, source_target_pairs={{0,8},{1,17},{2,10},{3,19},{4,12},{5,21},{6,14},{7,23},{8,0},{9,25... | collective-permute-start | bytes 49160 | tf_op jit(solution)/shard_map/ppermute | solution.py:450
  55.9 1.8 %collective-permute-start.18 = (f32[8,256]{1,0:T(8,128)S(1)}, f32[8,256]{1,0:T(8,128)S(1)}, u32[]{:S(2)}, u32[]{:S(2)}) collective-permute-start(f32[8,256]{1,0:T(8,128)S(1)} %get-tuple-element.108.refs_1_), channel_id=1, source_target_pairs={{0,1},{1,0},{2,3},{3,2},{4,5},{5,4},{6,7},{7,6},{8,9},{9,8},{10,11... | collective-permute-start | bytes 24584 | tf_op jit(solution)/shard_map/ppermute | solution.py:440
  60.1 1.2 %collective-permute-start.22 = (f32[64,64]{1,0:T(8,128)S(1)}, f32[64,64]{1,0:T(8,128)S(1)}, u32[]{:S(2)}, u32[]{:S(2)}) collective-permute-start(f32[64,64]{1,0:T(8,128)S(1)} %collective-permute-done.20.refs_4_), channel_id=1, source_target_pairs={{0,1},{1,0},{2,3},{3,2},{4,5},{5,4},{6,7},{7,6},{8,9},{9,8},{10,11... | collective-permute-start | bytes 49160 | tf_op jit(solution)/shard_map/ppermute | solution.py:440
  (1 other events, 0.8 us)
